TPU v7x, 256 devices: a whole 4x4x8 slice. The times are simulated.
256 devices in a mesh: pipe: 8 (over z), section: 4 (over y_hi, core), tensor: 8 (over x, y_lo).
Axes of the slice: x: 4, y: 4 (y_hi: 2, y_lo: 2; y = y_hi * 2 + y_lo), z: 8, core: 2. Of those that a mesh axis runs over, the one named last changes fastest.
Arguments:
- tokens: bfloat16 [8, 4, 2, 256, 8192], P('pipe', 'section', None, None, 'tensor'), may hold values from -51 to 51
- norm_gain: bfloat16 [4, 8192], P('section', 'tensor'), may hold values from 0.25 to 1.75
- held_kv: bfloat16 [4, 8192, 2048], P('section', 'tensor', 'pipe'), may hold values from -0.0625 to 0.0625
- block_holder: int32 [4, 8], replicated, may hold values from 0 to 7, each once within a row
- section_layer: int32 [8, 4], replicated, may hold values from 0 to 3, each once within a row
- cotangent: bfloat16 [8, 4, 2, 256, 2048], P('pipe', 'section', None, None, 'tensor'), may hold values from -6 to 6
Outputs:
- keys_values: bfloat16 [8, 4, 2, 256, 2048], P('pipe', 'section', None, None, 'tensor')
- token_grad: bfloat16 [8, 4, 2, 256, 8192], P('pipe', 'section', None, None, 'tensor')
- kv_grads: bfloat16 [4, 8192, 2048], P('section', 'tensor', 'pipe')
Inputs may be any that keep to these rules, and one draw needn't show every extreme that they name: Each row of section_layer is a permutation of the 4 window layers. Each row of block_holder is a permutation of the 8 relays.
All inputs are finite; a program needn't handle non-finite values.
Results may differ from a plain program's by a relative error of at most 0.0057.
Values may be sent and summed in bfloat16 or wider, within the bound.
No kernel may reach another device: no remote copies, remote signals or barrier semaphores. Data moves between devices by JAX's collectives and lax.ppermute only.
A program may use at most 128 MiB of HBM per device.

v0:
```python
import jax
import jax.numpy as jnp
from jax import lax
from jax.sharding import PartitionSpec as P

D = 8192


EPSILON = 1e-05


def invert_slots(holder_row):
    slot_count = holder_row.shape[0]
    slot_ids = jnp.arange(slot_count, dtype=jnp.int32)
    slot_match = holder_row[None, :] == slot_ids[:, None]
    return jnp.sum(jnp.where(slot_match, slot_ids[None, :], 0), axis=1)


def per_device(tokens, norm_gain, held_kv, block_holder, section_layer, cotangent):
    pipe_index = lax.axis_index("pipe")
    section_index = lax.axis_index("section")
    pipe_count = lax.axis_size("pipe")
    section_count = lax.axis_size("section")
    layer_index = section_layer[pipe_index, section_index]
    every_block, every_gain = (
        lax.all_gather(held_kv, ("pipe", "section"), axis=0, tiled=True),
        lax.all_gather(norm_gain, ("pipe", "section"), axis=0, tiled=True),
    )
    sources = jnp.arange(pipe_count, dtype=jnp.int32) * section_count + layer_index
    my_blocks = jnp.take(every_block, sources, axis=0)
    layer_gain = every_gain[layer_index]
    weight_blocks = jnp.take(my_blocks, block_holder[layer_index], axis=0)
    gain_f32 = layer_gain.astype(jnp.float32)
    micro_count = tokens.shape[2]
    tok_count = tokens.shape[3]
    feat_local = tokens.shape[4]
    row_count = micro_count * tok_count
    inputs = tokens.reshape(row_count, feat_local).astype(jnp.float32)
    squares = lax.psum(jnp.sum(inputs * inputs, axis=1), "tensor")
    scale_rows = lax.rsqrt(squares / D + EPSILON)
    normed = (inputs * scale_rows[:, None] * gain_f32).astype(jnp.bfloat16)
    partial_kv = jnp.einsum(
        "rd,bdc->rbc", normed, weight_blocks, preferred_element_type=jnp.float32
    ).reshape(row_count, -1)
    kv_local = lax.psum_scatter(partial_kv, "tensor", scatter_dimension=1, tiled=True)
    keys_values = kv_local.astype(jnp.bfloat16).reshape(1, 1, micro_count, tok_count, -1)
    upstream_local = cotangent.reshape(row_count, -1)
    upstream = lax.all_gather(upstream_local, "tensor", axis=1, tiled=True)
    upstream_blocks = upstream.reshape(row_count, pipe_count, -1)
    normed_grad = jnp.einsum(
        "rbc,bdc->rd", upstream_blocks, weight_blocks, preferred_element_type=jnp.float32
    )
    grad_blocks = jnp.einsum(
        "rd,rbc->bdc", normed, upstream_blocks, preferred_element_type=jnp.float32
    ).astype(jnp.bfloat16)
    outgoing_grads = jnp.take(grad_blocks, invert_slots(block_holder[layer_index]), axis=0)
    arrived = lax.all_to_all(outgoing_grads, "pipe", split_axis=0, concat_axis=0, tiled=True)
    layer_ids = jnp.arange(section_count, dtype=jnp.int32)
    owner_table = (section_layer[:, section_index][None, :] == layer_ids[:, None]).astype(
        jnp.bfloat16
    )
    per_layer = jnp.einsum("lq,qdc->ldc", owner_table, arrived, preferred_element_type=jnp.float32)
    summed = lax.psum_scatter(per_layer, "section", scatter_dimension=0, tiled=True)
    kv_grads = summed.astype(jnp.bfloat16)
    row_inner = lax.psum(jnp.sum(gain_f32 * normed_grad * inputs, axis=1), "tensor")
    token_grad = (
        scale_rows[:, None] * gain_f32 * normed_grad
        - inputs * (scale_rows**3 * row_inner / D)[:, None]
    ).astype(jnp.bfloat16)
    return (keys_values, token_grad.reshape(tokens.shape), kv_grads)


def solution(mesh):
    placed = (
        P("pipe", "section", None, None, "tensor"),
        P("section", "tensor"),
        P("section", "tensor", "pipe"),
        P(),
        P(),
        P("pipe", "section", None, None, "tensor"),
    )
    return jax.shard_map(
        per_device,
        mesh=mesh,
        in_specs=placed,
        out_specs=(
            P("pipe", "section", None, None, "tensor"),
            P("pipe", "section", None, None, "tensor"),
            P("section", "tensor", "pipe"),
        ),
        check_vma=False,
    )
```

profile of v0, /device:TPU:1, one launch (start us, length us, event | category | flops | bytes accessed | tf_op | source)
XLA Modules:
  0.0 425.6 jit_solution(6199539240854835074)
XLA Ops:
  7.2 0.0 all-gather.4.cloned.1.call-start
  7.2 0.7 all-gather.4.cloned.1.call-update
  7.9 0.0 all-gather.6.cloned.1.call-start
  7.9 1.8 copy.39
  9.7 0.0 all-gather.6.cloned.1.call-update
  9.8 0.0 reduce-scatter.3.cloned.1.call-start
  9.8 1.3 dynamic_slice.13
  14.3 1.5 fusion.6
  15.8 46.9 %all-gather = bf16[32,1,1024]{2,1,0:T(2,128)(2,1)S(1)} all-gather(bf16[1,1,1024]{2,1,0:T(2,128)(2,1)} %bitcast.61), channel_id=1, replica_groups=mesh['pipe'=8,'section'=4,'tensor'=8] {'pipe','section'}, dimensions={0}, use_global_device_ids=true | all-gather | bytes 67584 | tf_op jit(solution)/shard_map/all_gather | solution.py:27
  62.8 0.7 fusion.18
  63.4 0.7 compare_and_fusion.2
  64.1 0.7 compare_and_fusion.1
  64.8 0.1 select_reduce_fusion
  65.0 87.9 %all-gather.4.cloned.1.call-done = bf16[32,1024,256]{2,1,0:T(8,128)(2,1)} async-done(((bf16[1,1024,256]{2,1,0:T(8,128)(2,1)}), bf16[32,1024,256]{2,1,0:T(8,128)(2,1)}) %all-gather.4.cloned.1.call-update) | async-done | bytes 16777232 | tf_op jit(solution)/shard_map/all_gather | solution.py:26
  152.9 8.5 %gather_fusion = bf16[8,1024,256]{2,1,0:T(8,128)(2,1)} fusion(bf16[32,1024,256]{2,1,0:T(8,128)(2,1)} %all-gather.4.cloned.1.call-done, s32[1024]{0:T(1024)S(1)} %pad_clamp_fusion.2), kind=kCustom, calls=%fused_computation.2 | custom fusion | bytes 8388640 | tf_op jit(solution)/shard_map/jit(_take)/gather | solution.py:30
  161.4 4.7 %broadcast_select_fusion.2 = bf16[8,1024,256]{2,1,0:T(8,128)(2,1)} fusion(bf16[8,1024,256]{2,1,0:T(8,128)(2,1)} %gather_fusion, pred[8]{0:T(512)(128)(4,1)S(1)} %compare_and_fusion.2), kind=kLoop, calls=%fused_computation.8 | loop fusion | flops 2097152 | bytes 8388616 | tf_op jit(solution)/shard_map/jit(_take)/select_n | solution.py:30
  166.1 4.9 %gather_fusion.1 = bf16[8,1024,256]{2,1,0:T(8,128)(2,1)} fusion(bf16[8,1024,256]{2,1,0:T(8,128)(2,1)} %broadcast_select_fusion.2, s32[1024]{0:T(1024)S(1)} %pad_clamp_fusion.1), kind=kCustom, calls=%fused_computation.clone | custom fusion | bytes 8388640 | tf_op jit(solution)/shard_map/jit(_take)/gather | solution.py:32
  171.0 0.0 copy-start
  171.0 4.7 %fusion.10 = bf16[8,256,1024]{1,2,0:T(8,128)(2,1)} fusion(bf16[8,1024,256]{2,1,0:T(8,128)(2,1)} %gather_fusion.1, pred[8]{0:T(512)(128)(4,1)S(1)} %get-tuple-element.15), kind=kLoop, calls=%fused_computation.22 | loop fusion | flops 2097152 | bytes 8388616 | tf_op jit(solution)/shard_map/rd,bdc->rbc/dot_general | solution.py:42
  175.7 28.8 %all-gather.6.cloned.1.call-done = bf16[512,2048]{0,1:T(8,128)(2,1)} async-done(((bf16[512,256]{0,1:T(8,128)(2,1)}), bf16[512,2048]{0,1:T(8,128)(2,1)}) %all-gather.6.cloned.1.call-update) | async-done | bytes 2097168 | tf_op jit(solution)/shard_map/all_gather | solution.py:48
  204.5 0.0 copy-done
  204.5 5.4 %fusion.5 = (f32[512]{0:T(512)S(1)}, f32[1024,512,1]{0,1,2:T(8,128)S(1)}) fusion(bf16[1,1,2,256,1024]{4,3,2,1,0:T(8,128)(2,1)S(1)} %copy-done, f32[1024]{0:T(1024)S(1)} %bitcast.56, bf16[512,8,256]{0,2,1:T(8,128)(2,1)} %bitcast.62, bf16[8,1024,256]{2,1,0:T(8,128)(2,1)} %gather_fusion.1, pred[8]{0:T(512)(128)(4,1)S(1)} %get-tuple-element.15), kind=kOutput, calls=%fused_computation.14 | convolution fusion | flops 2151677440 | bytes 9443336 | tf_op jit(solution)/shard_map/rbc,bdc->rd/dot_general | solution.py:50
  209.9 14.6 %all-reduce = (f32[512]{0:T(512)S(1)}, f32[512]{0:T(512)S(1)}) all-reduce(f32[512]{0:T(512)S(1)} %bitcast.60, f32[512]{0:T(512)S(1)} %get-tuple-element.19), channel_id=1, replica_groups=mesh['pipe'=8,'section'=4,'tensor'=8] {'tensor'}, use_global_device_ids=true, to_apply=%region_1.2 | all-reduce | flops 1024 | bytes 8192 | tf_op jit(solution)/shard_map/psum | solution.py:39
  224.6 1.3 fusion.8
  225.8 6.5 %copy.29 = bf16[8,256,1024]{2,1,0:T(8,128)(2,1)} copy(bf16[8,256,1024]{1,2,0:T(8,128)(2,1)} %fusion.10) | data formatting | bytes 8388608 | tf_op jit(solution)/shard_map/rd,bdc->rbc/dot_general | solution.py:42
  232.3 6.8 %fusion.21 = f32[512,2048]{1,0:T(8,128)} fusion(bf16[512,1024]{1,0:T(8,128)(2,1)} %bitcast.51, bf16[2048,1024]{1,0:T(8,128)(2,1)} %bitcast.50), kind=kOutput, calls=%fused_computation.49 | convolution fusion | flops 2147483648 | bytes 9437184 | tf_op jit(solution)/shard_map/rd,bdc->rbc/dot_general | solution.py:42
  239.1 0.0 reduce-scatter.3.cloned.1.call-update
  239.2 6.3 %convert_bitcast_fusion = bf16[8,1024,256]{2,1,0:T(8,128)(2,1)} fusion(bf16[512,1024,1]{1,0,2:T(8,128)(2,1)} %bitcast.52, bf16[512,8,256]{0,2,1:T(8,128)(2,1)} %bitcast.63), kind=kOutput, calls=%fused_computation.5 | convolution fusion | flops 2149580800 | bytes 7340032 | tf_op jit(solution)/shard_map/rd,rbc->bdc/dot_general | solution.py:53
  245.4 5.0 %gather_fusion.2 = bf16[8,1024,256]{2,1,0:T(8,128)(2,1)} fusion(bf16[8,1024,256]{2,1,0:T(8,128)(2,1)} %convert_bitcast_fusion, s32[1024]{0:T(1024)S(1)} %pad_clamp_fusion), kind=kCustom, calls=%fused_computation.1.clone | custom fusion | bytes 8388640 | tf_op jit(solution)/shard_map/jit(_take)/gather | solution.py:56
  250.4 4.6 %broadcast_select_fusion = bf16[8,1024,256]{2,1,0:T(8,128)(2,1)} fusion(bf16[8,1024,256]{2,1,0:T(8,128)(2,1)} %gather_fusion.2, pred[8]{0:T(512)(128)(4,1)S(1)} %compare_and_fusion), kind=kLoop, calls=%fused_computation.6 | loop fusion | flops 2097152 | bytes 8388616 | tf_op jit(solution)/shard_map/jit(_take)/select_n | solution.py:56
  255.0 7.2 %all-to-all-start = ((bf16[8,1024,256]{2,1,0:T(8,128)(2,1)}), bf16[8,1024,256]{2,1,0:T(8,128)(2,1)}, u32[]{:S(2)}, u32[]{:S(2)}) async-start(bf16[8,1024,256]{2,1,0:T(8,128)(2,1)} %broadcast_select_fusion), calls=%async_computation.1 | async-start | bytes 8388608 | tf_op jit(solution)/shard_map/all_to_all | solution.py:57
  262.3 0.2 reduce-scatter.5.cloned.1.call-start
  262.5 0.7 fusion.17
  263.2 90.4 %all-to-all-done = bf16[8,1024,256]{2,1,0:T(8,128)(2,1)} async-done(((bf16[8,1024,256]{2,1,0:T(8,128)(2,1)}), bf16[8,1024,256]{2,1,0:T(8,128)(2,1)}, u32[]{:S(2)}, u32[]{:S(2)}) %all-to-all-start) | async-done | bytes 4194336 | tf_op jit(solution)/shard_map/all_to_all | solution.py:57
  353.6 4.9 %fusion = f32[4,1024,256]{2,0,1:T(4,128)S(1)} fusion(bf16[8,1024,256]{2,1,0:T(8,128)(2,1)} %all-to-all-done, s32[8]{0:T(128)S(1)} %fusion.17), kind=kOutput, calls=%fused_computation.3 | convolution fusion | flops 16777248 | bytes 8388640 | tf_op jit(solution)/shard_map/lq,qdc->ldc/dot_general | solution.py:62
  358.5 2.7 copy.35
  361.2 0.0 reduce-scatter.5.cloned.1.call-update
  361.3 1.4 fusion.3
  362.7 0.0 reduce-scatter.3.cloned.1.call-done
  362.7 1.8 convert_element_type.39
  364.5 52.6 %reduce-scatter.5.cloned.1.call-done = f32[1,1024,256]{2,1,0:T(8,128)} async-done(((f32[4,1024,256]{2,1,0:T(8,128)}), f32[1,1024,256]{2,1,0:T(8,128)}) %reduce-scatter.5.cloned.1.call-update) | async-done | bytes 1048592 | tf_op jit(solution)/shard_map/reduce_scatter | solution.py:63
  417.0 2.1 convert_element_type.45
  (10 shorter events, 0.1 us)
Async XLA Ops:
  7.2 145.7 %all-gather.4.cloned.1.call-start = ((), (), s32[]{:S(2)}) async-start(), calls=%async_computation.3 | async-start | bytes 17301504 | tf_op jit(solution)/shard_map/all_gather | solution.py:26
  7.9 196.6 %all-gather.6.cloned.1.call-start = ((), (), s32[]{:S(2)}) async-start(), calls=%async_computation.5 | async-start | bytes 2359296 | tf_op jit(solution)/shard_map/all_gather | solution.py:48
  9.8 352.9 %reduce-scatter.3.cloned.1.call-start = ((), (), s32[]{:S(2)}) async-start(), calls=%async_computation.4 | async-start | bytes 4718592 | tf_op jit(solution)/shard_map/reduce_scatter | solution.py:45
  171.0 33.5 %copy-start = (bf16[1,1,2,256,1024]{4,3,2,1,0:T(8,128)(2,1)S(1)}, bf16[1,1,2,256,1024]{4,3,2,1,0:T(8,128)(2,1)}, u32[]{:S(2)}) copy-start(bf16[1,1,2,256,1024]{4,3,2,1,0:T(8,128)(2,1)} %param.8) | copy-start | bytes 3145732
  255.0 98.6 %all-to-all-start = ((bf16[8,1024,256]{2,1,0:T(8,128)(2,1)}), bf16[8,1024,256]{2,1,0:T(8,128)(2,1)}, u32[]{:S(2)}, u32[]{:S(2)}) async-start(bf16[8,1024,256]{2,1,0:T(8,128)(2,1)} %broadcast_select_fusion), calls=%async_computation.1 | async-start | bytes 8388608 | tf_op jit(solution)/shard_map/all_to_all | solution.py:57
  262.3 154.8 %reduce-scatter.5.cloned.1.call-start = ((), (), s32[]{:S(2)}) async-start(), calls=%async_computation.6 | async-start | bytes 5242880 | tf_op jit(solution)/shard_map/reduce_scatter | solution.py:63
Sparse Core Ops, SparseCore 0:
  10.8 142.0 all-gather.3
  155.3 49.2 all-gather.5
  239.3 95.7 reduce-scatter.2
  361.4 55.5 reduce-scatter.4
where the time goes:
time: 426 us
  waiting for transfers between devices  260 us (61%)
  blocking collectives  61.5 us (14%)
  local copies, waits for them, and re-layouts  31.4 us (7%)
  other arithmetic  24.2 us (6%)
  matrix products  23.4 us (5%)
  between operations  17.1 us (4%)
  starting transfers between devices  7.58 us (2%)
    all_to_all x1, waiting for transfers between devices, per_device(): lax.all_to_all(outgoing_grads, 'pipe', split_axis=0, concat_axis=0, tiled...  90.4 us
    all_gather x1, waiting for transfers between devices, per_device(): lax.all_gather(held_kv, ('pipe', 'section'), axis=0, tiled=True)  87.9 us
    reduce_scatter x1, waiting for transfers between devices, per_device(): lax.psum_scatter(per_layer, 'section', scatter_dimension=0, tiled=True)  52.6 us
    all_gather x1, blocking collectives, per_device(): lax.all_gather(norm_gain, ('pipe', 'section'), axis=0, tiled=True)  46.9 us
    all_gather x1, waiting for transfers between devices, per_device(): upstream = lax.all_gather(upstream_local, 'tensor', axis=1, tiled=True)  28.8 us
    psum x1, blocking collectives, per_device(): squares = lax.psum(jnp.sum(inputs * inputs, axis=1), 'tensor')  14.6 us
  transfers between devices with their start and end apart: 5, of which 4 were waited for; matrix products, arithmetic and copies ran while one was open for 13% of the time, Pallas kernels for 0%

commit v1 on v0

v1 whole, which is shorter than its diff:
```python
import functools

import jax
import jax.numpy as jnp
from jax import lax
from jax.experimental import pallas as pl
from jax.experimental.pallas import tpu as pltpu
from jax.sharding import PartitionSpec as P

EPSILON = 1e-05
EXTRA = 16
F32 = jnp.float32
BF16 = jnp.bfloat16


def invert(row):
    ids = jnp.arange(row.shape[0], dtype=jnp.int32)
    return jnp.sum(jnp.where(row[None, :] == ids[:, None], ids[None, :], 0), axis=1)


def swap(x, axis, bits):
    size = lax.axis_size(axis)
    return lax.ppermute(x, axis, [(i, i ^ bits) for i in range(size)])


def shift(x, axis, step):
    size = lax.axis_size(axis)
    return lax.ppermute(x, axis, [(i, (i + step) % size) for i in range(size)])


def after(x, *others):
    return lax.optimization_barrier((x, *others))[0]


def choose(flag, x, y):
    flag = flag.reshape((1,) * x.ndim)
    return jnp.where(jnp.broadcast_to(flag, x.shape) != 0, x, y)


def split_rows(row_values):
    tiled = row_values.reshape(-1, 256)
    high = lax.reduce_precision(tiled, 8, 7)
    both = jnp.concatenate([high, tiled - high], axis=0)
    return jnp.pad(both, ((0, EXTRA - both.shape[0]), (0, 0))).astype(BF16)


def y_pairs(hi, lo):
    return [
        (s * 8 + t, (s ^ (2 * hi)) * 8 + (t ^ lo)) for s in range(4) for t in range(8)
    ]


def y_swap(x, hi, lo):
    return lax.ppermute(x, ("section", "tensor"), y_pairs(hi, lo))


def split_rows(row_values):
    tiled = row_values.reshape(-1, 256)
    high = lax.reduce_precision(tiled, 8, 7)
    both = jnp.concatenate([high, tiled - high], axis=0)
    return jnp.pad(both, ((0, EXTRA - both.shape[0]), (0, 0))).astype(BF16)


def y_pairs(hi, lo):
    return [
        (s * 8 + t, (s ^ (2 * hi)) * 8 + (t ^ lo)) for s in range(4) for t in range(8)
    ]


def y_swap(x, hi, lo):
    return lax.ppermute(x, ("section", "tensor"), y_pairs(hi, lo))


def pick(parts, index):
    out = parts[0]
    for i in range(1, len(parts)):
        out = jnp.where(index == i, parts[i], out)
    return out


def dw_kernel(slot_ref, normed_ref, g0, g1, g2a, g2b, g3, *outs):
    rows, feats = normed_ref.shape
    half = feats // 2
    pieces = (g0.at[0], g0.at[1], g1.at[0], g1.at[1], g2a, g2b, g3.at[0], g3.at[1])
    g_ref = outs[9]
    for q in range(8):
        g_ref[slot_ref[q]] = pieces[q][:rows, :]
    for f in range(0, feats, 256):
        turned = normed_ref[:, f : f + 256].T
        for d in range(8):
            grads = jnp.dot(turned, g_ref[d], preferred_element_type=F32).astype(BF16)
            if d != 4:
                outs[d][f : f + 256, :] = grads
            elif f < half:
                outs[4][f : f + 256, :] = grads
            else:
                outs[8][f - half : f - half + 256, :] = grads


def y_kernel(model, place_ref, normed_ref, r_ref, g_ref, *rest):
    w_refs, y_ref = rest[:9], rest[9]
    rows, feats = normed_ref.shape
    half = feats // 2
    inner = None
    for d in range(8):
        if d == 4:
            y = jnp.dot(normed_ref[:, :half], w_refs[4][...], preferred_element_type=F32)
            y += jnp.dot(normed_ref[:, half:], w_refs[8][...], preferred_element_type=F32)
        else:
            y = jnp.dot(normed_ref[...], w_refs[d][...], preferred_element_type=F32)
        y_ref[place_ref[d], :rows, :] = y.astype(BF16)
        term = y * g_ref[d].astype(F32)
        inner = term if inner is None else inner + term
    inner = jnp.sum(inner, axis=1, keepdims=True) * r_ref[...] * r_ref[...] * (1.0 / model)
    line = jnp.broadcast_to(inner, (rows, 128)).T[0:1, :]
    high = line.astype(BF16).astype(F32)
    low = line - high
    row = lax.broadcasted_iota(jnp.int32, (EXTRA, 256), 0)
    tile = jnp.zeros((EXTRA, 256), F32)
    for i, part in enumerate((high[:, :256], high[:, 256:], low[:, :256], low[:, 256:])):
        tile = jnp.where(row == i, jnp.broadcast_to(part, (EXTRA, 256)), tile)
    for b in range(8):
        y_ref[b, rows:, :] = tile.astype(BF16)


def a_kernel(r_ref, gain_ref, g_ref, *rest):
    w_refs, (a_ref, total) = rest[:9], rest[9:]
    rows, feats = total.shape
    half = feats // 2
    for d in range(8):
        g = g_ref[d]
        for h in range(2):
            if d == 4:
                w = w_refs[4 + 4 * h][...]
            else:
                w = w_refs[d][h * half : (h + 1) * half, :]
            term = lax.dot_general(
                g, w, (((1,), (1,)), ((), ())), preferred_element_type=F32
            )
            if d == 0:
                total[:, h * half : (h + 1) * half] = term
            else:
                total[:, h * half : (h + 1) * half] += term
    a_ref[...] = (total[...] * gain_ref[...].astype(F32) * r_ref[...]).astype(BF16)


def add_kernel(arrived_ref, own_ref, out_ref):
    out_ref[...] = (arrived_ref[...].astype(F32) + own_ref[...].astype(F32)).astype(BF16)


def join_kernel(cut, arrived_ref, own_ref, out_ref):
    half = arrived_ref.shape[0]
    own = own_ref[cut : cut + half, :].astype(F32)
    out_ref[cut : cut + half, :] = (arrived_ref[...].astype(F32) + own).astype(BF16)
    out_ref[half - cut : 2 * half - cut, :] = own_ref[half - cut : 2 * half - cut, :]


def last_kernel(plus_ref, minus_ref, own_ref, out_ref):
    total = own_ref[...].astype(F32) + plus_ref[...].astype(F32) + minus_ref[...].astype(F32)
    out_ref[...] = total.astype(BF16)


VMEM = pl.BlockSpec(memory_space=pltpu.VMEM)
SMEM = pl.BlockSpec(memory_space=pltpu.SMEM)
ANY = pl.BlockSpec(memory_space=pl.ANY)


def kernel_call(body, name, out_shape, operands, flops, nbytes, scratch=(), index=1):
    return pl.pallas_call(
        body,
        out_shape=out_shape,
        in_specs=[SMEM] * index + [VMEM] * (len(operands) - index),
        out_specs=[VMEM] * len(out_shape),
        scratch_shapes=list(scratch),
        compiler_params=pltpu.CompilerParams(vmem_limit_bytes=16 * 2**20),
        cost_estimate=pl.CostEstimate(flops=flops, bytes_accessed=nbytes, transcendentals=0),
        name=name,
    )(*operands)


def combine(body, name, own, *arrived):
    return pl.pallas_call(
        body,
        out_shape=jax.ShapeDtypeStruct(own.shape, BF16),
        in_specs=[VMEM] * (1 + len(arrived)),
        out_specs=VMEM,
        compiler_params=pltpu.CompilerParams(vmem_limit_bytes=6 * 2**20),
        cost_estimate=pl.CostEstimate(
            flops=own.size, bytes_accessed=6 * own.size, transcendentals=0
        ),
        name=name,
    )(*arrived, own)


def per_device(tokens, norm_gain, held_kv, block_holder, section_layer, cotangent):
    pipe = lax.axis_index("pipe")
    section = lax.axis_index("section")
    pipes = lax.axis_size("pipe")
    tensors = lax.axis_size("tensor")
    micro, tok, feats = tokens.shape[2:]
    rows = micro * tok
    model = feats * tensors
    held = held_kv[0]
    half = feats // 2
    cols = held.shape[1]

    def one(values, index):
        here = jnp.arange(values.shape[0], dtype=jnp.int32) == index
        return jnp.sum(jnp.where(here, values, 0)).reshape(1, 1)

    of_relay = jnp.arange(pipes, dtype=jnp.int32)[:, None] == pipe
    layers = jnp.sum(jnp.where(of_relay, section_layer, 0), axis=0)
    sections = invert(layers)
    every = jnp.arange(layers.shape[0], dtype=jnp.int32)
    near_sources = jnp.where((sections >> 1) == (every >> 1), 1, 0)
    core_sources = jnp.where((sections & 1) == (every & 1), 1, 0)
    near_workers = jnp.where((layers >> 1) == (every >> 1), 1, 0)
    core_workers = jnp.where((layers & 1) == (every & 1), 1, 0)
    source_near, source_core = one(near_sources, section), one(core_sources, section)
    worker_near, worker_core = one(near_workers, section), one(core_workers, section)
    far_source_core = one(core_sources, section ^ 2)
    sibling_worker_near = one(near_workers, section ^ 1)
    tensor = lax.axis_index("tensor")
    even = (1 - (tensor & 1)).reshape(1, 1)
    ids = jnp.arange(tensors, dtype=jnp.int32) ^ (tensor & ~1)
    of_layer = jnp.arange(layers.shape[0], dtype=jnp.int32)[:, None] == section
    holder_row = jnp.sum(jnp.where(of_layer, block_holder, 0), axis=0)
    holders = jnp.sum(
        jnp.where(ids[:, None] == jnp.arange(tensors)[None, :], holder_row[None, :], 0), axis=1
    )
    slots = (holders - pipe) & (pipes - 1)
    places = invert(slots)
    flags = (
        source_near,
        worker_near,
        source_core,
        worker_core,
        far_source_core,
        sibling_worker_near,
        even,
        slots,
        places,
    )

    top = rows // 2
    x_own = tokens.reshape(rows, feats)
    squares = jnp.sum(jnp.square(x_own.astype(F32)), axis=1)
    piece = jnp.concatenate([cotangent.reshape(rows, -1), split_rows(squares)], axis=0)
    up1, down1 = shift(held, "pipe", -1), shift(held, "pipe", 1)
    piece_other, x_other = swap(piece, "section", 1), swap(x_own, "section", 1)
    piece_other, x_other, flags = lax.optimization_barrier((piece_other, x_other, flags))
    (
        source_near,
        worker_near,
        source_core,
        worker_core,
        far_source_core,
        sibling_worker_near,
        even,
        slots,
        places,
    ) = flags
    piece_here = choose(source_core, piece, piece_other)
    piece_there = choose(far_source_core, piece, piece_other)
    flip_lo = y_swap(piece_here, 0, 1)
    flip_hi = y_swap(piece_there, 1, 0)
    flip_both = y_swap(piece_there, 1, 1)
    up1, down1, flip_lo, flip_hi, flip_both, x_other = lax.optimization_barrier(
        (up1, down1, flip_lo, flip_hi, flip_both, x_other)
    )

    up2, down2 = shift(up1, "pipe", -1), shift(down1, "pipe", 1)
    g_own = choose(source_near, piece_here, flip_hi)
    g_flip = choose(source_near, flip_lo, flip_both)
    pair = jnp.stack([choose(even, g_own, g_flip), choose(even, g_flip, g_own)])
    g1, g3 = swap(pair, "tensor", 2), swap(pair, "tensor", 6)
    x_there = choose(far_source_core, x_own, x_other)
    x_far0 = swap(x_there[:top], "section", 2)
    up2, down2, g1, g3, pair, x_far0, x_there = lax.optimization_barrier(
        (up2, down2, g1, g3, pair, x_far0, x_there)
    )

    up3, down3 = shift(up2, "pipe", -1), shift(down2, "pipe", 1)
    g2a, g2b = swap(g3[0], "tensor", 2), swap(g1[1], "tensor", 6)
    x_far1 = swap(x_there[top:], "section", 2)
    up3, down3, g1, g3, g2a, g2b, pair, x_far0, x_far1 = lax.optimization_barrier(
        (up3, down3, g1, g3, g2a, g2b, pair, x_far0, x_far1)
    )

    up4, down4 = shift(up3[:half], "pipe", -1), shift(down3[half:], "pipe", 1)
    x_near = choose(source_core, x_own, x_other)
    x = choose(source_near, x_near, jnp.concatenate([x_far0, x_far1], axis=0))
    g = (pair, g1, g2a, g2b, g3)
    lines = sum(
        jnp.sum(part.reshape(-1, rows + EXTRA, cols)[:, rows : rows + 4].astype(F32), axis=0)
        for part in g
    )
    mean = (lines[:2] + lines[2:]).reshape(rows, 1) / model
    r = lax.rsqrt(mean + EPSILON)
    normed = (x.astype(F32) * r * norm_gain.astype(F32)).astype(BF16)

    flops = 2 * rows * feats * cols * pipes
    whole = jax.ShapeDtypeStruct((feats, cols), BF16)
    part = jax.ShapeDtypeStruct((half, cols), BF16)
    *dw, g = kernel_call(
        dw_kernel,
        "weight_grads",
        (*[whole] * 4, part, *[whole] * 3, part, jax.ShapeDtypeStruct((pipes, rows, cols), BF16)),
        (slots, normed, *g),
        flops,
        9 * 2**20,
    )

    plus, minus = shift(dw[4], "pipe", 1), shift(dw[8], "pipe", -1)

    weights = (held, up1, up2, up3, up4, down3, down2, down1, down4)
    (y,) = kernel_call(
        functools.partial(y_kernel, model),
        "keys_values",
        (jax.ShapeDtypeStruct((tensors, rows + EXTRA, cols), BF16),),
        (places, normed, r, g, *weights),
        flops,
        9 * 2**20,
    )
    (a,) = kernel_call(
        a_kernel,
        "token_grads",
        (jax.ShapeDtypeStruct((rows, feats), BF16),),
        (r, norm_gain, after(g, y), *weights),
        flops,
        7 * 2**20,
        [pltpu.VMEM((rows, feats), F32)],
        index=0,
    )

    plus, minus, y, a = lax.optimization_barrier((plus, minus, y, a))

    def unpack(z):
        lines = z[rows : rows + 4].astype(F32)
        return lines[:2] + lines[2:]

    def total_of(parts):
        total = sum(part.astype(F32) for part in parts)
        return total[:rows].astype(BF16), unpack(total)

    def pack(total):
        return jnp.concatenate([total[0], split_rows(total[1])], axis=0)

    plus = combine(functools.partial(join_kernel, 0), "join", dw[3], plus)
    minus = combine(functools.partial(join_kernel, half), "join", dw[5], minus)
    plus, minus = shift(plus, "pipe", 1), shift(minus, "pipe", -1)
    to3, to1 = swap(y[4], "tensor", 2), swap(y[5], "tensor", 6)
    a0, a1 = a[:top], a[top:]
    a_far0 = swap(a0, "section", 2)
    plus, minus, to3, to1, a_far0, a1, y = lax.optimization_barrier(
        (plus, minus, to3, to1, a_far0, a1, y)
    )

    plus, minus = combine(add_kernel, "add", dw[2], plus), combine(add_kernel, "add", dw[6], minus)
    plus, minus = shift(plus, "pipe", 1), shift(minus, "pipe", -1)
    send1 = jnp.stack([y[2], pack(total_of([y[3], to1]))])
    send3 = jnp.stack([pack(total_of([y[6], to3])), y[7]])
    got1, got3 = swap(send1, "tensor", 2), swap(send3, "tensor", 6)
    a_far1 = swap(a1, "section", 2)
    plus, minus, got1, got3, a_far1, a0, a_far0 = lax.optimization_barrier(
        (plus, minus, got1, got3, a_far1, a0, a_far0)
    )

    plus, minus = combine(add_kernel, "add", dw[1], plus), combine(add_kernel, "add", dw[7], minus)
    plus, minus = shift(plus, "pipe", 1), shift(minus, "pipe", -1)
    parts = [y[:2], got1, got3]
    stays = pack(total_of([choose(even, p[0], p[1]) for p in parts]))
    leaves = pack(total_of([choose(even, p[1], p[0]) for p in parts]))
    flip_lo, flip_hi = y_swap(leaves, 0, 1), y_swap(stays, 1, 0)
    flip_both = y_swap(leaves, 1, 1)
    plus, minus, flip_lo, flip_hi, flip_both, a0, a1, a_far0, a_far1 = lax.optimization_barrier(
        (plus, minus, flip_lo, flip_hi, flip_both, a0, a1, a_far0, a_far1)
    )
    kv_grads = combine(last_kernel, "last", dw[0], plus, minus)[None]

    def come_back(here, across):
        other = swap(choose(sibling_worker_near, here, across), "section", 1)
        return choose(worker_core, choose(worker_near, here, across), other)

    packed = come_back(pack(total_of([stays, flip_lo])), pack(total_of([flip_hi, flip_both])))
    keys_values = packed[:rows].reshape(cotangent.shape)
    coef = unpack(packed).reshape(rows, 1)
    a = come_back(jnp.concatenate([a0, a1]), jnp.concatenate([a_far0, a_far1]))
    token_grad = (a.astype(F32) - x_own.astype(F32) * coef).astype(BF16)
    return (keys_values, token_grad.reshape(tokens.shape), kv_grads)


def solution(mesh):
    placed = (
        P("pipe", "section", None, None, "tensor"),
        P("section", "tensor"),
        P("section", "tensor", "pipe"),
        P(),
        P(),
        P("pipe", "section", None, None, "tensor"),
    )
    return jax.shard_map(
        per_device,
        mesh=mesh,
        in_specs=placed,
        out_specs=(
            P("pipe", "section", None, None, "tensor"),
            P("pipe", "section", None, None, "tensor"),
            P("section", "tensor", "pipe"),
        ),
        check_vma=False,
    )
```

time: 426 us -> 151 us (0.35)
  waiting for transfers between devices: 260 us -> 56.3 us
  blocking collectives: 61.5 us -> 0 us
  starting transfers between devices: 7.58 us -> 57.6 us
  local copies, waits for them, and re-layouts: 31.4 us -> 6.96 us
  matrix products: 23.4 us -> 0 us
  other arithmetic: 24.2 us -> 11.3 us
  Pallas kernels: 0 us -> 12.2 us
  between operations: 17.1 us -> 5.1 us
    all_gather x2 -> x0, waiting for transfers between devices: 117 us -> none  [the longest x1 87.9 us: per_device(): lax.all_gather(held_kv, ('pipe', 'section'), axis=0, tiled=True)]
    all_to_all x1 -> x0, waiting for transfers between devices: 90.4 us -> none  [per_device(): lax.all_to_all(outgoing_grads, 'pipe', split_axis=0, concat_axis=0, tiled...]
    ppermute x0 -> x38, starting transfers between devices: none -> 57.6 us  [the longest x16 30.3 us: swap(): return lax.ppermute(x, axis, [(i, i ^ bits) for i in range(size)])]
    ppermute x0 -> x38, waiting for transfers between devices: none -> 56.3 us  [the longest x16 24 us: swap(): return lax.ppermute(x, axis, [(i, i ^ bits) for i in range(size)])]
    reduce_scatter x2 -> x0, waiting for transfers between devices: 52.6 us -> none  [the longest x1 52.6 us: per_device(): lax.psum_scatter(per_layer, 'section', scatter_dimension=0, tiled=True)]
    all_gather x1 -> x0, blocking collectives: 46.9 us -> none  [per_device(): lax.all_gather(norm_gain, ('pipe', 'section'), axis=0, tiled=True)]
    dot_general x4 -> x0, matrix products: 23.4 us -> none  [the longest x1 6.82 us: per_device(): jnp.einsum('rd,bdc->rbc', normed, weight_blocks, preferred_element_type=j...]
    gather x3 -> x0, local copies, waits for them, and re-layouts: 18.4 us -> none  [the longest x1 8.51 us: per_device(): my_blocks = jnp.take(every_block, sources, axis=0)]
  transfers between devices with their start and end apart: 5 -> 38, of which waited for: 4 -> 19; matrix products, arithmetic and copies ran while one was open for 13% -> 7% of each run, Pallas kernels for 0% -> 8%
where the time goes in v1:
time: 151 us; the launch traced here: 149 us
  starting transfers between devices  57.6 us (38%)
  waiting for transfers between devices  56.3 us (37%)
  Pallas kernels  12.2 us (8%)
  other arithmetic  11.3 us (7%)
  local copies, waits for them, and re-layouts  6.96 us (5%)
  between operations  5.1 us (3%)
    ppermute x16, starting transfers between devices, swap(): return lax.ppermute(x, axis, [(i, i ^ bits) for i in range(size)])  30.3 us
    ppermute x16, waiting for transfers between devices, swap(): return lax.ppermute(x, axis, [(i, i ^ bits) for i in range(size)])  24 us
    ppermute x6, waiting for transfers between devices, y_swap(): return lax.ppermute(x, ('section', 'tensor'), y_pairs(hi, lo))  23.1 us
    ppermute x16, starting transfers between devices, shift(): return lax.ppermute(x, axis, [(i, (i + step) % size) for i in range(size)])  19.5 us
    pallas_call x3, Pallas kernels, kernel_call(): pl.pallas_call(body, out_shape=out_shape, in_specs=[SMEM] * index + [VMEM...  10.6 us
    ppermute x16, waiting for transfers between devices, shift(): return lax.ppermute(x, axis, [(i, (i + step) % size) for i in range(size)])  9.18 us
    ppermute x6, starting transfers between devices, y_swap(): return lax.ppermute(x, ('section', 'tensor'), y_pairs(hi, lo))  7.75 us
    unnamed x48, local copies, waits for them, and re-layouts  4.3 us
  transfers between devices with their start and end apart: 38, of which 19 were waited for; matrix products, arithmetic and copies ran while one was open for 7% of the time, Pallas kernels for 8%

profile of v1, /device:TPU:1, one launch (start us, length us, event | category | flops | bytes accessed | tf_op | source)
XLA Modules:
  0.0 149.4 jit_solution(15847335443390974746)
XLA Ops:
  0.6 6.5 %collective-permute-start.2 = (bf16[1024,256]{1,0:T(8,128)(2,1)}, bf16[1024,256]{1,0:T(8,128)(2,1)S(1)}, u32[]{:S(2)}, u32[]{:S(2)}) collective-permute-start(bf16[1024,256]{1,0:T(8,128)(2,1)} %bitcast.87), channel_id=1, source_target_pairs={{0,224},{32,0},{64,32},{96,64},{128,96},{160,128},{192,160},{224,1... | collective-permute-start | bytes 1572872 | tf_op jit(solution)/shard_map/ppermute | solution.py:28
  7.1 1.5 %multiply_reduce_fusion = f32[2,256]{1,0:T(2,128)S(1)} fusion(bf16[1,1,2,256,1024]{4,3,2,1,0:T(8,128)(2,1)} %param.6), kind=kLoop, calls=%fused_computation.2 | loop fusion | flops 1572352 | bytes 1050624 | tf_op jit(solution)/shard_map/reduce_sum | solution.py:247
  8.7 1.1 pad_maximum_fusion.3
  9.7 1.0 collective-permute-start
  10.9 0.8 select_reduce_fusion.4
  11.7 0.8 select_reduce_fusion.2
  12.8 0.8 fusion.39
  15.0 1.1 broadcast_select_fusion.5
  16.1 1.4 collective-permute-start.4
  17.5 2.6 %collective-permute-start.5 = (bf16[528,256]{1,0:T(8,128)(2,1)S(1)}, bf16[528,256]{1,0:T(8,128)(2,1)S(1)}, u32[]{:S(2)}, u32[]{:S(2)}) collective-permute-start(bf16[528,256]{1,0:T(8,128)(2,1)S(1)} %get-tuple-element.175), channel_id=1, source_target_pairs={{0,16},{1,17},{2,18},{3,19},{4,20},{5,21},{6,22},{7,23},{8,24},{9,... | collective-permute-start | bytes 811016 | tf_op jit(solution)/shard_map/ppermute | solution.py:71
  20.8 0.2 collective-permute-done.3.rest_7_
  21.0 2.8 %collective-permute-done.4 = bf16[528,256]{1,0:T(8,128)(2,1)S(1)} collective-permute-done((bf16[528,256]{1,0:T(8,128)(2,1)S(1)}, bf16[528,256]{1,0:T(8,128)(2,1)S(1)}, u32[]{:S(2)}, u32[]{:S(2)}) %collective-permute-start.4) | collective-permute-done | bytes 270368 | tf_op jit(solution)/shard_map/ppermute | solution.py:71
  23.9 8.3 %collective-permute-done.5 = bf16[528,256]{1,0:T(8,128)(2,1)S(1)} collective-permute-done((bf16[528,256]{1,0:T(8,128)(2,1)S(1)}, bf16[528,256]{1,0:T(8,128)(2,1)S(1)}, u32[]{:S(2)}, u32[]{:S(2)}) %collective-permute-start.5) | collective-permute-done | bytes 270368 | tf_op jit(solution)/shard_map/ppermute | solution.py:71
  32.1 2.0 %collective-permute-done.6 = bf16[528,256]{1,0:T(8,128)(2,1)S(1)} collective-permute-done((bf16[528,256]{1,0:T(8,128)(2,1)S(1)}, bf16[528,256]{1,0:T(8,128)(2,1)S(1)}, u32[]{:S(2)}, u32[]{:S(2)}) %collective-permute-start.6) | collective-permute-done | bytes 270368 | tf_op jit(solution)/shard_map/ppermute | solution.py:71
  34.3 2.6 %collective-permute-start.10 = (bf16[2,528,256]{2,1,0:T(8,128)(2,1)S(1)}, bf16[2,528,256]{2,1,0:T(8,128)(2,1)S(1)}, u32[]{:S(2)}, u32[]{:S(2)}) collective-permute-start(bf16[2,528,256]{2,1,0:T(8,128)(2,1)S(1)} %pad_maximum_fusion.g0), channel_id=1, source_target_pairs={{0,6},{1,7},{2,4},{3,5},{4,2},{5,3},{6,0},{7,1},{8,14},{9,15},{10,... | collective-permute-start | bytes 1622024 | tf_op jit(solution)/shard_map/ppermute | solution.py:23
  36.8 1.3 broadcast_select_fusion.1
  38.4 1.9 %collective-permute-start.7 = (bf16[1024,256]{1,0:T(8,128)(2,1)S(1)}, bf16[1024,256]{1,0:T(8,128)(2,1)S(1)}, u32[]{:S(2)}, u32[]{:S(2)}) collective-permute-start(bf16[1024,256]{1,0:T(8,128)(2,1)S(1)} %collective-permute-done.2.rest_1_), channel_id=1, source_target_pairs={{0,224},{32,0},{64,32},{96,64},{128,96},{160,128},{192,160},{224,1... | collective-permute-start | bytes 1572872 | tf_op jit(solution)/shard_map/ppermute | solution.py:28
  40.2 10.6 %collective-permute-done.11 = bf16[256,1024]{1,0:T(8,128)(2,1)S(1)} collective-permute-done((bf16[256,1024]{1,0:T(8,128)(2,1)S(1)}, bf16[256,1024]{1,0:T(8,128)(2,1)S(1)}, u32[]{:S(2)}, u32[]{:S(2)}) %collective-permute-start.11) | collective-permute-done | bytes 524320 | tf_op jit(solution)/shard_map/ppermute | solution.py:23
  50.9 0.8 collective-permute-done.8.rest_6_
  51.8 3.2 %collective-permute-start.16 = (bf16[256,1024]{1,0:T(8,128)(2,1)S(1)}, bf16[256,1024]{1,0:T(8,128)(2,1)S(1)}, u32[]{:S(2)}, u32[]{:S(2)}) collective-permute-start(bf16[256,1024]{1,0:T(8,128)(2,1)S(1)} %slice.201), channel_id=1, source_target_pairs={{0,16},{8,24},{16,0},{24,8},{1,17},{9,25},{17,1},{25,9},{2,18},{10... | collective-permute-start | bytes 1572872 | tf_op jit(solution)/shard_map/ppermute | solution.py:23
  55.0 0.3 collective-permute-start.12
  55.2 1.2 collective-permute-start.13
  56.4 1.5 %collective-permute-start.14 = (bf16[528,256]{1,0:T(8,128)(2,1)S(1)}, bf16[528,256]{1,0:T(8,128)(2,1)S(1)}, u32[]{:S(2)}, u32[]{:S(2)}) collective-permute-start(bf16[528,256]{1,0:T(8,128)(2,1)S(1)} %slice_bitcast_fusion.3), channel_id=1, source_target_pairs={{0,2},{1,3},{2,0},{3,1},{4,6},{5,7},{6,4},{7,5},{8,10},{9,11},{10,... | collective-permute-start | bytes 811016 | tf_op jit(solution)/shard_map/ppermute | solution.py:23
  58.0 0.3 collective-permute-start.15
  58.3 3.9 %collective-permute-done.14.g2a = bf16[528,256]{1,0:T(8,128)(2,1)S(1)} collective-permute-done((bf16[528,256]{1,0:T(8,128)(2,1)S(1)}, bf16[528,256]{1,0:T(8,128)(2,1)S(1)}, u32[]{:S(2)}, u32[]{:S(2)}) %collective-permute-start.14) | collective-permute-done | bytes 270368 | tf_op jit(solution)/shard_map/ppermute | solution.py:23
  62.1 2.7 %collective-permute-done.15.g2b = bf16[528,256]{1,0:T(8,128)(2,1)S(1)} collective-permute-done((bf16[528,256]{1,0:T(8,128)(2,1)S(1)}, bf16[528,256]{1,0:T(8,128)(2,1)S(1)}, u32[]{:S(2)}, u32[]{:S(2)}) %collective-permute-start.15) | collective-permute-done | bytes 270368 | tf_op jit(solution)/shard_map/ppermute | solution.py:23
  64.9 0.9 collective-permute-done.13.rest_5_
  65.8 0.7 slice.209
  66.5 0.7 collective-permute-start.19
  67.2 0.7 slice.210
  67.9 0.8 collective-permute-start.20
  68.8 0.6 multiply_convert_fusion.normed_ref
  69.5 1.0 copy-done.8
  70.6 1.0 copy-done.10
  71.6 1.0 copy-done.13
  72.6 1.0 copy-done.15
  73.5 3.1 %weight_grads.1 = (bf16[1024,256]{1,0:T(8,128)(2,1)S(1)}, bf16[1024,256]{1,0:T(8,128)(2,1)S(1)}, bf16[1024,256]{1,0:T(8,128)(2,1)S(1)}, bf16[1024,256]{1,0:T(8,1...) custom-call(s32[8]{0:T(128)S(1)} %subtract_and_fusion.slot_ref, ...), custom_call_target="tpu_custom_call" | custom-call | flops 2147483648 | bytes 9437184 | tf_op jit(solution)/shard_map/weight_grads/pallas_call | solution.py:169
  76.7 2.7 %collective-permute-start.18 = (bf16[512,256]{1,0:T(8,128)(2,1)S(1)}, bf16[512,256]{1,0:T(8,128)(2,1)S(1)}, u32[]{:S(2)}, u32[]{:S(2)}) collective-permute-start(bf16[512,256]{1,0:T(8,128)(2,1)S(1)} %get-tuple-element.104), channel_id=1, source_target_pairs={{0,224},{32,0},{64,32},{96,64},{128,96},{160,128},{192,160},{224,1... | collective-permute-start | bytes 786440 | tf_op jit(solution)/shard_map/ppermute | solution.py:28
  79.4 4.1 %keys_values.1 = bf16[8,528,256]{2,1,0:T(8,128)(2,1)S(1)} custom-call(s32[8]{0:T(128)S(1)} %select_reduce_fusion.place_ref, bf16[512,1024]{1,0:T(8,128)(2,1)S(1)} %multiply_convert_fusion.normed_ref, f32[512,1]{1,0:T(8,128)S(1)} %bitcast.85, bf16[8,512,256]{2,1,0:T(8,128)(2,1)S(1)} %get-tuple-element.109.g_ref, bf16[1024,256]{1,0:T(8,128)(2,1)S(1)} %bitcast.89, ...), custom_call_target="tpu_custom_call" | custom-call | flops 2147483648 | bytes 9437184 | tf_op jit(solution)/shard_map/keys_values/pallas_call | solution.py:169
  83.5 3.4 %token_grads.1 = bf16[512,1024]{1,0:T(8,128)(2,1)S(1)} custom-call(f32[512,1]{1,0:T(8,128)S(1)} %bitcast.86, bf16[1,1024]{1,0:T(2,128)(2,1)S(1)} %copy-done.11, bf16[8,512,256]{2,1,0:T(8,128)(2,1)S(1)} %get-tuple-element.109.g_ref, bf16[1024,256]{1,0:T(8,128)(2,1)S(1)} %bitcast.90, bf16[1024,256]{1,0:T(8,128)(2,1)S(1)} %collective-permute-done.2.rest_1_, ...), custom_call_target="tpu_custom_call" | custom-call | flops 2147483648 | bytes 7340032 | tf_op jit(solution)/shard_map/token_grads/pallas_call | solution.py:169
  87.0 0.7 collective-permute-start.22
  87.8 0.7 collective-permute-start.25
  88.6 1.1 collective-permute-start.21
  89.8 1.4 collective-permute-start.23
  91.4 3.8 %collective-permute-done.23 = bf16[528,256]{1,0:T(8,128)(2,1)S(1)} collective-permute-done((bf16[528,256]{1,0:T(8,128)(2,1)S(1)}, bf16[528,256]{1,0:T(8,128)(2,1)S(1)}, u32[]{:S(2)}, u32[]{:S(2)}) %collective-permute-start.23) | collective-permute-done | bytes 270368 | tf_op jit(solution)/shard_map/ppermute | solution.py:23
  95.2 2.6 %collective-permute-done.24 = bf16[528,256]{1,0:T(8,128)(2,1)S(1)} collective-permute-done((bf16[528,256]{1,0:T(8,128)(2,1)S(1)}, bf16[528,256]{1,0:T(8,128)(2,1)S(1)}, u32[]{:S(2)}, u32[]{:S(2)}) %collective-permute-start.24) | collective-permute-done | bytes 270368 | tf_op jit(solution)/shard_map/ppermute | solution.py:23
  98.3 0.7 collective-permute-start.29
  99.1 0.8 collective-permute-start.28
  100.0 0.7 collective-permute-start.27
  100.7 1.0 collective-permute-start.26
  101.7 2.2 %collective-permute-start.30 = (bf16[256,1024]{1,0:T(8,128)(2,1)S(1)}, bf16[256,1024]{1,0:T(8,128)(2,1)S(1)}, u32[]{:S(2)}, u32[]{:S(2)}) collective-permute-start(bf16[256,1024]{1,0:T(8,128)(2,1)S(1)} %get-tuple-element.139), channel_id=1, source_target_pairs={{0,16},{8,24},{16,0},{24,8},{1,17},{9,25},{17,1},{25,9},{2,18},{10... | collective-permute-start | bytes 1572872 | tf_op jit(solution)/shard_map/ppermute | solution.py:23
  103.9 4.4 %collective-permute-done.27.arrived_ref = bf16[1024,256]{1,0:T(8,128)(2,1)S(1)} collective-permute-done((bf16[1024,256]{1,0:T(8,128)(2,1)S(1)}, bf16[1024,256]{1,0:T(8,128)(2,1)S(1)}, u32[]{:S(2)}, u32[]{:S(2)}) %collective-permute-start.27) | collective-permute-done | bytes 524320 | tf_op jit(solution)/shard_map/ppermute | solution.py:28
  108.4 2.7 %collective-permute-done.26.arrived_ref = bf16[1024,256]{1,0:T(8,128)(2,1)S(1)} collective-permute-done((bf16[1024,256]{1,0:T(8,128)(2,1)S(1)}, bf16[1024,256]{1,0:T(8,128)(2,1)S(1)}, u32[]{:S(2)}, u32[]{:S(2)}) %collective-permute-start.26) | collective-permute-done | bytes 524320 | tf_op jit(solution)/shard_map/ppermute | solution.py:28
  111.2 0.3 convert_add_fusion.5
  111.8 1.9 %collective-permute-start.32 = (bf16[1024,256]{1,0:T(8,128)(2,1)S(1)}, bf16[1024,256]{1,0:T(8,128)(2,1)S(1)}, u32[]{:S(2)}, u32[]{:S(2)}) collective-permute-start(bf16[1024,256]{1,0:T(8,128)(2,1)S(1)} %add.202), channel_id=1, source_target_pairs={{0,224},{32,0},{64,32},{96,64},{128,96},{160,128},{192,160},{224,1... | collective-permute-start | bytes 1572872 | tf_op jit(solution)/shard_map/ppermute | solution.py:28
  113.9 2.2 %collective-permute-start.34 = (bf16[528,256]{1,0:T(8,128)(2,1)S(1)}, bf16[528,256]{1,0:T(8,128)(2,1)S(1)}, u32[]{:S(2)}, u32[]{:S(2)}) collective-permute-start(bf16[528,256]{1,0:T(8,128)(2,1)S(1)} %pad_maximum_fusion.4), channel_id=1, source_target_pairs={{0,16},{1,17},{2,18},{3,19},{4,20},{5,21},{6,22},{7,23},{8,24},{9,... | collective-permute-start | bytes 811016 | tf_op jit(solution)/shard_map/ppermute | solution.py:71
  116.2 1.5 collective-permute-start.35
  118.3 5.7 %collective-permute-done.34 = bf16[528,256]{1,0:T(8,128)(2,1)S(1)} collective-permute-done((bf16[528,256]{1,0:T(8,128)(2,1)S(1)}, bf16[528,256]{1,0:T(8,128)(2,1)S(1)}, u32[]{:S(2)}, u32[]{:S(2)}) %collective-permute-start.34) | collective-permute-done | bytes 270368 | tf_op jit(solution)/shard_map/ppermute | solution.py:71
  124.1 3.6 %collective-permute-done.33 = bf16[528,256]{1,0:T(8,128)(2,1)S(1)} collective-permute-done((bf16[528,256]{1,0:T(8,128)(2,1)S(1)}, bf16[528,256]{1,0:T(8,128)(2,1)S(1)}, u32[]{:S(2)}, u32[]{:S(2)}) %collective-permute-start.33) | collective-permute-done | bytes 270368 | tf_op jit(solution)/shard_map/ppermute | solution.py:71
  127.7 0.6 collective-permute-done.35
  128.8 15.5 %collective-permute-start.37 = (bf16[512,1024]{1,0:T(8,128)(2,1)S(1)}, bf16[512,1024]{1,0:T(8,128)(2,1)S(1)}, u32[]{:S(2)}, u32[]{:S(2)}) collective-permute-start(bf16[512,1024]{1,0:T(8,128)(2,1)S(1)} %broadcast_select_fusion), channel_id=1, source_target_pairs={{0,8},{8,0},{16,24},{24,16},{1,9},{9,1},{17,25},{25,17},{2,10},{10... | collective-permute-start | bytes 3145736 | tf_op jit(solution)/shard_map/ppermute | solution.py:23
  145.8 1.0 last.1
  147.1 0.7 slice.276
  147.8 1.6 %subtract_convert_fusion = bf16[512,1024]{1,0:T(8,128)(2,1)} fusion(f32[512]{0:T(512)S(1)} %bitcast.101, bf16[512,1024]{1,0:T(8,128)(2,1)S(1)} %collective-permute-done.37, bf16[512,1024]{1,0:T(8,128)(2,1)S(1)} %constant_dynamic-update-slice_fusion, bf16[512,1024]{1,0:T(8,128)(2,1)S(1)} %constant_dynamic-update-slice_fusion.2, pred[]{:T(512)} %bitcast.10, ...), kind=kLoop, calls=%fused_computation | loop fusion | flops 3670016 | bytes 5244930 | tf_op jit(solution)/shard_map/convert_element_type | solution.py:389
  (142 shorter events, 4.4 us)
Async XLA Ops:
  0.6 20.1 %collective-permute-start.2 = (bf16[1024,256]{1,0:T(8,128)(2,1)}, bf16[1024,256]{1,0:T(8,128)(2,1)S(1)}, u32[]{:S(2)}, u32[]{:S(2)}) collective-permute-start(bf16[1024,256]{1,0:T(8,128)(2,1)} %bitcast.87), channel_id=1, source_target_pairs={{0,224},{32,0},{64,32},{96,64},{128,96},{160,128},{192,160},{224,1... | collective-permute-start | bytes 1572872 | tf_op jit(solution)/shard_map/ppermute | solution.py:28
  7.1 13.9 %collective-permute-start.3 = (bf16[1024,256]{1,0:T(8,128)(2,1)}, bf16[1024,256]{1,0:T(8,128)(2,1)S(1)}, u32[]{:S(2)}, u32[]{:S(2)}) collective-permute-start(bf16[1024,256]{1,0:T(8,128)(2,1)} %bitcast.88), channel_id=1, source_target_pairs={{0,32},{32,64},{64,96},{96,128},{128,160},{160,192},{192,224},{224... | collective-permute-start | bytes 1572872 | tf_op jit(solution)/shard_map/ppermute | solution.py:28
  8.6 28.2 %copy-start.16 = (bf16[1,1,2,256,1024]{4,3,2,1,0:T(8,128)(2,1)S(1)}, bf16[1,1,2,256,1024]{4,3,2,1,0:T(8,128)(2,1)}, u32[]{:S(2)}) copy-start(bf16[1,1,2,256,1024]{4,3,2,1,0:T(8,128)(2,1)} %param.6) | copy-start | bytes 3145732
  9.7 3.9 %collective-permute-start = (bf16[528,256]{1,0:T(8,128)(2,1)S(1)}, bf16[528,256]{1,0:T(8,128)(2,1)}, u32[]{:S(2)}, u32[]{:S(2)}) collective-permute-start(bf16[528,256]{1,0:T(8,128)(2,1)S(1)} %pad_maximum_fusion.3), channel_id=1, source_target_pairs={{0,8},{8,0},{16,24},{24,16},{1,9},{9,1},{17,25},{25,17},{2,10},{10... | collective-permute-start | bytes 811016 | tf_op jit(solution)/shard_map/ppermute | solution.py:23
  10.8 2.9 %collective-permute-start.1 = (bf16[512,1024]{1,0:T(8,128)(2,1)}, bf16[512,1024]{1,0:T(8,128)(2,1)S(1)}, u32[]{:S(2)}, u32[]{:S(2)}) collective-permute-start(bf16[512,1024]{1,0:T(8,128)(2,1)} %bitcast.93), channel_id=1, source_target_pairs={{0,8},{8,0},{16,24},{24,16},{1,9},{9,1},{17,25},{25,17},{2,10},{10... | collective-permute-start | bytes 3145736 | tf_op jit(solution)/shard_map/ppermute | solution.py:23
  13.7 20.5 %copy-start.19 = (bf16[512,1024]{1,0:T(8,128)(2,1)}, bf16[512,1024]{1,0:T(8,128)(2,1)S(1)}, u32[]{:S(2)}) copy-start(bf16[512,1024]{1,0:T(8,128)(2,1)S(1)} %collective-permute-done.1) | copy-start | bytes 3145732
  16.1 7.7 %collective-permute-start.4 = (bf16[528,256]{1,0:T(8,128)(2,1)S(1)}, bf16[528,256]{1,0:T(8,128)(2,1)S(1)}, u32[]{:S(2)}, u32[]{:S(2)}) collective-permute-start(bf16[528,256]{1,0:T(8,128)(2,1)S(1)} %get-tuple-element.176), channel_id=1, source_target_pairs={{0,1},{1,0},{2,3},{3,2},{4,5},{5,4},{6,7},{7,6},{8,9},{9,8},{10,11... | collective-permute-start | bytes 811016 | tf_op jit(solution)/shard_map/ppermute | solution.py:71
  17.5 14.6 %collective-permute-start.5 = (bf16[528,256]{1,0:T(8,128)(2,1)S(1)}, bf16[528,256]{1,0:T(8,128)(2,1)S(1)}, u32[]{:S(2)}, u32[]{:S(2)}) collective-permute-start(bf16[528,256]{1,0:T(8,128)(2,1)S(1)} %get-tuple-element.175), channel_id=1, source_target_pairs={{0,16},{1,17},{2,18},{3,19},{4,20},{5,21},{6,22},{7,23},{8,24},{9,... | collective-permute-start | bytes 811016 | tf_op jit(solution)/shard_map/ppermute | solution.py:71
  20.1 14.0 %collective-permute-start.6 = (bf16[528,256]{1,0:T(8,128)(2,1)S(1)}, bf16[528,256]{1,0:T(8,128)(2,1)S(1)}, u32[]{:S(2)}, u32[]{:S(2)}) collective-permute-start(bf16[528,256]{1,0:T(8,128)(2,1)S(1)} %get-tuple-element.175), channel_id=1, source_target_pairs={{0,17},{1,16},{2,19},{3,18},{4,21},{5,20},{6,23},{7,22},{8,25},{9,... | collective-permute-start | bytes 811016 | tf_op jit(solution)/shard_map/ppermute | solution.py:71
  21.0 19.2 %copy-start.1 = (bf16[1024,256]{1,0:T(8,128)(2,1)}, bf16[1024,256]{1,0:T(8,128)(2,1)S(1)}, u32[]{:S(2)}) copy-start(bf16[1024,256]{1,0:T(8,128)(2,1)S(1)} %collective-permute-done.3.rest_7_) | copy-start | bytes 1572868
  34.3 17.4 %collective-permute-start.10 = (bf16[2,528,256]{2,1,0:T(8,128)(2,1)S(1)}, bf16[2,528,256]{2,1,0:T(8,128)(2,1)S(1)}, u32[]{:S(2)}, u32[]{:S(2)}) collective-permute-start(bf16[2,528,256]{2,1,0:T(8,128)(2,1)S(1)} %pad_maximum_fusion.g0), channel_id=1, source_target_pairs={{0,6},{1,7},{2,4},{3,5},{4,2},{5,3},{6,0},{7,1},{8,14},{9,15},{10,... | collective-permute-start | bytes 1622024 | tf_op jit(solution)/shard_map/ppermute | solution.py:23
  36.8 14.9 %collective-permute-start.9 = (bf16[2,528,256]{2,1,0:T(8,128)(2,1)S(1)}, bf16[2,528,256]{2,1,0:T(8,128)(2,1)S(1)}, u32[]{:S(2)}, u32[]{:S(2)}) collective-permute-start(bf16[2,528,256]{2,1,0:T(8,128)(2,1)S(1)} %pad_maximum_fusion.g0), channel_id=1, source_target_pairs={{0,2},{1,3},{2,0},{3,1},{4,6},{5,7},{6,4},{7,5},{8,10},{9,11},{10,... | collective-permute-start | bytes 1622024 | tf_op jit(solution)/shard_map/ppermute | solution.py:23
  38.2 20.1 %copy-start.11 = (bf16[1,1024]{1,0:T(2,128)(2,1)S(1)}, bf16[1,1024]{1,0:T(2,128)(2,1)}, u32[]{:S(2)}) copy-start(bf16[1,1024]{1,0:T(2,128)(2,1)} %gain_ref.1) | copy-start | bytes 6148
  38.2 30.5 %copy-start.17 = (bf16[1,1,2,256,1024]{4,3,2,1,0:T(8,128)(2,1)S(1)}, bf16[1,1,2,256,1024]{4,3,2,1,0:T(8,128)(2,1)}, u32[]{:S(2)}) copy-start(bf16[1,1,2,256,1024]{4,3,2,1,0:T(8,128)(2,1)} %param.6) | copy-start | bytes 3145732
  38.2 30.5 %copy-start.20 = (bf16[512,1024]{1,0:T(8,128)(2,1)S(1)}, bf16[512,1024]{1,0:T(8,128)(2,1)}, u32[]{:S(2)}) copy-start(bf16[512,1024]{1,0:T(8,128)(2,1)} %copy-done.19) | copy-start | bytes 3145732
  38.3 12.6 %collective-permute-start.11 = (bf16[256,1024]{1,0:T(8,128)(2,1)S(1)}, bf16[256,1024]{1,0:T(8,128)(2,1)S(1)}, u32[]{:S(2)}, u32[]{:S(2)}) collective-permute-start(bf16[256,1024]{1,0:T(8,128)(2,1)S(1)} %slice.253), channel_id=1, source_target_pairs={{0,16},{8,24},{16,0},{24,8},{1,17},{9,25},{17,1},{25,9},{2,18},{10... | collective-permute-start | bytes 1572872 | tf_op jit(solution)/shard_map/ppermute | solution.py:23
  38.4 12.5 %collective-permute-start.7 = (bf16[1024,256]{1,0:T(8,128)(2,1)S(1)}, bf16[1024,256]{1,0:T(8,128)(2,1)S(1)}, u32[]{:S(2)}, u32[]{:S(2)}) collective-permute-start(bf16[1024,256]{1,0:T(8,128)(2,1)S(1)} %collective-permute-done.2.rest_1_), channel_id=1, source_target_pairs={{0,224},{32,0},{64,32},{96,64},{128,96},{160,128},{192,160},{224,1... | collective-permute-start | bytes 1572872 | tf_op jit(solution)/shard_map/ppermute | solution.py:28
  40.2 11.5 %collective-permute-start.8 = (bf16[1024,256]{1,0:T(8,128)(2,1)S(1)}, bf16[1024,256]{1,0:T(8,128)(2,1)S(1)}, u32[]{:S(2)}, u32[]{:S(2)}) collective-permute-start(bf16[1024,256]{1,0:T(8,128)(2,1)S(1)} %collective-permute-done.3.rest_7_), channel_id=1, source_target_pairs={{0,32},{32,64},{64,96},{96,128},{128,160},{160,192},{192,224},{224... | collective-permute-start | bytes 1572872 | tf_op jit(solution)/shard_map/ppermute | solution.py:28
  50.9 17.8 %copy-start.3 = (bf16[1024,256]{1,0:T(8,128)(2,1)}, bf16[1024,256]{1,0:T(8,128)(2,1)S(1)}, u32[]{:S(2)}) copy-start(bf16[1024,256]{1,0:T(8,128)(2,1)S(1)} %collective-permute-done.7.rest_2_) | copy-start | bytes 1572868
  51.7 17.0 %copy-start.5 = (bf16[1024,256]{1,0:T(8,128)(2,1)}, bf16[1024,256]{1,0:T(8,128)(2,1)S(1)}, u32[]{:S(2)}) copy-start(bf16[1024,256]{1,0:T(8,128)(2,1)S(1)} %collective-permute-done.8.rest_6_) | copy-start | bytes 1572868
  51.7 17.0 %copy-start.7 = (bf16[2,528,256]{2,1,0:T(8,128)(2,1)}, bf16[2,528,256]{2,1,0:T(8,128)(2,1)S(1)}, u32[]{:S(2)}) copy-start(bf16[2,528,256]{2,1,0:T(8,128)(2,1)S(1)} %collective-permute-done.10.g3) | copy-start | bytes 1622020
  51.7 17.0 %copy-start.9 = (bf16[2,528,256]{2,1,0:T(8,128)(2,1)}, bf16[2,528,256]{2,1,0:T(8,128)(2,1)S(1)}, u32[]{:S(2)}) copy-start(bf16[2,528,256]{2,1,0:T(8,128)(2,1)S(1)} %collective-permute-done.9.g1) | copy-start | bytes 1622020
  51.8 13.1 %collective-permute-start.16 = (bf16[256,1024]{1,0:T(8,128)(2,1)S(1)}, bf16[256,1024]{1,0:T(8,128)(2,1)S(1)}, u32[]{:S(2)}, u32[]{:S(2)}) collective-permute-start(bf16[256,1024]{1,0:T(8,128)(2,1)S(1)} %slice.201), channel_id=1, source_target_pairs={{0,16},{8,24},{16,0},{24,8},{1,17},{9,25},{17,1},{25,9},{2,18},{10... | collective-permute-start | bytes 1572872 | tf_op jit(solution)/shard_map/ppermute | solution.py:23
  55.0 9.9 %collective-permute-start.12 = (bf16[1024,256]{1,0:T(8,128)(2,1)S(1)}, bf16[1024,256]{1,0:T(8,128)(2,1)S(1)}, u32[]{:S(2)}, u32[]{:S(2)}) collective-permute-start(bf16[1024,256]{1,0:T(8,128)(2,1)S(1)} %collective-permute-done.7.rest_2_), channel_id=1, source_target_pairs={{0,224},{32,0},{64,32},{96,64},{128,96},{160,128},{192,160},{224,1... | collective-permute-start | bytes 1572872 | tf_op jit(solution)/shard_map/ppermute | solution.py:28
  55.2 10.5 %collective-permute-start.13 = (bf16[1024,256]{1,0:T(8,128)(2,1)S(1)}, bf16[1024,256]{1,0:T(8,128)(2,1)S(1)}, u32[]{:S(2)}, u32[]{:S(2)}) collective-permute-start(bf16[1024,256]{1,0:T(8,128)(2,1)S(1)} %collective-permute-done.8.rest_6_), channel_id=1, source_target_pairs={{0,32},{32,64},{64,96},{96,128},{128,160},{160,192},{192,224},{224... | collective-permute-start | bytes 1572872 | tf_op jit(solution)/shard_map/ppermute | solution.py:28
  56.4 5.7 %collective-permute-start.14 = (bf16[528,256]{1,0:T(8,128)(2,1)S(1)}, bf16[528,256]{1,0:T(8,128)(2,1)S(1)}, u32[]{:S(2)}, u32[]{:S(2)}) collective-permute-start(bf16[528,256]{1,0:T(8,128)(2,1)S(1)} %slice_bitcast_fusion.3), channel_id=1, source_target_pairs={{0,2},{1,3},{2,0},{3,1},{4,6},{5,7},{6,4},{7,5},{8,10},{9,11},{10,... | collective-permute-start | bytes 811016 | tf_op jit(solution)/shard_map/ppermute | solution.py:23
  58.0 6.9 %collective-permute-start.15 = (bf16[528,256]{1,0:T(8,128)(2,1)S(1)}, bf16[528,256]{1,0:T(8,128)(2,1)S(1)}, u32[]{:S(2)}, u32[]{:S(2)}) collective-permute-start(bf16[528,256]{1,0:T(8,128)(2,1)S(1)} %slice_bitcast_fusion.2), channel_id=1, source_target_pairs={{0,6},{1,7},{2,4},{3,5},{4,2},{5,3},{6,0},{7,1},{8,14},{9,15},{10,... | collective-permute-start | bytes 811016 | tf_op jit(solution)/shard_map/ppermute | solution.py:23
  62.1 6.6 %copy-start.12 = (bf16[528,256]{1,0:T(8,128)(2,1)}, bf16[528,256]{1,0:T(8,128)(2,1)S(1)}, u32[]{:S(2)}) copy-start(bf16[528,256]{1,0:T(8,128)(2,1)S(1)} %collective-permute-done.14.g2a) | copy-start | bytes 811012
  64.9 3.9 %copy-start.14 = (bf16[528,256]{1,0:T(8,128)(2,1)}, bf16[528,256]{1,0:T(8,128)(2,1)S(1)}, u32[]{:S(2)}) copy-start(bf16[528,256]{1,0:T(8,128)(2,1)S(1)} %collective-permute-done.15.g2b) | copy-start | bytes 811012
  66.5 12.8 %collective-permute-start.19 = (bf16[512,256]{1,0:T(8,128)(2,1)}, bf16[512,256]{1,0:T(8,128)(2,1)}, u32[]{:S(2)}, u32[]{:S(2)}) collective-permute-start(bf16[512,256]{1,0:T(8,128)(2,1)} %slice.209), channel_id=1, source_target_pairs={{0,224},{32,0},{64,32},{96,64},{128,96},{160,128},{192,160},{224,1... | collective-permute-start | bytes 786440 | tf_op jit(solution)/shard_map/ppermute | solution.py:28
  67.9 11.4 %collective-permute-start.20 = (bf16[512,256]{1,0:T(8,128)(2,1)}, bf16[512,256]{1,0:T(8,128)(2,1)}, u32[]{:S(2)}, u32[]{:S(2)}) collective-permute-start(bf16[512,256]{1,0:T(8,128)(2,1)} %slice.210), channel_id=1, source_target_pairs={{0,32},{32,64},{64,96},{96,128},{128,160},{160,192},{192,224},{224... | collective-permute-start | bytes 786440 | tf_op jit(solution)/shard_map/ppermute | solution.py:28
  69.5 1.1 copy-start.8
  70.6 1.0 copy-start.10
  71.6 1.0 copy-start.13
  72.6 1.0 copy-start.15
  73.5 5.8 %copy-start = (bf16[1,1024,256]{2,1,0:T(8,128)(2,1)S(1)}, bf16[1,1024,256]{2,1,0:T(8,128)(2,1)}, u32[]{:S(2)}) copy-start(bf16[1,1024,256]{2,1,0:T(8,128)(2,1)} %param.8) | copy-start | bytes 1572868
  73.5 5.8 %copy-start.2 = (bf16[1024,256]{1,0:T(8,128)(2,1)S(1)}, bf16[1024,256]{1,0:T(8,128)(2,1)}, u32[]{:S(2)}) copy-start(bf16[1024,256]{1,0:T(8,128)(2,1)} %copy-done.1) | copy-start | bytes 1572868
  73.5 5.9 %copy-start.4 = (bf16[1024,256]{1,0:T(8,128)(2,1)S(1)}, bf16[1024,256]{1,0:T(8,128)(2,1)}, u32[]{:S(2)}) copy-start(bf16[1024,256]{1,0:T(8,128)(2,1)} %copy-done.3) | copy-start | bytes 1572868
  73.5 5.9 %copy-start.6 = (bf16[1024,256]{1,0:T(8,128)(2,1)S(1)}, bf16[1024,256]{1,0:T(8,128)(2,1)}, u32[]{:S(2)}) copy-start(bf16[1024,256]{1,0:T(8,128)(2,1)} %copy-done.5) | copy-start | bytes 1572868
  76.6 10.3 %collective-permute-start.17 = (bf16[512,256]{1,0:T(8,128)(2,1)S(1)}, bf16[512,256]{1,0:T(8,128)(2,1)S(1)}, u32[]{:S(2)}, u32[]{:S(2)}) collective-permute-start(bf16[512,256]{1,0:T(8,128)(2,1)S(1)} %get-tuple-element.103), channel_id=1, source_target_pairs={{0,32},{32,64},{64,96},{96,128},{128,160},{160,192},{192,224},{224... | collective-permute-start | bytes 786440 | tf_op jit(solution)/shard_map/ppermute | solution.py:28
  76.7 10.3 %collective-permute-start.18 = (bf16[512,256]{1,0:T(8,128)(2,1)S(1)}, bf16[512,256]{1,0:T(8,128)(2,1)S(1)}, u32[]{:S(2)}, u32[]{:S(2)}) collective-permute-start(bf16[512,256]{1,0:T(8,128)(2,1)S(1)} %get-tuple-element.104), channel_id=1, source_target_pairs={{0,224},{32,0},{64,32},{96,64},{128,96},{160,128},{192,160},{224,1... | collective-permute-start | bytes 786440 | tf_op jit(solution)/shard_map/ppermute | solution.py:28
  87.0 10.7 %collective-permute-start.22 = (bf16[1024,256]{1,0:T(8,128)(2,1)S(1)}, bf16[1024,256]{1,0:T(8,128)(2,1)S(1)}, u32[]{:S(2)}, u32[]{:S(2)}) collective-permute-start(bf16[1024,256]{1,0:T(8,128)(2,1)S(1)} %join.3), channel_id=1, source_target_pairs={{0,224},{32,0},{64,32},{96,64},{128,96},{160,128},{192,160},{224,1... | collective-permute-start | bytes 1572872 | tf_op jit(solution)/shard_map/ppermute | solution.py:28
  87.8 9.9 %collective-permute-start.25 = (bf16[256,1024]{1,0:T(8,128)(2,1)S(1)}, bf16[256,1024]{1,0:T(8,128)(2,1)S(1)}, u32[]{:S(2)}, u32[]{:S(2)}) collective-permute-start(bf16[256,1024]{1,0:T(8,128)(2,1)S(1)} %get-tuple-element.138), channel_id=1, source_target_pairs={{0,16},{8,24},{16,0},{24,8},{1,17},{9,25},{17,1},{25,9},{2,18},{10... | collective-permute-start | bytes 1572872 | tf_op jit(solution)/shard_map/ppermute | solution.py:23
  88.6 9.3 %collective-permute-start.21 = (bf16[1024,256]{1,0:T(8,128)(2,1)S(1)}, bf16[1024,256]{1,0:T(8,128)(2,1)S(1)}, u32[]{:S(2)}, u32[]{:S(2)}) collective-permute-start(bf16[1024,256]{1,0:T(8,128)(2,1)S(1)} %join.2), channel_id=1, source_target_pairs={{0,32},{32,64},{64,96},{96,128},{128,160},{160,192},{192,224},{224... | collective-permute-start | bytes 1572872 | tf_op jit(solution)/shard_map/ppermute | solution.py:28
  89.8 5.4 %collective-permute-start.23 = (bf16[528,256]{1,0:T(8,128)(2,1)S(1)}, bf16[528,256]{1,0:T(8,128)(2,1)S(1)}, u32[]{:S(2)}, u32[]{:S(2)}) collective-permute-start(bf16[528,256]{1,0:T(8,128)(2,1)S(1)} %get-tuple-element.158), channel_id=1, source_target_pairs={{0,2},{1,3},{2,0},{3,1},{4,6},{5,7},{6,4},{7,5},{8,10},{9,11},{10,... | collective-permute-start | bytes 811016 | tf_op jit(solution)/shard_map/ppermute | solution.py:23
  91.2 6.5 %collective-permute-start.24 = (bf16[528,256]{1,0:T(8,128)(2,1)S(1)}, bf16[528,256]{1,0:T(8,128)(2,1)S(1)}, u32[]{:S(2)}, u32[]{:S(2)}) collective-permute-start(bf16[528,256]{1,0:T(8,128)(2,1)S(1)} %get-tuple-element.157), channel_id=1, source_target_pairs={{0,6},{1,7},{2,4},{3,5},{4,2},{5,3},{6,0},{7,1},{8,14},{9,15},{10,... | collective-permute-start | bytes 811016 | tf_op jit(solution)/shard_map/ppermute | solution.py:23
  98.3 13.0 %collective-permute-start.29 = (bf16[2,528,256]{2,1,0:T(8,128)(2,1)S(1)}, bf16[2,528,256]{2,1,0:T(8,128)(2,1)S(1)}, u32[]{:S(2)}, u32[]{:S(2)}) collective-permute-start(bf16[2,528,256]{2,1,0:T(8,128)(2,1)S(1)} %pad_maximum_fusion.2), channel_id=1, source_target_pairs={{0,6},{1,7},{2,4},{3,5},{4,2},{5,3},{6,0},{7,1},{8,14},{9,15},{10,... | collective-permute-start | bytes 1622024 | tf_op jit(solution)/shard_map/ppermute | solution.py:23
  99.1 12.2 %collective-permute-start.28 = (bf16[2,528,256]{2,1,0:T(8,128)(2,1)S(1)}, bf16[2,528,256]{2,1,0:T(8,128)(2,1)S(1)}, u32[]{:S(2)}, u32[]{:S(2)}) collective-permute-start(bf16[2,528,256]{2,1,0:T(8,128)(2,1)S(1)} %pad_maximum_fusion.1), channel_id=1, source_target_pairs={{0,2},{1,3},{2,0},{3,1},{4,6},{5,7},{6,4},{7,5},{8,10},{9,11},{10,... | collective-permute-start | bytes 1622024 | tf_op jit(solution)/shard_map/ppermute | solution.py:23
  100.0 8.4 %collective-permute-start.27 = (bf16[1024,256]{1,0:T(8,128)(2,1)S(1)}, bf16[1024,256]{1,0:T(8,128)(2,1)S(1)}, u32[]{:S(2)}, u32[]{:S(2)}) collective-permute-start(bf16[1024,256]{1,0:T(8,128)(2,1)S(1)} %add.200), channel_id=1, source_target_pairs={{0,224},{32,0},{64,32},{96,64},{128,96},{160,128},{192,160},{224,1... | collective-permute-start | bytes 1572872 | tf_op jit(solution)/shard_map/ppermute | solution.py:28
  100.7 10.3 %collective-permute-start.26 = (bf16[1024,256]{1,0:T(8,128)(2,1)S(1)}, bf16[1024,256]{1,0:T(8,128)(2,1)S(1)}, u32[]{:S(2)}, u32[]{:S(2)}) collective-permute-start(bf16[1024,256]{1,0:T(8,128)(2,1)S(1)} %add.199), channel_id=1, source_target_pairs={{0,32},{32,64},{64,96},{96,128},{128,160},{160,192},{192,224},{224... | collective-permute-start | bytes 1572872 | tf_op jit(solution)/shard_map/ppermute | solution.py:28
  101.7 9.5 %collective-permute-start.30 = (bf16[256,1024]{1,0:T(8,128)(2,1)S(1)}, bf16[256,1024]{1,0:T(8,128)(2,1)S(1)}, u32[]{:S(2)}, u32[]{:S(2)}) collective-permute-start(bf16[256,1024]{1,0:T(8,128)(2,1)S(1)} %get-tuple-element.139), channel_id=1, source_target_pairs={{0,16},{8,24},{16,0},{24,8},{1,17},{9,25},{17,1},{25,9},{2,18},{10... | collective-permute-start | bytes 1572872 | tf_op jit(solution)/shard_map/ppermute | solution.py:23
  111.8 16.5 %collective-permute-start.32 = (bf16[1024,256]{1,0:T(8,128)(2,1)S(1)}, bf16[1024,256]{1,0:T(8,128)(2,1)S(1)}, u32[]{:S(2)}, u32[]{:S(2)}) collective-permute-start(bf16[1024,256]{1,0:T(8,128)(2,1)S(1)} %add.202), channel_id=1, source_target_pairs={{0,224},{32,0},{64,32},{96,64},{128,96},{160,128},{192,160},{224,1... | collective-permute-start | bytes 1572872 | tf_op jit(solution)/shard_map/ppermute | solution.py:28
  113.8 14.5 %collective-permute-start.31 = (bf16[1024,256]{1,0:T(8,128)(2,1)S(1)}, bf16[1024,256]{1,0:T(8,128)(2,1)S(1)}, u32[]{:S(2)}, u32[]{:S(2)}) collective-permute-start(bf16[1024,256]{1,0:T(8,128)(2,1)S(1)} %add.201), channel_id=1, source_target_pairs={{0,32},{32,64},{64,96},{96,128},{128,160},{160,192},{192,224},{224... | collective-permute-start | bytes 1572872 | tf_op jit(solution)/shard_map/ppermute | solution.py:28
  113.9 10.1 %collective-permute-start.34 = (bf16[528,256]{1,0:T(8,128)(2,1)S(1)}, bf16[528,256]{1,0:T(8,128)(2,1)S(1)}, u32[]{:S(2)}, u32[]{:S(2)}) collective-permute-start(bf16[528,256]{1,0:T(8,128)(2,1)S(1)} %pad_maximum_fusion.4), channel_id=1, source_target_pairs={{0,16},{1,17},{2,18},{3,19},{4,20},{5,21},{6,22},{7,23},{8,24},{9,... | collective-permute-start | bytes 811016 | tf_op jit(solution)/shard_map/ppermute | solution.py:71
  116.1 11.5 %collective-permute-start.33 = (bf16[528,256]{1,0:T(8,128)(2,1)S(1)}, bf16[528,256]{1,0:T(8,128)(2,1)S(1)}, u32[]{:S(2)}, u32[]{:S(2)}) collective-permute-start(bf16[528,256]{1,0:T(8,128)(2,1)S(1)} %pad_maximum_fusion.5), channel_id=1, source_target_pairs={{0,1},{1,0},{2,3},{3,2},{4,5},{5,4},{6,7},{7,6},{8,9},{9,8},{10,11... | collective-permute-start | bytes 811016 | tf_op jit(solution)/shard_map/ppermute | solution.py:71
  116.2 12.0 %collective-permute-start.35 = (bf16[528,256]{1,0:T(8,128)(2,1)S(1)}, bf16[528,256]{1,0:T(8,128)(2,1)S(1)}, u32[]{:S(2)}, u32[]{:S(2)}) collective-permute-start(bf16[528,256]{1,0:T(8,128)(2,1)S(1)} %pad_maximum_fusion.5), channel_id=1, source_target_pairs={{0,17},{1,16},{2,19},{3,18},{4,21},{5,20},{6,23},{7,22},{8,25},{9,... | collective-permute-start | bytes 811016 | tf_op jit(solution)/shard_map/ppermute | solution.py:71
  128.8 19.0 %collective-permute-start.37 = (bf16[512,1024]{1,0:T(8,128)(2,1)S(1)}, bf16[512,1024]{1,0:T(8,128)(2,1)S(1)}, u32[]{:S(2)}, u32[]{:S(2)}) collective-permute-start(bf16[512,1024]{1,0:T(8,128)(2,1)S(1)} %broadcast_select_fusion), channel_id=1, source_target_pairs={{0,8},{8,0},{16,24},{24,16},{1,9},{9,1},{17,25},{25,17},{2,10},{10... | collective-permute-start | bytes 3145736 | tf_op jit(solution)/shard_map/ppermute | solution.py:23
  144.3 3.5 %copy-start.18 = (bf16[1,1,2,256,1024]{4,3,2,1,0:T(8,128)(2,1)S(1)}, bf16[1,1,2,256,1024]{4,3,2,1,0:T(8,128)(2,1)}, u32[]{:S(2)}) copy-start(bf16[1,1,2,256,1024]{4,3,2,1,0:T(8,128)(2,1)} %param.6) | copy-start | bytes 3145732
  144.4 2.6 %collective-permute-start.36 = (bf16[528,256]{1,0:T(8,128)(2,1)S(1)}, bf16[528,256]{1,0:T(8,128)(2,1)S(1)}, u32[]{:S(2)}, u32[]{:S(2)}) collective-permute-start(bf16[528,256]{1,0:T(8,128)(2,1)S(1)} %broadcast_select_fusion.2), channel_id=1, source_target_pairs={{0,8},{8,0},{16,24},{24,16},{1,9},{9,1},{17,25},{25,17},{2,10},{10... | collective-permute-start | bytes 811016 | tf_op jit(solution)/shard_map/ppermute | solution.py:23

commit v2 on v1

v2 whole, which is shorter than its diff:
```python
import functools

import jax
import jax.numpy as jnp
from jax import lax
from jax.experimental import pallas as pl
from jax.experimental.pallas import tpu as pltpu
from jax.sharding import PartitionSpec as P

EPSILON = 1e-05
EXTRA = 16
F32 = jnp.float32
BF16 = jnp.bfloat16


def invert(row):
    ids = jnp.arange(row.shape[0], dtype=jnp.int32)
    return jnp.sum(jnp.where(row[None, :] == ids[:, None], ids[None, :], 0), axis=1)


def swap(x, axis, bits):
    size = lax.axis_size(axis)
    return lax.ppermute(x, axis, [(i, i ^ bits) for i in range(size)])


def shift(x, axis, step):
    size = lax.axis_size(axis)
    return lax.ppermute(x, axis, [(i, (i + step) % size) for i in range(size)])


def after(x, *others):
    return lax.optimization_barrier((x, *others))[0]


def choose(flag, x, y):
    flag = flag.reshape((1,) * x.ndim)
    return jnp.where(jnp.broadcast_to(flag, x.shape) != 0, x, y)


def split_rows(row_values):
    tiled = row_values.reshape(-1, 256)
    high = lax.reduce_precision(tiled, 8, 7)
    both = jnp.concatenate([high, tiled - high], axis=0)
    return jnp.pad(both, ((0, EXTRA - both.shape[0]), (0, 0))).astype(BF16)


def y_pairs(hi, lo):
    return [
        (s * 8 + t, (s ^ (2 * hi)) * 8 + (t ^ lo)) for s in range(4) for t in range(8)
    ]


def y_swap(x, hi, lo):
    return lax.ppermute(x, ("section", "tensor"), y_pairs(hi, lo))


def split_rows(row_values):
    tiled = row_values.reshape(-1, 256)
    high = lax.reduce_precision(tiled, 8, 7)
    both = jnp.concatenate([high, tiled - high], axis=0)
    return jnp.pad(both, ((0, EXTRA - both.shape[0]), (0, 0))).astype(BF16)


def y_pairs(hi, lo):
    return [
        (s * 8 + t, (s ^ (2 * hi)) * 8 + (t ^ lo)) for s in range(4) for t in range(8)
    ]


def y_swap(x, hi, lo):
    return lax.ppermute(x, ("section", "tensor"), y_pairs(hi, lo))


def pick(parts, index):
    out = parts[0]
    for i in range(1, len(parts)):
        out = jnp.where(index == i, parts[i], out)
    return out


def dw_kernel(model, slot_ref, pick_ref, x_ref, other, far, gain_ref, *rest):
    g0, g1, g2a, g2b, g3, normed_ref, r_ref, g_ref, own, p1, p2, p3, p4, m1, m2, m3, m4 = rest
    rows, feats = normed_ref.shape
    top, half = rows // 2, feats // 2
    pieces = (g0.at[0], g0.at[1], g1.at[0], g1.at[1], g2a, g2b, g3.at[0], g3.at[1])
    sums = sum(piece[rows:, :].astype(F32) for piece in pieces)
    scale = lax.rsqrt((sums[:2] + sums[2:4]) / model + EPSILON)
    for h in range(2):
        here = slice(h * top, (h + 1) * top)
        r_ref[here, :] = jnp.broadcast_to(scale[h : h + 1, :], (128, top)).T
        for i, source in enumerate((x_ref, other, far)):

            @pl.when(pick_ref[0] == i)
            def _():
                scaled = source[here, :].astype(F32) * r_ref[here, 0:1]
                normed_ref[here, :] = (scaled * gain_ref[...].astype(F32)).astype(BF16)

    for q in range(8):
        g_ref[slot_ref[q]] = pieces[q][:rows, :]
    uppers = (own, p4, p3, p2, p1, m1, m2, m3)
    lowers = (own, p3, p2, p1, m1, m2, m3, m4)
    for f in range(0, feats, 256):
        turned = normed_ref[:, f : f + 256].T
        for d in range(8):
            out_ref = uppers[d] if f < half else lowers[d]
            at = f - half if out_ref is m4 else f
            grads = jnp.dot(turned, g_ref[d], preferred_element_type=F32)
            out_ref[at : at + 256, :] = grads.astype(BF16)


def weight_halves(refs):
    held, up1, up2u, up_b, up_c, down1, down2l, down_b, down_c = refs
    half = up2u.shape[0]
    up, lo = slice(0, half), slice(half, 2 * half)
    return (
        (held.at[up], held.at[lo]),
        (up1.at[up], up1.at[lo]),
        (up2u, up_b.at[lo]),
        (up_b.at[up], up_c.at[lo]),
        (up_c.at[up], down_c.at[lo]),
        (down_c.at[up], down_b.at[lo]),
        (down_b.at[up], down2l),
        (down1.at[up], down1.at[lo]),
    )


def y_kernel(model, place_ref, normed_ref, r_ref, g_ref, *rest):
    y_ref = rest[9]
    rows, feats = normed_ref.shape
    half = feats // 2
    inner = None
    for d, (upper, lower) in enumerate(weight_halves(rest[:9])):
        y = jnp.dot(normed_ref[:, :half], upper[...], preferred_element_type=F32)
        y += jnp.dot(normed_ref[:, half:], lower[...], preferred_element_type=F32)
        y_ref[place_ref[d], :rows, :] = y.astype(BF16)
        term = y * g_ref[d].astype(F32)
        inner = term if inner is None else inner + term
    inner = jnp.sum(inner, axis=1, keepdims=True) * jnp.square(r_ref[:, 0:1]) * (1.0 / model)
    line = jnp.broadcast_to(inner, (rows, 128)).T[0:1, :]
    high = line.astype(BF16).astype(F32)
    low = line - high
    row = lax.broadcasted_iota(jnp.int32, (EXTRA, 256), 0)
    tile = jnp.zeros((EXTRA, 256), F32)
    for i, part in enumerate((high[:, :256], high[:, 256:], low[:, :256], low[:, 256:])):
        tile = jnp.where(row == i, jnp.broadcast_to(part, (EXTRA, 256)), tile)
    for b in range(8):
        y_ref[b, rows:, :] = tile.astype(BF16)


def a_kernel(r_ref, gain_ref, g_ref, *rest):
    a_ref, total = rest[9:]
    rows, feats = total.shape
    half = feats // 2
    for d, halves in enumerate(weight_halves(rest[:9])):
        g = g_ref[d]
        for h in range(2):
            here = slice(h * half, (h + 1) * half)
            term = lax.dot_general(
                g, halves[h][...], (((1,), (1,)), ((), ())), preferred_element_type=F32
            )
            if d == 0:
                total[:, here] = term
            else:
                total[:, here] += term
    a_ref[...] = (total[...] * gain_ref[...].astype(F32) * r_ref[:, 0:1]).astype(BF16)


def add_kernel(arrived_ref, own_ref, out_ref):
    out_ref[...] = (arrived_ref[...].astype(F32) + own_ref[...].astype(F32)).astype(BF16)


def last_kernel(plus_ref, minus_ref, plus_u, minus_l, own_ref, out_ref):
    half = plus_u.shape[0]
    for here, x_ref, y_ref in (
        (slice(0, half), plus_u, minus_ref.at[:half]),
        (slice(half, 2 * half), minus_l, plus_ref.at[half:]),
    ):
        total = own_ref[here, :].astype(F32) + x_ref[...].astype(F32) + y_ref[...].astype(F32)
        out_ref[here, :] = total.astype(BF16)


VMEM = pl.BlockSpec(memory_space=pltpu.VMEM)
SMEM = pl.BlockSpec(memory_space=pltpu.SMEM)
ANY = pl.BlockSpec(memory_space=pl.ANY)


def kernel_call(body, name, out_shape, operands, scratch=(), index=1):
    return pl.pallas_call(
        body,
        out_shape=out_shape,
        in_specs=[SMEM] * index + [VMEM] * (len(operands) - index),
        out_specs=[VMEM] * len(out_shape),
        scratch_shapes=list(scratch),
        compiler_params=pltpu.CompilerParams(vmem_limit_bytes=24 * 2**20),
        name=name,
    )(*operands)


def combine(body, name, own, *arrived):
    return pl.pallas_call(
        body,
        out_shape=jax.ShapeDtypeStruct(own.shape, BF16),
        in_specs=[VMEM] * (1 + len(arrived)),
        out_specs=VMEM,
        compiler_params=pltpu.CompilerParams(vmem_limit_bytes=6 * 2**20),
        cost_estimate=pl.CostEstimate(
            flops=own.size, bytes_accessed=6 * own.size, transcendentals=0
        ),
        name=name,
    )(*arrived, own)


def per_device(tokens, norm_gain, held_kv, block_holder, section_layer, cotangent):
    pipe = lax.axis_index("pipe")
    section = lax.axis_index("section")
    pipes = lax.axis_size("pipe")
    tensors = lax.axis_size("tensor")
    micro, tok, feats = tokens.shape[2:]
    rows = micro * tok
    model = feats * tensors
    held = held_kv[0]
    half = feats // 2
    cols = held.shape[1]

    def one(values, index):
        here = jnp.arange(values.shape[0], dtype=jnp.int32) == index
        return jnp.sum(jnp.where(here, values, 0)).reshape(1, 1)

    of_relay = jnp.arange(pipes, dtype=jnp.int32)[:, None] == pipe
    layers = jnp.sum(jnp.where(of_relay, section_layer, 0), axis=0)
    sections = invert(layers)
    every = jnp.arange(layers.shape[0], dtype=jnp.int32)
    near_sources = jnp.where((sections >> 1) == (every >> 1), 1, 0)
    core_sources = jnp.where((sections & 1) == (every & 1), 1, 0)
    near_workers = jnp.where((layers >> 1) == (every >> 1), 1, 0)
    core_workers = jnp.where((layers & 1) == (every & 1), 1, 0)
    source_near, source_core = one(near_sources, section), one(core_sources, section)
    worker_near, worker_core = one(near_workers, section), one(core_workers, section)
    far_source_core = one(core_sources, section ^ 2)
    sibling_worker_near = one(near_workers, section ^ 1)
    tensor = lax.axis_index("tensor")
    even = (1 - (tensor & 1)).reshape(1, 1)
    ids = jnp.arange(tensors, dtype=jnp.int32) ^ (tensor & ~1)
    of_layer = jnp.arange(layers.shape[0], dtype=jnp.int32)[:, None] == section
    holder_row = jnp.sum(jnp.where(of_layer, block_holder, 0), axis=0)
    holders = jnp.sum(
        jnp.where(ids[:, None] == jnp.arange(tensors)[None, :], holder_row[None, :], 0), axis=1
    )
    slots = (holders - pipe) & (pipes - 1)
    places = invert(slots)
    pick = jnp.where(source_near != 0, jnp.where(source_core != 0, 0, 1), 2).reshape(1)
    flags = (
        worker_near,
        worker_core,
        source_near,
        source_core,
        far_source_core,
        sibling_worker_near,
        even,
        slots,
        places,
        pick,
    )

    top = rows // 2
    x_own = tokens.reshape(rows, feats)
    squares = jnp.sum(jnp.square(x_own.astype(F32)), axis=1)
    piece = jnp.concatenate([cotangent.reshape(rows, -1), split_rows(squares)], axis=0)
    held_later = after(held, piece)
    up1, down1 = shift(held_later, "pipe", -1), shift(held_later, "pipe", 1)
    piece_other, x_other = swap(piece, "section", 1), swap(x_own, "section", 1)
    piece_other, flags = lax.optimization_barrier((piece_other, flags))
    (
        worker_near,
        worker_core,
        source_near,
        source_core,
        far_source_core,
        sibling_worker_near,
        even,
        slots,
        places,
        pick,
    ) = flags
    piece_here = choose(source_core, piece, piece_other)
    piece_there = choose(far_source_core, piece, piece_other)
    flip_hi = y_swap(piece_there, 1, 0)
    up2u, down2l = after(up1[:half], piece_here, piece_there), after(down1[half:], piece_here)
    up2u, down2l = shift(up2u, "pipe", -1), shift(down2l, "pipe", 1)
    x_there = choose(far_source_core, x_own, x_other)
    g_own = after(choose(source_near, piece_here, flip_hi), x_there)
    x_far = swap(x_there, "section", 2)
    g_flip = y_swap(g_own, 0, 1)
    up2u, down2l, g_own, g_flip = lax.optimization_barrier((up2u, down2l, g_own, g_flip))

    up_b = shift(jnp.concatenate([up2u, up1[half:]], axis=0), "pipe", -1)
    down_b = shift(jnp.concatenate([down1[:half], down2l], axis=0), "pipe", 1)
    pair = jnp.stack([choose(even, g_own, g_flip), choose(even, g_flip, g_own)])
    g1, g3 = swap(pair, "tensor", 2), swap(pair, "tensor", 6)
    up_b, down_b, g1, g3, pair = lax.optimization_barrier((up_b, down_b, g1, g3, pair))

    up_c, down_c = shift(up_b, "pipe", -1), shift(down_b, "pipe", 1)
    g2a, g2b = swap(g3[0], "tensor", 2), swap(g1[1], "tensor", 6)
    up_c, down_c, g1, g3, g2a, g2b, pair, x_far = lax.optimization_barrier(
        (up_c, down_c, g1, g3, g2a, g2b, pair, x_far)
    )
    weights = (held, up1, up2u, up_b, up_c, down1, down2l, down_b, down_c)

    whole = jax.ShapeDtypeStruct((feats, cols), BF16)
    part = jax.ShapeDtypeStruct((half, cols), BF16)
    normed, r, g, own, p1, p2, p3, p4, m1, m2, m3, m4 = kernel_call(
        functools.partial(dw_kernel, model),
        "weight_grads",
        (
            jax.ShapeDtypeStruct((rows, feats), BF16),
            jax.ShapeDtypeStruct((rows, 128), F32),
            jax.ShapeDtypeStruct((pipes, rows, cols), BF16),
            *[whole] * 4,
            part,
            *[whole] * 3,
            part,
        ),
        (slots, pick, x_own, x_other, x_far, norm_gain, pair, g1, g2a, g2b, g3),
        index=2,
    )
    plus, minus = shift(p1, "pipe", 1), shift(m1, "pipe", -1)
    (a,) = kernel_call(
        a_kernel,
        "token_grads",
        (jax.ShapeDtypeStruct((rows, feats), BF16),),
        (r, norm_gain, g, *weights),
        [pltpu.VMEM((rows, feats), F32)],
        index=0,
    )
    (y,) = kernel_call(
        functools.partial(y_kernel, model),
        "keys_values",
        (jax.ShapeDtypeStruct((tensors, rows + EXTRA, cols), BF16),),
        (places, normed, r, after(g, a), *weights),
    )
    to3, to1 = swap(y[4], "tensor", 2), swap(y[5], "tensor", 6)
    a_far = swap(a, "section", 2)

    def unpack(z):
        lines = z[rows : rows + 4].astype(F32)
        return lines[:2] + lines[2:]

    def total_of(parts):
        total = sum(part.astype(F32) for part in parts)
        return total[:rows].astype(BF16), unpack(total)

    def pack(total):
        return jnp.concatenate([total[0], split_rows(total[1])], axis=0)

    plus, minus = after(plus, y), after(minus, y)
    plus, minus = combine(add_kernel, "add", p2, plus), combine(add_kernel, "add", m2, minus)
    plus, minus, to3, to1 = lax.optimization_barrier((plus, minus, to3, to1))
    plus, minus = shift(plus, "pipe", 1), shift(minus, "pipe", -1)
    send1 = jnp.stack([y[2], pack(total_of([y[3], to1]))])
    send3 = jnp.stack([pack(total_of([y[6], to3])), y[7]])
    got1, got3 = swap(send1, "tensor", 2), swap(send3, "tensor", 6)

    plus, minus = combine(add_kernel, "add", p3, plus), combine(add_kernel, "add", m3, minus)
    plus, minus, got1, got3, a_far = lax.optimization_barrier((plus, minus, got1, got3, a_far))
    plus, minus = shift(plus, "pipe", 1), shift(minus, "pipe", -1)
    parts = [y[:2], got1, got3]
    stays = pack(total_of([choose(even, p[0], p[1]) for p in parts]))
    leaves = pack(total_of([choose(even, p[1], p[0]) for p in parts]))
    flip_lo, flip_hi = y_swap(leaves, 0, 1), y_swap(stays, 1, 0)
    flip_both = y_swap(leaves, 1, 1)

    plus_u = combine(add_kernel, "add", p4, plus[:half])
    minus_l = combine(add_kernel, "add", m4, minus[half:])
    plus_u, minus_l, flip_lo, flip_hi, flip_both = lax.optimization_barrier(
        (plus_u, minus_l, flip_lo, flip_hi, flip_both)
    )
    plus_u, minus_l = shift(plus_u, "pipe", 1), shift(minus_l, "pipe", -1)

    def come_back(here, across):
        other = swap(choose(sibling_worker_near, here, across), "section", 1)
        return choose(worker_core, choose(worker_near, here, across), other)

    packed = come_back(pack(total_of([stays, flip_lo])), pack(total_of([flip_hi, flip_both])))
    keys_values = packed[:rows].reshape(cotangent.shape)
    coef = unpack(packed).reshape(rows, 1)
    a = come_back(a, a_far)
    token_grad = (a.astype(F32) - x_own.astype(F32) * coef).astype(BF16)
    kv_grads = combine(
        last_kernel, "last", own, plus, minus, after(plus_u, token_grad, packed), minus_l
    )[None]
    return (keys_values, token_grad.reshape(tokens.shape), kv_grads)


def solution(mesh):
    placed = (
        P("pipe", "section", None, None, "tensor"),
        P("section", "tensor"),
        P("section", "tensor", "pipe"),
        P(),
        P(),
        P("pipe", "section", None, None, "tensor"),
    )
    return jax.shard_map(
        per_device,
        mesh=mesh,
        in_specs=placed,
        out_specs=(
            P("pipe", "section", None, None, "tensor"),
            P("pipe", "section", None, None, "tensor"),
            P("section", "tensor", "pipe"),
        ),
        check_vma=False,
    )
```

time: 151 us -> 134 us (0.89)
  starting transfers between devices: 57.6 us -> 50.8 us
  local copies, waits for them, and re-layouts: 6.96 us -> 1.15 us
  waiting for transfers between devices: 56.3 us -> 52.8 us
    ppermute x16, waiting for transfers between devices: 9.18 us -> 35.3 us  [shift(): return lax.ppermute(x, axis, [(i, (i + step) % size) for i in range(size)])]
    ppermute x6 -> x5, waiting for transfers between devices: 23.1 us -> 0.01 us  [y_swap(): return lax.ppermute(x, ('section', 'tensor'), y_pairs(hi, lo))]
    ppermute x16 -> x14, starting transfers between devices: 30.3 us -> 20.3 us  [swap(): return lax.ppermute(x, axis, [(i, i ^ bits) for i in range(size)])]
    ppermute x16 -> x14, waiting for transfers between devices: 24 us -> 17.5 us  [swap(): return lax.ppermute(x, axis, [(i, i ^ bits) for i in range(size)])]
    unnamed x48 -> x9, local copies, waits for them, and re-layouts: 4.3 us -> 0.03 us
    ppermute x16, starting transfers between devices: 19.5 us -> 22 us  [shift(): return lax.ppermute(x, axis, [(i, (i + step) % size) for i in range(size)])]
    ppermute x6 -> x5, starting transfers between devices: 7.75 us -> 8.5 us  [y_swap(): return lax.ppermute(x, ('section', 'tensor'), y_pairs(hi, lo))]
  transfers between devices with their start and end apart: 38 -> 35, of which waited for: 19 -> 12; matrix products, arithmetic and copies ran while one was open for 7% -> 6% of each run, Pallas kernels for 8% -> 5%
where the time goes in v2:
time: 134 us
  waiting for transfers between devices  52.8 us (39%)
  starting transfers between devices  50.8 us (38%)
  other arithmetic  11.3 us (8%)
  Pallas kernels  11.2 us (8%)
  between operations  6.24 us (5%)
    ppermute x16, waiting for transfers between devices, shift(): return lax.ppermute(x, axis, [(i, (i + step) % size) for i in range(size)])  35.3 us
    ppermute x16, starting transfers between devices, shift(): return lax.ppermute(x, axis, [(i, (i + step) % size) for i in range(size)])  22 us
    ppermute x14, starting transfers between devices, swap(): return lax.ppermute(x, axis, [(i, i ^ bits) for i in range(size)])  20.3 us
    ppermute x14, waiting for transfers between devices, swap(): return lax.ppermute(x, axis, [(i, i ^ bits) for i in range(size)])  17.5 us
    pallas_call x3, Pallas kernels, kernel_call(): pl.pallas_call(body, out_shape=out_shape, in_specs=[SMEM] * index + [VMEM...  9.63 us
    ppermute x5, starting transfers between devices, y_swap(): return lax.ppermute(x, ('section', 'tensor'), y_pairs(hi, lo))  8.5 us
  transfers between devices with their start and end apart: 35, of which 12 were waited for; matrix products, arithmetic and copies ran while one was open for 6% of the time, Pallas kernels for 5%

profile of v2, /device:TPU:1, one launch (start us, length us, event | category | flops | bytes accessed | tf_op | source)
XLA Modules:
  0.0 133.5 jit_solution(16041048776782237187)
XLA Ops:
  0.7 1.6 %multiply_reduce_fusion = f32[2,256]{1,0:T(2,128)S(1)} fusion(bf16[1,1,2,256,1024]{4,3,2,1,0:T(8,128)(2,1)} %param.6), kind=kLoop, calls=%fused_computation.1 | loop fusion | flops 1572352 | bytes 1050624 | tf_op jit(solution)/shard_map/reduce_sum | solution.py:267
  2.3 1.7 %pad_maximum_fusion.5 = bf16[528,256]{1,0:T(8,128)(2,1)} fusion(bf16[16,256]{1,0:T(8,128)(2,1)S(1)} %fusion.16, bf16[512,256]{1,0:T(8,128)(2,1)} %bitcast.74), kind=kLoop, calls=%fused_computation.25 | loop fusion | flops 540672 | bytes 540672 | tf_op jit(solution)/shard_map/concatenate | solution.py:268
  4.0 3.2 %collective-permute-start = (bf16[528,256]{1,0:T(8,128)(2,1)}, bf16[528,256]{1,0:T(8,128)(2,1)}, u32[]{:S(2)}, u32[]{:S(2)}) collective-permute-start(bf16[528,256]{1,0:T(8,128)(2,1)} %pad_maximum_fusion.5), channel_id=1, source_target_pairs={{0,8},{8,0},{16,24},{24,16},{1,9},{9,1},{17,25},{25,17},{2,10},{10... | collective-permute-start | bytes 811016 | tf_op jit(solution)/shard_map/ppermute | solution.py:23
  7.2 0.2 collective-permute-start.1
  7.4 0.8 select_reduce_fusion.4
  8.2 0.1 select_reduce_fusion.3
  8.4 0.8 fusion.35
  10.4 0.8 select_reduce_fusion.2
  11.2 0.2 select_reduce_fusion.1
  12.2 1.0 broadcast_select_fusion.4
  13.2 3.1 %collective-permute-start.6 = (bf16[528,256]{1,0:T(8,128)(2,1)S(1)}, bf16[528,256]{1,0:T(8,128)(2,1)S(1)}, u32[]{:S(2)}, u32[]{:S(2)}) collective-permute-start(bf16[528,256]{1,0:T(8,128)(2,1)S(1)} %broadcast_select_fusion.4), channel_id=1, source_target_pairs={{0,16},{1,17},{2,18},{3,19},{4,20},{5,21},{6,22},{7,23},{8,24},{9,... | collective-permute-start | bytes 811016 | tf_op jit(solution)/shard_map/ppermute | solution.py:71
  16.3 3.7 %collective-permute-start.2 = (bf16[1024,256]{1,0:T(8,128)(2,1)S(1)}, bf16[1024,256]{1,0:T(8,128)(2,1)S(1)}, u32[]{:S(2)}, u32[]{:S(2)}) collective-permute-start(bf16[1024,256]{1,0:T(8,128)(2,1)S(1)} %bitcast.71), channel_id=1, source_target_pairs={{0,224},{32,0},{64,32},{96,64},{128,96},{160,128},{192,160},{224,1... | collective-permute-start | bytes 1572872 | tf_op jit(solution)/shard_map/ppermute | solution.py:28
  21.2 2.4 %collective-permute-done.4.rest_5_ = bf16[1024,256]{1,0:T(8,128)(2,1)S(1)} collective-permute-done((bf16[1024,256]{1,0:T(8,128)(2,1)}, bf16[1024,256]{1,0:T(8,128)(2,1)S(1)}, u32[]{:S(2)}, u32[]{:S(2)}) %collective-permute-start.4) | collective-permute-done | bytes 524320 | tf_op jit(solution)/shard_map/ppermute | solution.py:28
  23.6 1.1 broadcast_select_fusion.3
  24.7 0.2 broadcast_select_fusion.1
  24.9 1.4 %collective-permute-start.7 = (bf16[528,256]{1,0:T(8,128)(2,1)S(1)}, bf16[528,256]{1,0:T(8,128)(2,1)S(1)}, u32[]{:S(2)}, u32[]{:S(2)}) collective-permute-start(bf16[528,256]{1,0:T(8,128)(2,1)S(1)} %broadcast_select_fusion.3), channel_id=1, source_target_pairs={{0,1},{1,0},{2,3},{3,2},{4,5},{5,4},{6,7},{7,6},{8,9},{9,8},{10,11... | collective-permute-start | bytes 811016 | tf_op jit(solution)/shard_map/ppermute | solution.py:71
  26.3 4.1 %collective-permute-done.2.rest_1_ = bf16[1024,256]{1,0:T(8,128)(2,1)S(1)} collective-permute-done((bf16[1024,256]{1,0:T(8,128)(2,1)S(1)}, bf16[1024,256]{1,0:T(8,128)(2,1)S(1)}, u32[]{:S(2)}, u32[]{:S(2)}) %collective-permute-start.2) | collective-permute-done | bytes 524320 | tf_op jit(solution)/shard_map/ppermute | solution.py:28
  30.5 0.7 collective-permute-start.5
  31.2 2.8 %collective-permute-start.3 = (bf16[512,256]{1,0:T(8,128)(2,1)S(1)}, bf16[512,256]{1,0:T(8,128)(2,1)S(1)}, u32[]{:S(2)}, u32[]{:S(2)}) collective-permute-start(bf16[512,256]{1,0:T(8,128)(2,1)S(1)} %get-tuple-element.75), channel_id=1, source_target_pairs={{0,224},{32,0},{64,32},{96,64},{128,96},{160,128},{192,160},{224,1... | collective-permute-start | bytes 786440 | tf_op jit(solution)/shard_map/ppermute | solution.py:28
  34.1 4.9 %collective-permute-done.5.rest_6_ = bf16[512,256]{1,0:T(8,128)(2,1)S(1)} collective-permute-done((bf16[512,256]{1,0:T(8,128)(2,1)S(1)}, bf16[512,256]{1,0:T(8,128)(2,1)S(1)}, u32[]{:S(2)}, u32[]{:S(2)}) %collective-permute-start.5) | collective-permute-done | bytes 262176 | tf_op jit(solution)/shard_map/ppermute | solution.py:28
  38.9 0.4 collective-permute-done.3.rest_2_
  39.5 2.6 %collective-permute-start.11 = (bf16[2,528,256]{2,1,0:T(8,128)(2,1)S(1)}, bf16[2,528,256]{2,1,0:T(8,128)(2,1)S(1)}, u32[]{:S(2)}, u32[]{:S(2)}) collective-permute-start(bf16[2,528,256]{2,1,0:T(8,128)(2,1)S(1)} %pad_maximum_fusion.rest_0_), channel_id=1, source_target_pairs={{0,6},{1,7},{2,4},{3,5},{4,2},{5,3},{6,0},{7,1},{8,14},{9,15},{10,... | collective-permute-start | bytes 1622024 | tf_op jit(solution)/shard_map/ppermute | solution.py:23
  42.1 2.1 %collective-permute-start.9 = (bf16[1024,256]{1,0:T(8,128)(2,1)S(1)}, bf16[1024,256]{1,0:T(8,128)(2,1)S(1)}, u32[]{:S(2)}, u32[]{:S(2)}) collective-permute-start(bf16[1024,256]{1,0:T(8,128)(2,1)S(1)} %pad_maximum_fusion.4), channel_id=1, source_target_pairs={{0,32},{32,64},{64,96},{96,128},{128,160},{160,192},{192,224},{224... | collective-permute-start | bytes 1572872 | tf_op jit(solution)/shard_map/ppermute | solution.py:28
  44.3 0.7 collective-permute-start.8
  45.0 0.5 collective-permute-start.16
  45.5 8.8 %collective-permute-done.9.rest_7_ = bf16[1024,256]{1,0:T(8,128)(2,1)S(1)} collective-permute-done((bf16[1024,256]{1,0:T(8,128)(2,1)S(1)}, bf16[1024,256]{1,0:T(8,128)(2,1)S(1)}, u32[]{:S(2)}, u32[]{:S(2)}) %collective-permute-start.9) | collective-permute-done | bytes 524320 | tf_op jit(solution)/shard_map/ppermute | solution.py:28
  54.3 0.3 collective-permute-done.8.rest_3_
  54.6 2.2 %collective-permute-start.12 = (bf16[1024,256]{1,0:T(8,128)(2,1)S(1)}, bf16[1024,256]{1,0:T(8,128)(2,1)S(1)}, u32[]{:S(2)}, u32[]{:S(2)}) collective-permute-start(bf16[1024,256]{1,0:T(8,128)(2,1)S(1)} %collective-permute-done.8.rest_3_), channel_id=1, source_target_pairs={{0,224},{32,0},{64,32},{96,64},{128,96},{160,128},{192,160},{224,1... | collective-permute-start | bytes 1572872 | tf_op jit(solution)/shard_map/ppermute | solution.py:28
  56.8 1.5 %collective-permute-start.14 = (bf16[528,256]{1,0:T(8,128)(2,1)S(1)}, bf16[528,256]{1,0:T(8,128)(2,1)S(1)}, u32[]{:S(2)}, u32[]{:S(2)}) collective-permute-start(bf16[528,256]{1,0:T(8,128)(2,1)S(1)} %slice_bitcast_fusion.5), channel_id=1, source_target_pairs={{0,2},{1,3},{2,0},{3,1},{4,6},{5,7},{6,4},{7,5},{8,10},{9,11},{10,... | collective-permute-start | bytes 811016 | tf_op jit(solution)/shard_map/ppermute | solution.py:23
  58.3 0.2 collective-permute-start.15
  58.5 9.5 %collective-permute-done.16.far = bf16[512,1024]{1,0:T(8,128)(2,1)S(1)} collective-permute-done((bf16[512,1024]{1,0:T(8,128)(2,1)S(1)}, bf16[512,1024]{1,0:T(8,128)(2,1)S(1)}, u32[]{:S(2)}, u32[]{:S(2)}) %collective-permute-start.16) | collective-permute-done | bytes 1048608 | tf_op jit(solution)/shard_map/ppermute | solution.py:23
  68.1 3.7 %weight_grads.1 = (bf16[512,1024]{1,0:T(8,128)(2,1)S(1)}, f32[512,128]{1,0:T(8,128)S(1)}, bf16[8,512,256]{2,1,0:T(8,128)(2,1)S(1)}, bf16[1024,256]{1,0:T(8,128)(...) custom-call(s32[8]{0:T(128)S(1)} %subtract_and_fusion.slot_ref, ...), custom_call_target="tpu_custom_call" | custom-call | tf_op jit(solution)/shard_map/weight_grads/pallas_call | solution.py:188
  71.7 0.4 collective-permute-start.18
  72.1 1.2 collective-permute-start.17
  73.3 2.4 %token_grads.1 = bf16[512,1024]{1,0:T(8,128)(2,1)S(1)} custom-call(f32[512,128]{1,0:T(8,128)S(1)} %get-tuple-element.95.r_ref, bf16[1,1024]{1,0:T(2,128)(2,1)S(1)} %copy-done.2, bf16[8,512,256]{2,1,0:T(8,128)(2,1)S(1)} %get-tuple-element.99.g_ref, bf16[1024,256]{1,0:T(8,128)(2,1)S(1)} %bitcast.72, bf16[1024,256]{1,0:T(8,128)(2,1)S(1)} %collective-permute-done.2.rest_1_, ...), custom_call_target="tpu_custom_call" | custom-call | tf_op jit(solution)/shard_map/token_grads/pallas_call | solution.py:188
  75.7 3.6 %keys_values.1 = bf16[8,528,256]{2,1,0:T(8,128)(2,1)S(1)} custom-call(s32[8]{0:T(128)S(1)} %select_reduce_fusion.place_ref, bf16[512,1024]{1,0:T(8,128)(2,1)S(1)} %get-tuple-element.94.normed_ref, f32[512,128]{1,0:T(8,128)S(1)} %get-tuple-element.95.r_ref, bf16[8,512,256]{2,1,0:T(8,128)(2,1)S(1)} %get-tuple-element.99.g_ref, bf16[1024,256]{1,0:T(8,128)(2,1)S(1)} %bitcast.73, ...), custom_call_target="tpu_custom_call" | custom-call | tf_op jit(solution)/shard_map/keys_values/pallas_call | solution.py:188
  79.3 0.8 collective-permute-start.20
  80.2 0.8 collective-permute-start.19
  80.9 0.7 collective-permute-start.25
  81.6 0.1 add.132
  81.7 0.1 add.131
  81.9 4.4 %collective-permute-done.20 = bf16[528,256]{1,0:T(8,128)(2,1)S(1)} collective-permute-done((bf16[528,256]{1,0:T(8,128)(2,1)S(1)}, bf16[528,256]{1,0:T(8,128)(2,1)S(1)}, u32[]{:S(2)}, u32[]{:S(2)}) %collective-permute-start.20) | collective-permute-done | bytes 270368 | tf_op jit(solution)/shard_map/ppermute | solution.py:23
  86.5 1.5 %collective-permute-start.24 = (bf16[2,528,256]{2,1,0:T(8,128)(2,1)S(1)}, bf16[2,528,256]{2,1,0:T(8,128)(2,1)S(1)}, u32[]{:S(2)}, u32[]{:S(2)}) collective-permute-start(bf16[2,528,256]{2,1,0:T(8,128)(2,1)S(1)} %pad_maximum_fusion.2), channel_id=1, source_target_pairs={{0,6},{1,7},{2,4},{3,5},{4,2},{5,3},{6,0},{7,1},{8,14},{9,15},{10,... | collective-permute-start | bytes 1622024 | tf_op jit(solution)/shard_map/ppermute | solution.py:23
  88.2 0.3 collective-permute-start.23
  88.5 0.4 collective-permute-start.21
  88.9 2.4 %collective-permute-start.22 = (bf16[1024,256]{1,0:T(8,128)(2,1)S(1)}, bf16[1024,256]{1,0:T(8,128)(2,1)S(1)}, u32[]{:S(2)}, u32[]{:S(2)}) collective-permute-start(bf16[1024,256]{1,0:T(8,128)(2,1)S(1)} %add.132), channel_id=1, source_target_pairs={{0,224},{32,0},{64,32},{96,64},{128,96},{160,128},{192,160},{224,1... | collective-permute-start | bytes 1572872 | tf_op jit(solution)/shard_map/ppermute | solution.py:28
  92.0 6.2 %collective-permute-done.21.arrived_ref = bf16[1024,256]{1,0:T(8,128)(2,1)S(1)} collective-permute-done((bf16[1024,256]{1,0:T(8,128)(2,1)S(1)}, bf16[1024,256]{1,0:T(8,128)(2,1)S(1)}, u32[]{:S(2)}, u32[]{:S(2)}) %collective-permute-start.21) | collective-permute-done | bytes 524320 | tf_op jit(solution)/shard_map/ppermute | solution.py:28
  98.1 0.1 add.133
  98.3 0.1 add.134
  98.4 3.6 %collective-permute-done.25 = bf16[512,1024]{1,0:T(8,128)(2,1)S(1)} collective-permute-done((bf16[512,1024]{1,0:T(8,128)(2,1)S(1)}, bf16[512,1024]{1,0:T(8,128)(2,1)S(1)}, u32[]{:S(2)}, u32[]{:S(2)}) %collective-permute-start.25) | collective-permute-done | bytes 1048608 | tf_op jit(solution)/shard_map/ppermute | solution.py:23
  102.0 0.3 convert_add_fusion.5
  102.4 1.5 %collective-permute-start.30 = (bf16[528,256]{1,0:T(8,128)(2,1)S(1)}, bf16[528,256]{1,0:T(8,128)(2,1)S(1)}, u32[]{:S(2)}, u32[]{:S(2)}) collective-permute-start(bf16[528,256]{1,0:T(8,128)(2,1)S(1)} %pad_maximum_fusion.7), channel_id=1, source_target_pairs={{0,17},{1,16},{2,19},{3,18},{4,21},{5,20},{6,23},{7,22},{8,25},{9,... | collective-permute-start | bytes 811016 | tf_op jit(solution)/shard_map/ppermute | solution.py:71
  103.9 0.4 collective-permute-start.26
  104.4 2.2 %collective-permute-start.27 = (bf16[1024,256]{1,0:T(8,128)(2,1)S(1)}, bf16[1024,256]{1,0:T(8,128)(2,1)S(1)}, u32[]{:S(2)}, u32[]{:S(2)}) collective-permute-start(bf16[1024,256]{1,0:T(8,128)(2,1)S(1)} %add.134), channel_id=1, source_target_pairs={{0,224},{32,0},{64,32},{96,64},{128,96},{160,128},{192,160},{224,1... | collective-permute-start | bytes 1572872 | tf_op jit(solution)/shard_map/ppermute | solution.py:28
  106.7 2.5 %collective-permute-start.29 = (bf16[528,256]{1,0:T(8,128)(2,1)S(1)}, bf16[528,256]{1,0:T(8,128)(2,1)S(1)}, u32[]{:S(2)}, u32[]{:S(2)}) collective-permute-start(bf16[528,256]{1,0:T(8,128)(2,1)S(1)} %pad_maximum_fusion.6), channel_id=1, source_target_pairs={{0,16},{1,17},{2,18},{3,19},{4,20},{5,21},{6,22},{7,23},{8,24},{9,... | collective-permute-start | bytes 811016 | tf_op jit(solution)/shard_map/ppermute | solution.py:71
  109.3 4.2 %collective-permute-done.26.plus_ref = bf16[1024,256]{1,0:T(8,128)(2,1)S(1)} collective-permute-done((bf16[1024,256]{1,0:T(8,128)(2,1)S(1)}, bf16[1024,256]{1,0:T(8,128)(2,1)S(1)}, u32[]{:S(2)}, u32[]{:S(2)}) %collective-permute-start.26) | collective-permute-done | bytes 524320 | tf_op jit(solution)/shard_map/ppermute | solution.py:28
  113.5 7.2 %collective-permute-start.32 = (bf16[512,1024]{1,0:T(8,128)(2,1)S(1)}, bf16[512,1024]{1,0:T(8,128)(2,1)S(1)}, u32[]{:S(2)}, u32[]{:S(2)}) collective-permute-start(bf16[512,1024]{1,0:T(8,128)(2,1)S(1)} %broadcast_select_fusion), channel_id=1, source_target_pairs={{0,8},{8,0},{16,24},{24,16},{1,9},{9,1},{17,25},{25,17},{2,10},{10... | collective-permute-start | bytes 3145736 | tf_op jit(solution)/shard_map/ppermute | solution.py:23
  121.3 0.8 collective-permute-start.31
  123.3 1.4 %collective-permute-start.33 = (bf16[512,256]{1,0:T(8,128)(2,1)S(1)}, bf16[512,256]{1,0:T(8,128)(2,1)S(1)}, u32[]{:S(2)}, u32[]{:S(2)}) collective-permute-start(bf16[512,256]{1,0:T(8,128)(2,1)S(1)} %add.135), channel_id=1, source_target_pairs={{0,32},{32,64},{64,96},{96,128},{128,160},{160,192},{192,224},{224... | collective-permute-start | bytes 786440 | tf_op jit(solution)/shard_map/ppermute | solution.py:28
  124.7 1.4 %collective-permute-start.34 = (bf16[512,256]{1,0:T(8,128)(2,1)S(1)}, bf16[512,256]{1,0:T(8,128)(2,1)S(1)}, u32[]{:S(2)}, u32[]{:S(2)}) collective-permute-start(bf16[512,256]{1,0:T(8,128)(2,1)S(1)} %add.136), channel_id=1, source_target_pairs={{0,224},{32,0},{64,32},{96,64},{128,96},{160,128},{192,160},{224,1... | collective-permute-start | bytes 786440 | tf_op jit(solution)/shard_map/ppermute | solution.py:28
  126.2 0.7 slice.257
  126.9 1.6 %subtract_convert_fusion = bf16[512,1024]{1,0:T(8,128)(2,1)} fusion(f32[512]{0:T(512)S(1)} %bitcast.80, bf16[512,1024]{1,0:T(8,128)(2,1)S(1)} %collective-permute-done.32, bf16[512,1024]{1,0:T(8,128)(2,1)S(1)} %token_grads.1, bf16[512,1024]{1,0:T(8,128)(2,1)S(1)} %collective-permute-done.25, pred[]{:T(512)} %bitcast.10, pred[]{:T(512)} %bitcast.9, ...), kind=kLoop, calls=%fused_computation | loop fusion | flops 3670016 | bytes 5244930 | tf_op jit(solution)/shard_map/convert_element_type | solution.py:387
  128.5 4.0 %collective-permute-done.33.plus_u = bf16[512,256]{1,0:T(8,128)(2,1)S(1)} collective-permute-done((bf16[512,256]{1,0:T(8,128)(2,1)S(1)}, bf16[512,256]{1,0:T(8,128)(2,1)S(1)}, u32[]{:S(2)}, u32[]{:S(2)}) %collective-permute-start.33) | collective-permute-done | bytes 262176 | tf_op jit(solution)/shard_map/ppermute | solution.py:28
  132.5 1.0 last.1
  (88 shorter events, 1.8 us)
Async XLA Ops:
  0.6 24.1 %copy-start = (bf16[1,1,2,256,1024]{4,3,2,1,0:T(8,128)(2,1)S(1)}, bf16[1,1,2,256,1024]{4,3,2,1,0:T(8,128)(2,1)}, u32[]{:S(2)}) copy-start(bf16[1,1,2,256,1024]{4,3,2,1,0:T(8,128)(2,1)} %param.6) | copy-start | bytes 3145732
  0.6 23.0 %copy-start.3 = (bf16[1,1,2,256,256]{4,3,2,1,0:T(8,128)(2,1)S(1)}, bf16[1,1,2,256,256]{4,3,2,1,0:T(8,128)(2,1)}, u32[]{:S(2)}) copy-start(bf16[1,1,2,256,256]{4,3,2,1,0:T(8,128)(2,1)} %param.11) | copy-start | bytes 786436
  0.7 15.6 %copy-start.1 = (bf16[1,1024,256]{2,1,0:T(8,128)(2,1)S(1)}, bf16[1,1024,256]{2,1,0:T(8,128)(2,1)}, u32[]{:S(2)}) copy-start(bf16[1,1024,256]{2,1,0:T(8,128)(2,1)} %param.8) | copy-start | bytes 1572868
  4.0 7.5 %collective-permute-start = (bf16[528,256]{1,0:T(8,128)(2,1)}, bf16[528,256]{1,0:T(8,128)(2,1)}, u32[]{:S(2)}, u32[]{:S(2)}) collective-permute-start(bf16[528,256]{1,0:T(8,128)(2,1)} %pad_maximum_fusion.5), channel_id=1, source_target_pairs={{0,8},{8,0},{16,24},{24,16},{1,9},{9,1},{17,25},{25,17},{2,10},{10... | collective-permute-start | bytes 811016 | tf_op jit(solution)/shard_map/ppermute | solution.py:23
  7.2 16.3 %collective-permute-start.4 = (bf16[1024,256]{1,0:T(8,128)(2,1)}, bf16[1024,256]{1,0:T(8,128)(2,1)S(1)}, u32[]{:S(2)}, u32[]{:S(2)}) collective-permute-start(bf16[1024,256]{1,0:T(8,128)(2,1)} %bitcast.70), channel_id=1, source_target_pairs={{0,32},{32,64},{64,96},{96,128},{128,160},{160,192},{192,224},{224... | collective-permute-start | bytes 1572872 | tf_op jit(solution)/shard_map/ppermute | solution.py:28
  7.2 17.5 %collective-permute-start.1 = (bf16[512,1024]{1,0:T(8,128)(2,1)}, bf16[512,1024]{1,0:T(8,128)(2,1)S(1)}, u32[]{:S(2)}, u32[]{:S(2)}) collective-permute-start(bf16[512,1024]{1,0:T(8,128)(2,1)} %bitcast.68), channel_id=1, source_target_pairs={{0,8},{8,0},{16,24},{24,16},{1,9},{9,1},{17,25},{25,17},{2,10},{10... | collective-permute-start | bytes 3145736 | tf_op jit(solution)/shard_map/ppermute | solution.py:23
  13.2 10.4 %collective-permute-start.6 = (bf16[528,256]{1,0:T(8,128)(2,1)S(1)}, bf16[528,256]{1,0:T(8,128)(2,1)S(1)}, u32[]{:S(2)}, u32[]{:S(2)}) collective-permute-start(bf16[528,256]{1,0:T(8,128)(2,1)S(1)} %broadcast_select_fusion.4), channel_id=1, source_target_pairs={{0,16},{1,17},{2,18},{3,19},{4,20},{5,21},{6,22},{7,23},{8,24},{9,... | collective-permute-start | bytes 811016 | tf_op jit(solution)/shard_map/ppermute | solution.py:71
  16.3 14.2 %collective-permute-start.2 = (bf16[1024,256]{1,0:T(8,128)(2,1)S(1)}, bf16[1024,256]{1,0:T(8,128)(2,1)S(1)}, u32[]{:S(2)}, u32[]{:S(2)}) collective-permute-start(bf16[1024,256]{1,0:T(8,128)(2,1)S(1)} %bitcast.71), channel_id=1, source_target_pairs={{0,224},{32,0},{64,32},{96,64},{128,96},{160,128},{192,160},{224,1... | collective-permute-start | bytes 1572872 | tf_op jit(solution)/shard_map/ppermute | solution.py:28
  24.9 14.5 %collective-permute-start.7 = (bf16[528,256]{1,0:T(8,128)(2,1)S(1)}, bf16[528,256]{1,0:T(8,128)(2,1)S(1)}, u32[]{:S(2)}, u32[]{:S(2)}) collective-permute-start(bf16[528,256]{1,0:T(8,128)(2,1)S(1)} %broadcast_select_fusion.3), channel_id=1, source_target_pairs={{0,1},{1,0},{2,3},{3,2},{4,5},{5,4},{6,7},{7,6},{8,9},{9,8},{10,11... | collective-permute-start | bytes 811016 | tf_op jit(solution)/shard_map/ppermute | solution.py:71
  30.5 8.5 %collective-permute-start.5 = (bf16[512,256]{1,0:T(8,128)(2,1)S(1)}, bf16[512,256]{1,0:T(8,128)(2,1)S(1)}, u32[]{:S(2)}, u32[]{:S(2)}) collective-permute-start(bf16[512,256]{1,0:T(8,128)(2,1)S(1)} %get-tuple-element.76), channel_id=1, source_target_pairs={{0,32},{32,64},{64,96},{96,128},{128,160},{160,192},{192,224},{224... | collective-permute-start | bytes 786440 | tf_op jit(solution)/shard_map/ppermute | solution.py:28
  31.2 8.2 %collective-permute-start.3 = (bf16[512,256]{1,0:T(8,128)(2,1)S(1)}, bf16[512,256]{1,0:T(8,128)(2,1)S(1)}, u32[]{:S(2)}, u32[]{:S(2)}) collective-permute-start(bf16[512,256]{1,0:T(8,128)(2,1)S(1)} %get-tuple-element.75), channel_id=1, source_target_pairs={{0,224},{32,0},{64,32},{96,64},{128,96},{160,128},{192,160},{224,1... | collective-permute-start | bytes 786440 | tf_op jit(solution)/shard_map/ppermute | solution.py:28
  39.4 28.6 %copy-start.2 = (bf16[1,1024]{1,0:T(2,128)(2,1)S(1)}, bf16[1,1024]{1,0:T(2,128)(2,1)}, u32[]{:S(2)}) copy-start(bf16[1,1024]{1,0:T(2,128)(2,1)} %gain_ref.3) | copy-start | bytes 6148
  39.5 15.1 %collective-permute-start.11 = (bf16[2,528,256]{2,1,0:T(8,128)(2,1)S(1)}, bf16[2,528,256]{2,1,0:T(8,128)(2,1)S(1)}, u32[]{:S(2)}, u32[]{:S(2)}) collective-permute-start(bf16[2,528,256]{2,1,0:T(8,128)(2,1)S(1)} %pad_maximum_fusion.rest_0_), channel_id=1, source_target_pairs={{0,6},{1,7},{2,4},{3,5},{4,2},{5,3},{6,0},{7,1},{8,14},{9,15},{10,... | collective-permute-start | bytes 1622024 | tf_op jit(solution)/shard_map/ppermute | solution.py:23
  42.1 12.5 %collective-permute-start.10 = (bf16[2,528,256]{2,1,0:T(8,128)(2,1)S(1)}, bf16[2,528,256]{2,1,0:T(8,128)(2,1)S(1)}, u32[]{:S(2)}, u32[]{:S(2)}) collective-permute-start(bf16[2,528,256]{2,1,0:T(8,128)(2,1)S(1)} %pad_maximum_fusion.rest_0_), channel_id=1, source_target_pairs={{0,2},{1,3},{2,0},{3,1},{4,6},{5,7},{6,4},{7,5},{8,10},{9,11},{10,... | collective-permute-start | bytes 1622024 | tf_op jit(solution)/shard_map/ppermute | solution.py:23
  42.1 12.1 %collective-permute-start.9 = (bf16[1024,256]{1,0:T(8,128)(2,1)S(1)}, bf16[1024,256]{1,0:T(8,128)(2,1)S(1)}, u32[]{:S(2)}, u32[]{:S(2)}) collective-permute-start(bf16[1024,256]{1,0:T(8,128)(2,1)S(1)} %pad_maximum_fusion.4), channel_id=1, source_target_pairs={{0,32},{32,64},{64,96},{96,128},{128,160},{160,192},{192,224},{224... | collective-permute-start | bytes 1572872 | tf_op jit(solution)/shard_map/ppermute | solution.py:28
  44.3 10.3 %collective-permute-start.8 = (bf16[1024,256]{1,0:T(8,128)(2,1)S(1)}, bf16[1024,256]{1,0:T(8,128)(2,1)S(1)}, u32[]{:S(2)}, u32[]{:S(2)}) collective-permute-start(bf16[1024,256]{1,0:T(8,128)(2,1)S(1)} %pad_maximum_fusion.3), channel_id=1, source_target_pairs={{0,224},{32,0},{64,32},{96,64},{128,96},{160,128},{192,160},{224,1... | collective-permute-start | bytes 1572872 | tf_op jit(solution)/shard_map/ppermute | solution.py:28
  45.0 23.0 %collective-permute-start.16 = (bf16[512,1024]{1,0:T(8,128)(2,1)S(1)}, bf16[512,1024]{1,0:T(8,128)(2,1)S(1)}, u32[]{:S(2)}, u32[]{:S(2)}) collective-permute-start(bf16[512,1024]{1,0:T(8,128)(2,1)S(1)} %broadcast_select_fusion.1), channel_id=1, source_target_pairs={{0,16},{8,24},{16,0},{24,8},{1,17},{9,25},{17,1},{25,9},{2,18},{10... | collective-permute-start | bytes 3145736 | tf_op jit(solution)/shard_map/ppermute | solution.py:23
  54.6 13.4 %collective-permute-start.12 = (bf16[1024,256]{1,0:T(8,128)(2,1)S(1)}, bf16[1024,256]{1,0:T(8,128)(2,1)S(1)}, u32[]{:S(2)}, u32[]{:S(2)}) collective-permute-start(bf16[1024,256]{1,0:T(8,128)(2,1)S(1)} %collective-permute-done.8.rest_3_), channel_id=1, source_target_pairs={{0,224},{32,0},{64,32},{96,64},{128,96},{160,128},{192,160},{224,1... | collective-permute-start | bytes 1572872 | tf_op jit(solution)/shard_map/ppermute | solution.py:28
  56.8 11.3 %collective-permute-start.13 = (bf16[1024,256]{1,0:T(8,128)(2,1)S(1)}, bf16[1024,256]{1,0:T(8,128)(2,1)S(1)}, u32[]{:S(2)}, u32[]{:S(2)}) collective-permute-start(bf16[1024,256]{1,0:T(8,128)(2,1)S(1)} %collective-permute-done.9.rest_7_), channel_id=1, source_target_pairs={{0,32},{32,64},{64,96},{96,128},{128,160},{160,192},{192,224},{224... | collective-permute-start | bytes 1572872 | tf_op jit(solution)/shard_map/ppermute | solution.py:28
  56.8 11.2 %collective-permute-start.14 = (bf16[528,256]{1,0:T(8,128)(2,1)S(1)}, bf16[528,256]{1,0:T(8,128)(2,1)S(1)}, u32[]{:S(2)}, u32[]{:S(2)}) collective-permute-start(bf16[528,256]{1,0:T(8,128)(2,1)S(1)} %slice_bitcast_fusion.5), channel_id=1, source_target_pairs={{0,2},{1,3},{2,0},{3,1},{4,6},{5,7},{6,4},{7,5},{8,10},{9,11},{10,... | collective-permute-start | bytes 811016 | tf_op jit(solution)/shard_map/ppermute | solution.py:23
  58.3 9.7 %collective-permute-start.15 = (bf16[528,256]{1,0:T(8,128)(2,1)S(1)}, bf16[528,256]{1,0:T(8,128)(2,1)S(1)}, u32[]{:S(2)}, u32[]{:S(2)}) collective-permute-start(bf16[528,256]{1,0:T(8,128)(2,1)S(1)} %slice_bitcast_fusion.4), channel_id=1, source_target_pairs={{0,6},{1,7},{2,4},{3,5},{4,2},{5,3},{6,0},{7,1},{8,14},{9,15},{10,... | collective-permute-start | bytes 811016 | tf_op jit(solution)/shard_map/ppermute | solution.py:23
  71.7 9.9 %collective-permute-start.18 = (bf16[1024,256]{1,0:T(8,128)(2,1)S(1)}, bf16[1024,256]{1,0:T(8,128)(2,1)S(1)}, u32[]{:S(2)}, u32[]{:S(2)}) collective-permute-start(bf16[1024,256]{1,0:T(8,128)(2,1)S(1)} %get-tuple-element.103), channel_id=1, source_target_pairs={{0,224},{32,0},{64,32},{96,64},{128,96},{160,128},{192,160},{224,1... | collective-permute-start | bytes 1572872 | tf_op jit(solution)/shard_map/ppermute | solution.py:28
  72.1 9.6 %collective-permute-start.17 = (bf16[1024,256]{1,0:T(8,128)(2,1)S(1)}, bf16[1024,256]{1,0:T(8,128)(2,1)S(1)}, u32[]{:S(2)}, u32[]{:S(2)}) collective-permute-start(bf16[1024,256]{1,0:T(8,128)(2,1)S(1)} %get-tuple-element.100), channel_id=1, source_target_pairs={{0,32},{32,64},{64,96},{96,128},{128,160},{160,192},{192,224},{224... | collective-permute-start | bytes 1572872 | tf_op jit(solution)/shard_map/ppermute | solution.py:28
  79.3 6.9 %collective-permute-start.20 = (bf16[528,256]{1,0:T(8,128)(2,1)S(1)}, bf16[528,256]{1,0:T(8,128)(2,1)S(1)}, u32[]{:S(2)}, u32[]{:S(2)}) collective-permute-start(bf16[528,256]{1,0:T(8,128)(2,1)S(1)} %get-tuple-element.141), channel_id=1, source_target_pairs={{0,6},{1,7},{2,4},{3,5},{4,2},{5,3},{6,0},{7,1},{8,14},{9,15},{10,... | collective-permute-start | bytes 811016 | tf_op jit(solution)/shard_map/ppermute | solution.py:23
  80.2 6.1 %collective-permute-start.19 = (bf16[528,256]{1,0:T(8,128)(2,1)S(1)}, bf16[528,256]{1,0:T(8,128)(2,1)S(1)}, u32[]{:S(2)}, u32[]{:S(2)}) collective-permute-start(bf16[528,256]{1,0:T(8,128)(2,1)S(1)} %get-tuple-element.142), channel_id=1, source_target_pairs={{0,2},{1,3},{2,0},{3,1},{4,6},{5,7},{6,4},{7,5},{8,10},{9,11},{10,... | collective-permute-start | bytes 811016 | tf_op jit(solution)/shard_map/ppermute | solution.py:23
  80.9 21.1 %collective-permute-start.25 = (bf16[512,1024]{1,0:T(8,128)(2,1)S(1)}, bf16[512,1024]{1,0:T(8,128)(2,1)S(1)}, u32[]{:S(2)}, u32[]{:S(2)}) collective-permute-start(bf16[512,1024]{1,0:T(8,128)(2,1)S(1)} %token_grads.1), channel_id=1, source_target_pairs={{0,16},{8,24},{16,0},{24,8},{1,17},{9,25},{17,1},{25,9},{2,18},{10... | collective-permute-start | bytes 3145736 | tf_op jit(solution)/shard_map/ppermute | solution.py:23
  86.5 15.4 %collective-permute-start.24 = (bf16[2,528,256]{2,1,0:T(8,128)(2,1)S(1)}, bf16[2,528,256]{2,1,0:T(8,128)(2,1)S(1)}, u32[]{:S(2)}, u32[]{:S(2)}) collective-permute-start(bf16[2,528,256]{2,1,0:T(8,128)(2,1)S(1)} %pad_maximum_fusion.2), channel_id=1, source_target_pairs={{0,6},{1,7},{2,4},{3,5},{4,2},{5,3},{6,0},{7,1},{8,14},{9,15},{10,... | collective-permute-start | bytes 1622024 | tf_op jit(solution)/shard_map/ppermute | solution.py:23
  88.2 13.8 %collective-permute-start.23 = (bf16[2,528,256]{2,1,0:T(8,128)(2,1)S(1)}, bf16[2,528,256]{2,1,0:T(8,128)(2,1)S(1)}, u32[]{:S(2)}, u32[]{:S(2)}) collective-permute-start(bf16[2,528,256]{2,1,0:T(8,128)(2,1)S(1)} %pad_maximum_fusion.1), channel_id=1, source_target_pairs={{0,2},{1,3},{2,0},{3,1},{4,6},{5,7},{6,4},{7,5},{8,10},{9,11},{10,... | collective-permute-start | bytes 1622024 | tf_op jit(solution)/shard_map/ppermute | solution.py:23
  88.5 9.7 %collective-permute-start.21 = (bf16[1024,256]{1,0:T(8,128)(2,1)S(1)}, bf16[1024,256]{1,0:T(8,128)(2,1)S(1)}, u32[]{:S(2)}, u32[]{:S(2)}) collective-permute-start(bf16[1024,256]{1,0:T(8,128)(2,1)S(1)} %add.131), channel_id=1, source_target_pairs={{0,32},{32,64},{64,96},{96,128},{128,160},{160,192},{192,224},{224... | collective-permute-start | bytes 1572872 | tf_op jit(solution)/shard_map/ppermute | solution.py:28
  88.9 9.4 %collective-permute-start.22 = (bf16[1024,256]{1,0:T(8,128)(2,1)S(1)}, bf16[1024,256]{1,0:T(8,128)(2,1)S(1)}, u32[]{:S(2)}, u32[]{:S(2)}) collective-permute-start(bf16[1024,256]{1,0:T(8,128)(2,1)S(1)} %add.132), channel_id=1, source_target_pairs={{0,224},{32,0},{64,32},{96,64},{128,96},{160,128},{192,160},{224,1... | collective-permute-start | bytes 1572872 | tf_op jit(solution)/shard_map/ppermute | solution.py:28
  102.4 18.5 %collective-permute-start.30 = (bf16[528,256]{1,0:T(8,128)(2,1)S(1)}, bf16[528,256]{1,0:T(8,128)(2,1)S(1)}, u32[]{:S(2)}, u32[]{:S(2)}) collective-permute-start(bf16[528,256]{1,0:T(8,128)(2,1)S(1)} %pad_maximum_fusion.7), channel_id=1, source_target_pairs={{0,17},{1,16},{2,19},{3,18},{4,21},{5,20},{6,23},{7,22},{8,25},{9,... | collective-permute-start | bytes 811016 | tf_op jit(solution)/shard_map/ppermute | solution.py:71
  103.9 17.0 %collective-permute-start.28 = (bf16[528,256]{1,0:T(8,128)(2,1)S(1)}, bf16[528,256]{1,0:T(8,128)(2,1)S(1)}, u32[]{:S(2)}, u32[]{:S(2)}) collective-permute-start(bf16[528,256]{1,0:T(8,128)(2,1)S(1)} %pad_maximum_fusion.7), channel_id=1, source_target_pairs={{0,1},{1,0},{2,3},{3,2},{4,5},{5,4},{6,7},{7,6},{8,9},{9,8},{10,11... | collective-permute-start | bytes 811016 | tf_op jit(solution)/shard_map/ppermute | solution.py:71
  103.9 9.5 %collective-permute-start.26 = (bf16[1024,256]{1,0:T(8,128)(2,1)S(1)}, bf16[1024,256]{1,0:T(8,128)(2,1)S(1)}, u32[]{:S(2)}, u32[]{:S(2)}) collective-permute-start(bf16[1024,256]{1,0:T(8,128)(2,1)S(1)} %add.133), channel_id=1, source_target_pairs={{0,32},{32,64},{64,96},{96,128},{128,160},{160,192},{192,224},{224... | collective-permute-start | bytes 1572872 | tf_op jit(solution)/shard_map/ppermute | solution.py:28
  104.4 16.4 %collective-permute-start.27 = (bf16[1024,256]{1,0:T(8,128)(2,1)S(1)}, bf16[1024,256]{1,0:T(8,128)(2,1)S(1)}, u32[]{:S(2)}, u32[]{:S(2)}) collective-permute-start(bf16[1024,256]{1,0:T(8,128)(2,1)S(1)} %add.134), channel_id=1, source_target_pairs={{0,224},{32,0},{64,32},{96,64},{128,96},{160,128},{192,160},{224,1... | collective-permute-start | bytes 1572872 | tf_op jit(solution)/shard_map/ppermute | solution.py:28
  106.7 14.3 %collective-permute-start.29 = (bf16[528,256]{1,0:T(8,128)(2,1)S(1)}, bf16[528,256]{1,0:T(8,128)(2,1)S(1)}, u32[]{:S(2)}, u32[]{:S(2)}) collective-permute-start(bf16[528,256]{1,0:T(8,128)(2,1)S(1)} %pad_maximum_fusion.6), channel_id=1, source_target_pairs={{0,16},{1,17},{2,18},{3,19},{4,20},{5,21},{6,22},{7,23},{8,24},{9,... | collective-permute-start | bytes 811016 | tf_op jit(solution)/shard_map/ppermute | solution.py:71
  113.5 13.5 %collective-permute-start.32 = (bf16[512,1024]{1,0:T(8,128)(2,1)S(1)}, bf16[512,1024]{1,0:T(8,128)(2,1)S(1)}, u32[]{:S(2)}, u32[]{:S(2)}) collective-permute-start(bf16[512,1024]{1,0:T(8,128)(2,1)S(1)} %broadcast_select_fusion), channel_id=1, source_target_pairs={{0,8},{8,0},{16,24},{24,16},{1,9},{9,1},{17,25},{25,17},{2,10},{10... | collective-permute-start | bytes 3145736 | tf_op jit(solution)/shard_map/ppermute | solution.py:23
  121.3 4.8 %collective-permute-start.31 = (bf16[528,256]{1,0:T(8,128)(2,1)S(1)}, bf16[528,256]{1,0:T(8,128)(2,1)S(1)}, u32[]{:S(2)}, u32[]{:S(2)}) collective-permute-start(bf16[528,256]{1,0:T(8,128)(2,1)S(1)} %broadcast_select_fusion.2), channel_id=1, source_target_pairs={{0,8},{8,0},{16,24},{24,16},{1,9},{9,1},{17,25},{25,17},{2,10},{10... | collective-permute-start | bytes 811016 | tf_op jit(solution)/shard_map/ppermute | solution.py:23
  123.3 9.2 %collective-permute-start.33 = (bf16[512,256]{1,0:T(8,128)(2,1)S(1)}, bf16[512,256]{1,0:T(8,128)(2,1)S(1)}, u32[]{:S(2)}, u32[]{:S(2)}) collective-permute-start(bf16[512,256]{1,0:T(8,128)(2,1)S(1)} %add.135), channel_id=1, source_target_pairs={{0,32},{32,64},{64,96},{96,128},{128,160},{160,192},{192,224},{224... | collective-permute-start | bytes 786440 | tf_op jit(solution)/shard_map/ppermute | solution.py:28
  124.7 7.8 %collective-permute-start.34 = (bf16[512,256]{1,0:T(8,128)(2,1)S(1)}, bf16[512,256]{1,0:T(8,128)(2,1)S(1)}, u32[]{:S(2)}, u32[]{:S(2)}) collective-permute-start(bf16[512,256]{1,0:T(8,128)(2,1)S(1)} %add.136), channel_id=1, source_target_pairs={{0,224},{32,0},{64,32},{96,64},{128,96},{160,128},{192,160},{224,1... | collective-permute-start | bytes 786440 | tf_op jit(solution)/shard_map/ppermute | solution.py:28

commit v3 on v2

--- a/solution.py
+++ b/solution.py
@@ -79,7 +79,7 @@
 
 
 def dw_kernel(model, slot_ref, pick_ref, x_ref, other, far, gain_ref, *rest):
-    g0, g1, g2a, g2b, g3, normed_ref, r_ref, g_ref, own, p1, p2, p3, p4, m1, m2, m3, m4 = rest
+    g0, g1, g2a, g2b, g3, normed_ref, r_ref, g_ref, p1, m1 = rest
     rows, feats = normed_ref.shape
     top, half = rows // 2, feats // 2
     pieces = (g0.at[0], g0.at[1], g1.at[0], g1.at[1], g2a, g2b, g3.at[0], g3.at[1])
@@ -97,12 +97,21 @@
 
     for q in range(8):
         g_ref[slot_ref[q]] = pieces[q][:rows, :]
-    uppers = (own, p4, p3, p2, p1, m1, m2, m3)
-    lowers = (own, p3, p2, p1, m1, m2, m3, m4)
     for f in range(0, feats, 256):
         turned = normed_ref[:, f : f + 256].T
-        for d in range(8):
-            out_ref = uppers[d] if f < half else lowers[d]
+        for d, out_ref in ((4, p1), (5, m1)) if f < half else ((3, p1), (4, m1)):
+            grads = jnp.dot(turned, g_ref[d], preferred_element_type=F32)
+            out_ref[f : f + 256, :] = grads.astype(BF16)
+
+
+def dw_rest_kernel(normed_ref, g_ref, own, p2, p3, p4, m2, m3, m4):
+    feats = normed_ref.shape[1]
+    half = feats // 2
+    uppers = ((0, own), (1, p4), (2, p3), (3, p2), (6, m2), (7, m3))
+    lowers = ((0, own), (1, p3), (2, p2), (5, m2), (6, m3), (7, m4))
+    for f in range(0, feats, 256):
+        turned = normed_ref[:, f : f + 256].T
+        for d, out_ref in uppers if f < half else lowers:
             at = f - half if out_ref is m4 else f
             grads = jnp.dot(turned, g_ref[d], preferred_element_type=F32)
             out_ref[at : at + 256, :] = grads.astype(BF16)
@@ -308,17 +317,15 @@
 
     whole = jax.ShapeDtypeStruct((feats, cols), BF16)
     part = jax.ShapeDtypeStruct((half, cols), BF16)
-    normed, r, g, own, p1, p2, p3, p4, m1, m2, m3, m4 = kernel_call(
+    normed, r, g, p1, m1 = kernel_call(
         functools.partial(dw_kernel, model),
         "weight_grads",
         (
             jax.ShapeDtypeStruct((rows, feats), BF16),
             jax.ShapeDtypeStruct((rows, 128), F32),
             jax.ShapeDtypeStruct((pipes, rows, cols), BF16),
-            *[whole] * 4,
-            part,
-            *[whole] * 3,
-            part,
+            whole,
+            whole,
         ),
         (slots, pick, x_own, x_other, x_far, norm_gain, pair, g1, g2a, g2b, g3),
         index=2,
@@ -337,6 +344,13 @@
         "keys_values",
         (jax.ShapeDtypeStruct((tensors, rows + EXTRA, cols), BF16),),
         (places, normed, r, after(g, a), *weights),
+    )
+    own, p2, p3, p4, m2, m3, m4 = kernel_call(
+        dw_rest_kernel,
+        "more_weight_grads",
+        (whole, whole, whole, part, whole, whole, part),
+        (after(normed, y, a), g),
+        index=0,
     )
     to3, to1 = swap(y[4], "tensor", 2), swap(y[5], "tensor", 6)
     a_far = swap(a, "section", 2)

time: 134 us -> 133 us (level)
    pallas_call x3 -> x4, Pallas kernels: 9.63 us -> 9.82 us  [kernel_call(): pl.pallas_call(body, out_shape=out_shape, in_specs=[SMEM] * index + [VMEM...]
  transfers between devices with their start and end apart: 35 -> 35, of which waited for: 12 -> 13; matrix products, arithmetic and copies ran while one was open for 6% -> 6% of each run, Pallas kernels for 5% -> 6%
where the time goes in v3:
time: 133 us; the launch traced here: 132 us
  waiting for transfers between devices  52.4 us (39%)
  starting transfers between devices  50.7 us (38%)
  Pallas kernels  11.4 us (9%)
  other arithmetic  10.4 us (8%)
  between operations  6.3 us (5%)
    ppermute x16, waiting for transfers between devices, shift(): return lax.ppermute(x, axis, [(i, (i + step) % size) for i in range(size)])  36.2 us
    ppermute x16, starting transfers between devices, shift(): return lax.ppermute(x, axis, [(i, (i + step) % size) for i in range(size)])  22.1 us
    ppermute x14, starting transfers between devices, swap(): return lax.ppermute(x, axis, [(i, i ^ bits) for i in range(size)])  20.2 us
    ppermute x14, waiting for transfers between devices, swap(): return lax.ppermute(x, axis, [(i, i ^ bits) for i in range(size)])  16.2 us
    pallas_call x4, Pallas kernels, kernel_call(): pl.pallas_call(body, out_shape=out_shape, in_specs=[SMEM] * index + [VMEM...  9.82 us
    ppermute x5, starting transfers between devices, y_swap(): return lax.ppermute(x, ('section', 'tensor'), y_pairs(hi, lo))  8.34 us
  transfers between devices with their start and end apart: 35, of which 13 were waited for; matrix products, arithmetic and copies ran while one was open for 6% of the time, Pallas kernels for 6%

profile of v3, /device:TPU:1, one launch (start us, length us, event | category | flops | bytes accessed | tf_op | source)
XLA Modules:
  0.0 132.3 jit_solution(12347737422751379852)
XLA Ops:
  0.7 1.6 %multiply_reduce_fusion = f32[2,256]{1,0:T(2,128)S(1)} fusion(bf16[1,1,2,256,1024]{4,3,2,1,0:T(8,128)(2,1)} %param.6), kind=kLoop, calls=%fused_computation.1 | loop fusion | flops 1572352 | bytes 1050624 | tf_op jit(solution)/shard_map/reduce_sum | solution.py:276
  2.3 1.7 %pad_maximum_fusion.5 = bf16[528,256]{1,0:T(8,128)(2,1)} fusion(bf16[16,256]{1,0:T(8,128)(2,1)S(1)} %fusion.16, bf16[512,256]{1,0:T(8,128)(2,1)} %bitcast.74), kind=kLoop, calls=%fused_computation.25 | loop fusion | flops 540672 | bytes 540672 | tf_op jit(solution)/shard_map/concatenate | solution.py:277
  4.0 3.2 %collective-permute-start = (bf16[528,256]{1,0:T(8,128)(2,1)}, bf16[528,256]{1,0:T(8,128)(2,1)}, u32[]{:S(2)}, u32[]{:S(2)}) collective-permute-start(bf16[528,256]{1,0:T(8,128)(2,1)} %pad_maximum_fusion.5), channel_id=1, source_target_pairs={{0,8},{8,0},{16,24},{24,16},{1,9},{9,1},{17,25},{25,17},{2,10},{10... | collective-permute-start | bytes 811016 | tf_op jit(solution)/shard_map/ppermute | solution.py:23
  7.2 0.2 collective-permute-start.1
  7.4 0.8 select_reduce_fusion.4
  8.4 0.8 fusion.35
  10.4 0.8 select_reduce_fusion.2
  11.2 0.2 select_reduce_fusion.1
  12.2 1.1 broadcast_select_fusion.4
  13.3 2.9 %collective-permute-start.6 = (bf16[528,256]{1,0:T(8,128)(2,1)S(1)}, bf16[528,256]{1,0:T(8,128)(2,1)S(1)}, u32[]{:S(2)}, u32[]{:S(2)}) collective-permute-start(bf16[528,256]{1,0:T(8,128)(2,1)S(1)} %broadcast_select_fusion.4), channel_id=1, source_target_pairs={{0,16},{1,17},{2,18},{3,19},{4,20},{5,21},{6,22},{7,23},{8,24},{9,... | collective-permute-start | bytes 811016 | tf_op jit(solution)/shard_map/ppermute | solution.py:71
  16.2 3.8 %collective-permute-start.2 = (bf16[1024,256]{1,0:T(8,128)(2,1)S(1)}, bf16[1024,256]{1,0:T(8,128)(2,1)S(1)}, u32[]{:S(2)}, u32[]{:S(2)}) collective-permute-start(bf16[1024,256]{1,0:T(8,128)(2,1)S(1)} %bitcast.71), channel_id=1, source_target_pairs={{0,224},{32,0},{64,32},{96,64},{128,96},{160,128},{192,160},{224,1... | collective-permute-start | bytes 1572872 | tf_op jit(solution)/shard_map/ppermute | solution.py:28
  21.3 2.3 %collective-permute-done.4.rest_5_ = bf16[1024,256]{1,0:T(8,128)(2,1)S(1)} collective-permute-done((bf16[1024,256]{1,0:T(8,128)(2,1)}, bf16[1024,256]{1,0:T(8,128)(2,1)S(1)}, u32[]{:S(2)}, u32[]{:S(2)}) %collective-permute-start.4) | collective-permute-done | bytes 524320 | tf_op jit(solution)/shard_map/ppermute | solution.py:28
  23.6 0.1 broadcast_select_fusion.3
  23.8 0.2 broadcast_select_fusion.1
  24.0 1.4 %collective-permute-start.7 = (bf16[528,256]{1,0:T(8,128)(2,1)S(1)}, bf16[528,256]{1,0:T(8,128)(2,1)S(1)}, u32[]{:S(2)}, u32[]{:S(2)}) collective-permute-start(bf16[528,256]{1,0:T(8,128)(2,1)S(1)} %broadcast_select_fusion.3), channel_id=1, source_target_pairs={{0,1},{1,0},{2,3},{3,2},{4,5},{5,4},{6,7},{7,6},{8,9},{9,8},{10,11... | collective-permute-start | bytes 811016 | tf_op jit(solution)/shard_map/ppermute | solution.py:71
  25.4 5.1 %collective-permute-done.2.rest_1_ = bf16[1024,256]{1,0:T(8,128)(2,1)S(1)} collective-permute-done((bf16[1024,256]{1,0:T(8,128)(2,1)S(1)}, bf16[1024,256]{1,0:T(8,128)(2,1)S(1)}, u32[]{:S(2)}, u32[]{:S(2)}) %collective-permute-start.2) | collective-permute-done | bytes 524320 | tf_op jit(solution)/shard_map/ppermute | solution.py:28
  30.5 1.0 collective-permute-start.5
  31.5 2.6 %collective-permute-start.3 = (bf16[512,256]{1,0:T(8,128)(2,1)S(1)}, bf16[512,256]{1,0:T(8,128)(2,1)S(1)}, u32[]{:S(2)}, u32[]{:S(2)}) collective-permute-start(bf16[512,256]{1,0:T(8,128)(2,1)S(1)} %get-tuple-element.76), channel_id=1, source_target_pairs={{0,224},{32,0},{64,32},{96,64},{128,96},{160,128},{192,160},{224,1... | collective-permute-start | bytes 786440 | tf_op jit(solution)/shard_map/ppermute | solution.py:28
  34.1 4.9 %collective-permute-done.5.rest_6_ = bf16[512,256]{1,0:T(8,128)(2,1)S(1)} collective-permute-done((bf16[512,256]{1,0:T(8,128)(2,1)S(1)}, bf16[512,256]{1,0:T(8,128)(2,1)S(1)}, u32[]{:S(2)}, u32[]{:S(2)}) %collective-permute-start.5) | collective-permute-done | bytes 262176 | tf_op jit(solution)/shard_map/ppermute | solution.py:28
  38.9 0.6 collective-permute-done.3.rest_2_
  39.7 2.6 %collective-permute-start.11 = (bf16[2,528,256]{2,1,0:T(8,128)(2,1)S(1)}, bf16[2,528,256]{2,1,0:T(8,128)(2,1)S(1)}, u32[]{:S(2)}, u32[]{:S(2)}) collective-permute-start(bf16[2,528,256]{2,1,0:T(8,128)(2,1)S(1)} %pad_maximum_fusion.rest_0_), channel_id=1, source_target_pairs={{0,6},{1,7},{2,4},{3,5},{4,2},{5,3},{6,0},{7,1},{8,14},{9,15},{10,... | collective-permute-start | bytes 1622024 | tf_op jit(solution)/shard_map/ppermute | solution.py:23
  42.3 2.1 %collective-permute-start.9 = (bf16[1024,256]{1,0:T(8,128)(2,1)S(1)}, bf16[1024,256]{1,0:T(8,128)(2,1)S(1)}, u32[]{:S(2)}, u32[]{:S(2)}) collective-permute-start(bf16[1024,256]{1,0:T(8,128)(2,1)S(1)} %pad_maximum_fusion.4), channel_id=1, source_target_pairs={{0,32},{32,64},{64,96},{96,128},{128,160},{160,192},{192,224},{224... | collective-permute-start | bytes 1572872 | tf_op jit(solution)/shard_map/ppermute | solution.py:28
  44.4 0.7 collective-permute-start.8
  45.2 0.1 collective-permute-start.16
  45.3 9.2 %collective-permute-done.9.rest_7_ = bf16[1024,256]{1,0:T(8,128)(2,1)S(1)} collective-permute-done((bf16[1024,256]{1,0:T(8,128)(2,1)S(1)}, bf16[1024,256]{1,0:T(8,128)(2,1)S(1)}, u32[]{:S(2)}, u32[]{:S(2)}) %collective-permute-start.9) | collective-permute-done | bytes 524320 | tf_op jit(solution)/shard_map/ppermute | solution.py:28
  54.5 0.3 collective-permute-done.8.rest_3_
  54.9 2.2 %collective-permute-start.12 = (bf16[1024,256]{1,0:T(8,128)(2,1)S(1)}, bf16[1024,256]{1,0:T(8,128)(2,1)S(1)}, u32[]{:S(2)}, u32[]{:S(2)}) collective-permute-start(bf16[1024,256]{1,0:T(8,128)(2,1)S(1)} %collective-permute-done.8.rest_3_), channel_id=1, source_target_pairs={{0,224},{32,0},{64,32},{96,64},{128,96},{160,128},{192,160},{224,1... | collective-permute-start | bytes 1572872 | tf_op jit(solution)/shard_map/ppermute | solution.py:28
  57.1 1.5 %collective-permute-start.14 = (bf16[528,256]{1,0:T(8,128)(2,1)S(1)}, bf16[528,256]{1,0:T(8,128)(2,1)S(1)}, u32[]{:S(2)}, u32[]{:S(2)}) collective-permute-start(bf16[528,256]{1,0:T(8,128)(2,1)S(1)} %slice_bitcast_fusion.5), channel_id=1, source_target_pairs={{0,2},{1,3},{2,0},{3,1},{4,6},{5,7},{6,4},{7,5},{8,10},{9,11},{10,... | collective-permute-start | bytes 811016 | tf_op jit(solution)/shard_map/ppermute | solution.py:23
  58.6 0.2 collective-permute-start.15
  58.8 9.5 %collective-permute-done.16.far = bf16[512,1024]{1,0:T(8,128)(2,1)S(1)} collective-permute-done((bf16[512,1024]{1,0:T(8,128)(2,1)S(1)}, bf16[512,1024]{1,0:T(8,128)(2,1)S(1)}, u32[]{:S(2)}, u32[]{:S(2)}) %collective-permute-start.16) | collective-permute-done | bytes 1048608 | tf_op jit(solution)/shard_map/ppermute | solution.py:23
  68.3 2.0 %weight_grads.1 = (bf16[512,1024]{1,0:T(8,128)(2,1)S(1)}, f32[512,128]{1,0:T(8,128)S(1)}, bf16[8,512,256]{2,1,0:T(8,128)(2,1)S(1)}, bf16[1024,256]{1,0:T(8,128)(2,1)S(1)}, bf16[1024,256]{1,0:T(8,128)(2,1)S(1)}) custom-call(s32[8]{0:T(128)S(1)} %subtract_and_fusion.slot_ref, s32[1]{0:T(128)} %bitcast.8.pick_ref, bf16[512,1024]{1,0:T(8,128)(2,1)S(1)} %bitcast.69, ...), custom_call_target="tpu_custom_call" | custom-call | tf_op jit(solution)/shard_map/weight_grads/pallas_call | solution.py:197
  70.5 1.5 %collective-permute-start.17 = (bf16[1024,256]{1,0:T(8,128)(2,1)S(1)}, bf16[1024,256]{1,0:T(8,128)(2,1)S(1)}, u32[]{:S(2)}, u32[]{:S(2)}) collective-permute-start(bf16[1024,256]{1,0:T(8,128)(2,1)S(1)} %get-tuple-element.101), channel_id=1, source_target_pairs={{0,32},{32,64},{64,96},{96,128},{128,160},{160,192},{192,224},{224... | collective-permute-start | bytes 1572872 | tf_op jit(solution)/shard_map/ppermute | solution.py:28
  71.9 2.4 %token_grads.1 = bf16[512,1024]{1,0:T(8,128)(2,1)S(1)} custom-call(f32[512,128]{1,0:T(8,128)S(1)} %get-tuple-element.96.r_ref, bf16[1,1024]{1,0:T(2,128)(2,1)S(1)} %copy-done.2, bf16[8,512,256]{2,1,0:T(8,128)(2,1)S(1)} %get-tuple-element.100.g_ref, bf16[1024,256]{1,0:T(8,128)(2,1)S(1)} %bitcast.72, bf16[1024,256]{1,0:T(8,128)(2,1)S(1)} %collective-permute-done.2.rest_1_, ...), custom_call_target="tpu_custom_call" | custom-call | tf_op jit(solution)/shard_map/token_grads/pallas_call | solution.py:197
  74.3 3.6 %keys_values.1 = bf16[8,528,256]{2,1,0:T(8,128)(2,1)S(1)} custom-call(s32[8]{0:T(128)S(1)} %select_reduce_fusion.place_ref, bf16[512,1024]{1,0:T(8,128)(2,1)S(1)} %get-tuple-element.103.normed_ref, f32[512,128]{1,0:T(8,128)S(1)} %get-tuple-element.96.r_ref, bf16[8,512,256]{2,1,0:T(8,128)(2,1)S(1)} %get-tuple-element.100.g_ref, ...), custom_call_target="tpu_custom_call" | custom-call | tf_op jit(solution)/shard_map/keys_values/pallas_call | solution.py:197
  78.0 0.8 collective-permute-start.20
  78.8 0.8 collective-permute-start.19
  79.6 0.1 collective-permute-start.25
  79.7 1.8 %more_weight_grads.1 = (bf16[1024,256]{1,0:T(8,128)(2,1)S(1)}, bf16[1024,256]{1,0:T(8,128)(2,1)S(1)}, bf16[1024,256]{1,0:T(8,128)(2,1)S(1)}, bf16[512,256]{1,0:T...) custom-call(bf16[512,1024]{1,0:T(8,128)(2,1)S(1)} %get-tuple-element.10, ...), custom_call_target="tpu_custom_call" | custom-call | tf_op jit(solution)/shard_map/more_weight_grads/pallas_call | solution.py:197
  81.5 0.1 add.132
  81.7 0.1 add.131
  81.8 3.1 %collective-permute-done.20 = bf16[528,256]{1,0:T(8,128)(2,1)S(1)} collective-permute-done((bf16[528,256]{1,0:T(8,128)(2,1)S(1)}, bf16[528,256]{1,0:T(8,128)(2,1)S(1)}, u32[]{:S(2)}, u32[]{:S(2)}) %collective-permute-start.20) | collective-permute-done | bytes 270368 | tf_op jit(solution)/shard_map/ppermute | solution.py:23
  85.2 1.5 %collective-permute-start.24 = (bf16[2,528,256]{2,1,0:T(8,128)(2,1)S(1)}, bf16[2,528,256]{2,1,0:T(8,128)(2,1)S(1)}, u32[]{:S(2)}, u32[]{:S(2)}) collective-permute-start(bf16[2,528,256]{2,1,0:T(8,128)(2,1)S(1)} %pad_maximum_fusion.2), channel_id=1, source_target_pairs={{0,6},{1,7},{2,4},{3,5},{4,2},{5,3},{6,0},{7,1},{8,14},{9,15},{10,... | collective-permute-start | bytes 1622024 | tf_op jit(solution)/shard_map/ppermute | solution.py:23
  86.8 0.3 collective-permute-start.23
  87.1 0.4 collective-permute-start.21
  87.5 2.4 %collective-permute-start.22 = (bf16[1024,256]{1,0:T(8,128)(2,1)S(1)}, bf16[1024,256]{1,0:T(8,128)(2,1)S(1)}, u32[]{:S(2)}, u32[]{:S(2)}) collective-permute-start(bf16[1024,256]{1,0:T(8,128)(2,1)S(1)} %add.132), channel_id=1, source_target_pairs={{0,224},{32,0},{64,32},{96,64},{128,96},{160,128},{192,160},{224,1... | collective-permute-start | bytes 1572872 | tf_op jit(solution)/shard_map/ppermute | solution.py:28
  90.5 6.3 %collective-permute-done.21.arrived_ref = bf16[1024,256]{1,0:T(8,128)(2,1)S(1)} collective-permute-done((bf16[1024,256]{1,0:T(8,128)(2,1)S(1)}, bf16[1024,256]{1,0:T(8,128)(2,1)S(1)}, u32[]{:S(2)}, u32[]{:S(2)}) %collective-permute-start.21) | collective-permute-done | bytes 524320 | tf_op jit(solution)/shard_map/ppermute | solution.py:28
  96.8 0.1 add.133
  96.9 0.1 add.134
  97.0 3.6 %collective-permute-done.25 = bf16[512,1024]{1,0:T(8,128)(2,1)S(1)} collective-permute-done((bf16[512,1024]{1,0:T(8,128)(2,1)S(1)}, bf16[512,1024]{1,0:T(8,128)(2,1)S(1)}, u32[]{:S(2)}, u32[]{:S(2)}) %collective-permute-start.25) | collective-permute-done | bytes 1048608 | tf_op jit(solution)/shard_map/ppermute | solution.py:23
  100.6 0.3 convert_add_fusion.5
  101.1 0.9 collective-permute-start.30
  102.0 0.5 collective-permute-start.26
  102.5 2.2 %collective-permute-start.27 = (bf16[1024,256]{1,0:T(8,128)(2,1)S(1)}, bf16[1024,256]{1,0:T(8,128)(2,1)S(1)}, u32[]{:S(2)}, u32[]{:S(2)}) collective-permute-start(bf16[1024,256]{1,0:T(8,128)(2,1)S(1)} %add.134), channel_id=1, source_target_pairs={{0,224},{32,0},{64,32},{96,64},{128,96},{160,128},{192,160},{224,1... | collective-permute-start | bytes 1572872 | tf_op jit(solution)/shard_map/ppermute | solution.py:28
  104.7 3.1 %collective-permute-start.29 = (bf16[528,256]{1,0:T(8,128)(2,1)S(1)}, bf16[528,256]{1,0:T(8,128)(2,1)S(1)}, u32[]{:S(2)}, u32[]{:S(2)}) collective-permute-start(bf16[528,256]{1,0:T(8,128)(2,1)S(1)} %pad_maximum_fusion.6), channel_id=1, source_target_pairs={{0,16},{1,17},{2,18},{3,19},{4,20},{5,21},{6,22},{7,23},{8,24},{9,... | collective-permute-start | bytes 811016 | tf_op jit(solution)/shard_map/ppermute | solution.py:71
  107.9 3.3 %collective-permute-done.26.plus_ref = bf16[1024,256]{1,0:T(8,128)(2,1)S(1)} collective-permute-done((bf16[1024,256]{1,0:T(8,128)(2,1)S(1)}, bf16[1024,256]{1,0:T(8,128)(2,1)S(1)}, u32[]{:S(2)}, u32[]{:S(2)}) %collective-permute-start.26) | collective-permute-done | bytes 524320 | tf_op jit(solution)/shard_map/ppermute | solution.py:28
  111.2 8.0 %collective-permute-start.32 = (bf16[512,1024]{1,0:T(8,128)(2,1)S(1)}, bf16[512,1024]{1,0:T(8,128)(2,1)S(1)}, u32[]{:S(2)}, u32[]{:S(2)}) collective-permute-start(bf16[512,1024]{1,0:T(8,128)(2,1)S(1)} %broadcast_select_fusion), channel_id=1, source_target_pairs={{0,8},{8,0},{16,24},{24,16},{1,9},{9,1},{17,25},{25,17},{2,10},{10... | collective-permute-start | bytes 3145736 | tf_op jit(solution)/shard_map/ppermute | solution.py:23
  119.8 0.8 collective-permute-start.31
  122.0 1.1 collective-permute-start.33
  123.1 1.6 %collective-permute-start.34 = (bf16[512,256]{1,0:T(8,128)(2,1)S(1)}, bf16[512,256]{1,0:T(8,128)(2,1)S(1)}, u32[]{:S(2)}, u32[]{:S(2)}) collective-permute-start(bf16[512,256]{1,0:T(8,128)(2,1)S(1)} %add.136), channel_id=1, source_target_pairs={{0,224},{32,0},{64,32},{96,64},{128,96},{160,128},{192,160},{224,1... | collective-permute-start | bytes 786440 | tf_op jit(solution)/shard_map/ppermute | solution.py:28
  124.9 0.7 slice.257
  125.6 1.6 %subtract_convert_fusion = bf16[512,1024]{1,0:T(8,128)(2,1)} fusion(f32[512]{0:T(512)S(1)} %bitcast.80, bf16[512,1024]{1,0:T(8,128)(2,1)S(1)} %collective-permute-done.32, bf16[512,1024]{1,0:T(8,128)(2,1)S(1)} %token_grads.1, bf16[512,1024]{1,0:T(8,128)(2,1)S(1)} %collective-permute-done.25, pred[]{:T(512)} %bitcast.10, pred[]{:T(512)} %bitcast.9, ...), kind=kLoop, calls=%fused_computation | loop fusion | flops 3670016 | bytes 5244930 | tf_op jit(solution)/shard_map/convert_element_type | solution.py:401
  127.2 4.0 %collective-permute-done.33.plus_u = bf16[512,256]{1,0:T(8,128)(2,1)S(1)} collective-permute-done((bf16[512,256]{1,0:T(8,128)(2,1)S(1)}, bf16[512,256]{1,0:T(8,128)(2,1)S(1)}, u32[]{:S(2)}, u32[]{:S(2)}) %collective-permute-start.33) | collective-permute-done | bytes 262176 | tf_op jit(solution)/shard_map/ppermute | solution.py:28
  131.2 0.1 collective-permute-done.34.minus_l
  131.4 1.0 last.1
  (89 shorter events, 2.0 us)
Async XLA Ops:
  0.6 23.2 %copy-start = (bf16[1,1,2,256,1024]{4,3,2,1,0:T(8,128)(2,1)S(1)}, bf16[1,1,2,256,1024]{4,3,2,1,0:T(8,128)(2,1)}, u32[]{:S(2)}) copy-start(bf16[1,1,2,256,1024]{4,3,2,1,0:T(8,128)(2,1)} %param.6) | copy-start | bytes 3145732
  0.6 23.0 %copy-start.3 = (bf16[1,1,2,256,256]{4,3,2,1,0:T(8,128)(2,1)S(1)}, bf16[1,1,2,256,256]{4,3,2,1,0:T(8,128)(2,1)}, u32[]{:S(2)}) copy-start(bf16[1,1,2,256,256]{4,3,2,1,0:T(8,128)(2,1)} %param.11) | copy-start | bytes 786436
  0.7 15.5 %copy-start.1 = (bf16[1,1024,256]{2,1,0:T(8,128)(2,1)S(1)}, bf16[1,1024,256]{2,1,0:T(8,128)(2,1)}, u32[]{:S(2)}) copy-start(bf16[1,1024,256]{2,1,0:T(8,128)(2,1)} %param.8) | copy-start | bytes 1572868
  4.0 7.5 %collective-permute-start = (bf16[528,256]{1,0:T(8,128)(2,1)}, bf16[528,256]{1,0:T(8,128)(2,1)}, u32[]{:S(2)}, u32[]{:S(2)}) collective-permute-start(bf16[528,256]{1,0:T(8,128)(2,1)} %pad_maximum_fusion.5), channel_id=1, source_target_pairs={{0,8},{8,0},{16,24},{24,16},{1,9},{9,1},{17,25},{25,17},{2,10},{10... | collective-permute-start | bytes 811016 | tf_op jit(solution)/shard_map/ppermute | solution.py:23
  7.2 16.3 %collective-permute-start.4 = (bf16[1024,256]{1,0:T(8,128)(2,1)}, bf16[1024,256]{1,0:T(8,128)(2,1)S(1)}, u32[]{:S(2)}, u32[]{:S(2)}) collective-permute-start(bf16[1024,256]{1,0:T(8,128)(2,1)} %bitcast.70), channel_id=1, source_target_pairs={{0,32},{32,64},{64,96},{96,128},{128,160},{160,192},{192,224},{224... | collective-permute-start | bytes 1572872 | tf_op jit(solution)/shard_map/ppermute | solution.py:28
  7.2 16.5 %collective-permute-start.1 = (bf16[512,1024]{1,0:T(8,128)(2,1)}, bf16[512,1024]{1,0:T(8,128)(2,1)S(1)}, u32[]{:S(2)}, u32[]{:S(2)}) collective-permute-start(bf16[512,1024]{1,0:T(8,128)(2,1)} %bitcast.68), channel_id=1, source_target_pairs={{0,8},{8,0},{16,24},{24,16},{1,9},{9,1},{17,25},{25,17},{2,10},{10... | collective-permute-start | bytes 3145736 | tf_op jit(solution)/shard_map/ppermute | solution.py:23
  13.3 10.3 %collective-permute-start.6 = (bf16[528,256]{1,0:T(8,128)(2,1)S(1)}, bf16[528,256]{1,0:T(8,128)(2,1)S(1)}, u32[]{:S(2)}, u32[]{:S(2)}) collective-permute-start(bf16[528,256]{1,0:T(8,128)(2,1)S(1)} %broadcast_select_fusion.4), channel_id=1, source_target_pairs={{0,16},{1,17},{2,18},{3,19},{4,20},{5,21},{6,22},{7,23},{8,24},{9,... | collective-permute-start | bytes 811016 | tf_op jit(solution)/shard_map/ppermute | solution.py:71
  16.2 14.3 %collective-permute-start.2 = (bf16[1024,256]{1,0:T(8,128)(2,1)S(1)}, bf16[1024,256]{1,0:T(8,128)(2,1)S(1)}, u32[]{:S(2)}, u32[]{:S(2)}) collective-permute-start(bf16[1024,256]{1,0:T(8,128)(2,1)S(1)} %bitcast.71), channel_id=1, source_target_pairs={{0,224},{32,0},{64,32},{96,64},{128,96},{160,128},{192,160},{224,1... | collective-permute-start | bytes 1572872 | tf_op jit(solution)/shard_map/ppermute | solution.py:28
  24.0 15.6 %collective-permute-start.7 = (bf16[528,256]{1,0:T(8,128)(2,1)S(1)}, bf16[528,256]{1,0:T(8,128)(2,1)S(1)}, u32[]{:S(2)}, u32[]{:S(2)}) collective-permute-start(bf16[528,256]{1,0:T(8,128)(2,1)S(1)} %broadcast_select_fusion.3), channel_id=1, source_target_pairs={{0,1},{1,0},{2,3},{3,2},{4,5},{5,4},{6,7},{7,6},{8,9},{9,8},{10,11... | collective-permute-start | bytes 811016 | tf_op jit(solution)/shard_map/ppermute | solution.py:71
  30.5 8.5 %collective-permute-start.5 = (bf16[512,256]{1,0:T(8,128)(2,1)S(1)}, bf16[512,256]{1,0:T(8,128)(2,1)S(1)}, u32[]{:S(2)}, u32[]{:S(2)}) collective-permute-start(bf16[512,256]{1,0:T(8,128)(2,1)S(1)} %get-tuple-element.77), channel_id=1, source_target_pairs={{0,32},{32,64},{64,96},{96,128},{128,160},{160,192},{192,224},{224... | collective-permute-start | bytes 786440 | tf_op jit(solution)/shard_map/ppermute | solution.py:28
  31.5 8.1 %collective-permute-start.3 = (bf16[512,256]{1,0:T(8,128)(2,1)S(1)}, bf16[512,256]{1,0:T(8,128)(2,1)S(1)}, u32[]{:S(2)}, u32[]{:S(2)}) collective-permute-start(bf16[512,256]{1,0:T(8,128)(2,1)S(1)} %get-tuple-element.76), channel_id=1, source_target_pairs={{0,224},{32,0},{64,32},{96,64},{128,96},{160,128},{192,160},{224,1... | collective-permute-start | bytes 786440 | tf_op jit(solution)/shard_map/ppermute | solution.py:28
  39.6 28.7 %copy-start.2 = (bf16[1,1024]{1,0:T(2,128)(2,1)S(1)}, bf16[1,1024]{1,0:T(2,128)(2,1)}, u32[]{:S(2)}) copy-start(bf16[1,1024]{1,0:T(2,128)(2,1)} %gain_ref.3) | copy-start | bytes 6148
  39.7 15.2 %collective-permute-start.11 = (bf16[2,528,256]{2,1,0:T(8,128)(2,1)S(1)}, bf16[2,528,256]{2,1,0:T(8,128)(2,1)S(1)}, u32[]{:S(2)}, u32[]{:S(2)}) collective-permute-start(bf16[2,528,256]{2,1,0:T(8,128)(2,1)S(1)} %pad_maximum_fusion.rest_0_), channel_id=1, source_target_pairs={{0,6},{1,7},{2,4},{3,5},{4,2},{5,3},{6,0},{7,1},{8,14},{9,15},{10,... | collective-permute-start | bytes 1622024 | tf_op jit(solution)/shard_map/ppermute | solution.py:23
  42.3 12.6 %collective-permute-start.10 = (bf16[2,528,256]{2,1,0:T(8,128)(2,1)S(1)}, bf16[2,528,256]{2,1,0:T(8,128)(2,1)S(1)}, u32[]{:S(2)}, u32[]{:S(2)}) collective-permute-start(bf16[2,528,256]{2,1,0:T(8,128)(2,1)S(1)} %pad_maximum_fusion.rest_0_), channel_id=1, source_target_pairs={{0,2},{1,3},{2,0},{3,1},{4,6},{5,7},{6,4},{7,5},{8,10},{9,11},{10,... | collective-permute-start | bytes 1622024 | tf_op jit(solution)/shard_map/ppermute | solution.py:23
  42.3 12.2 %collective-permute-start.9 = (bf16[1024,256]{1,0:T(8,128)(2,1)S(1)}, bf16[1024,256]{1,0:T(8,128)(2,1)S(1)}, u32[]{:S(2)}, u32[]{:S(2)}) collective-permute-start(bf16[1024,256]{1,0:T(8,128)(2,1)S(1)} %pad_maximum_fusion.4), channel_id=1, source_target_pairs={{0,32},{32,64},{64,96},{96,128},{128,160},{160,192},{192,224},{224... | collective-permute-start | bytes 1572872 | tf_op jit(solution)/shard_map/ppermute | solution.py:28
  44.4 10.4 %collective-permute-start.8 = (bf16[1024,256]{1,0:T(8,128)(2,1)S(1)}, bf16[1024,256]{1,0:T(8,128)(2,1)S(1)}, u32[]{:S(2)}, u32[]{:S(2)}) collective-permute-start(bf16[1024,256]{1,0:T(8,128)(2,1)S(1)} %pad_maximum_fusion.3), channel_id=1, source_target_pairs={{0,224},{32,0},{64,32},{96,64},{128,96},{160,128},{192,160},{224,1... | collective-permute-start | bytes 1572872 | tf_op jit(solution)/shard_map/ppermute | solution.py:28
  45.2 23.1 %collective-permute-start.16 = (bf16[512,1024]{1,0:T(8,128)(2,1)S(1)}, bf16[512,1024]{1,0:T(8,128)(2,1)S(1)}, u32[]{:S(2)}, u32[]{:S(2)}) collective-permute-start(bf16[512,1024]{1,0:T(8,128)(2,1)S(1)} %broadcast_select_fusion.1), channel_id=1, source_target_pairs={{0,16},{8,24},{16,0},{24,8},{1,17},{9,25},{17,1},{25,9},{2,18},{10... | collective-permute-start | bytes 3145736 | tf_op jit(solution)/shard_map/ppermute | solution.py:23
  54.9 13.4 %collective-permute-start.12 = (bf16[1024,256]{1,0:T(8,128)(2,1)S(1)}, bf16[1024,256]{1,0:T(8,128)(2,1)S(1)}, u32[]{:S(2)}, u32[]{:S(2)}) collective-permute-start(bf16[1024,256]{1,0:T(8,128)(2,1)S(1)} %collective-permute-done.8.rest_3_), channel_id=1, source_target_pairs={{0,224},{32,0},{64,32},{96,64},{128,96},{160,128},{192,160},{224,1... | collective-permute-start | bytes 1572872 | tf_op jit(solution)/shard_map/ppermute | solution.py:28
  57.1 11.3 %collective-permute-start.13 = (bf16[1024,256]{1,0:T(8,128)(2,1)S(1)}, bf16[1024,256]{1,0:T(8,128)(2,1)S(1)}, u32[]{:S(2)}, u32[]{:S(2)}) collective-permute-start(bf16[1024,256]{1,0:T(8,128)(2,1)S(1)} %collective-permute-done.9.rest_7_), channel_id=1, source_target_pairs={{0,32},{32,64},{64,96},{96,128},{128,160},{160,192},{192,224},{224... | collective-permute-start | bytes 1572872 | tf_op jit(solution)/shard_map/ppermute | solution.py:28
  57.1 11.2 %collective-permute-start.14 = (bf16[528,256]{1,0:T(8,128)(2,1)S(1)}, bf16[528,256]{1,0:T(8,128)(2,1)S(1)}, u32[]{:S(2)}, u32[]{:S(2)}) collective-permute-start(bf16[528,256]{1,0:T(8,128)(2,1)S(1)} %slice_bitcast_fusion.5), channel_id=1, source_target_pairs={{0,2},{1,3},{2,0},{3,1},{4,6},{5,7},{6,4},{7,5},{8,10},{9,11},{10,... | collective-permute-start | bytes 811016 | tf_op jit(solution)/shard_map/ppermute | solution.py:23
  58.6 9.7 %collective-permute-start.15 = (bf16[528,256]{1,0:T(8,128)(2,1)S(1)}, bf16[528,256]{1,0:T(8,128)(2,1)S(1)}, u32[]{:S(2)}, u32[]{:S(2)}) collective-permute-start(bf16[528,256]{1,0:T(8,128)(2,1)S(1)} %slice_bitcast_fusion.4), channel_id=1, source_target_pairs={{0,6},{1,7},{2,4},{3,5},{4,2},{5,3},{6,0},{7,1},{8,14},{9,15},{10,... | collective-permute-start | bytes 811016 | tf_op jit(solution)/shard_map/ppermute | solution.py:23
  70.4 11.2 %collective-permute-start.18 = (bf16[1024,256]{1,0:T(8,128)(2,1)S(1)}, bf16[1024,256]{1,0:T(8,128)(2,1)S(1)}, u32[]{:S(2)}, u32[]{:S(2)}) collective-permute-start(bf16[1024,256]{1,0:T(8,128)(2,1)S(1)} %get-tuple-element.105), channel_id=1, source_target_pairs={{0,224},{32,0},{64,32},{96,64},{128,96},{160,128},{192,160},{224,1... | collective-permute-start | bytes 1572872 | tf_op jit(solution)/shard_map/ppermute | solution.py:28
  70.5 11.2 %collective-permute-start.17 = (bf16[1024,256]{1,0:T(8,128)(2,1)S(1)}, bf16[1024,256]{1,0:T(8,128)(2,1)S(1)}, u32[]{:S(2)}, u32[]{:S(2)}) collective-permute-start(bf16[1024,256]{1,0:T(8,128)(2,1)S(1)} %get-tuple-element.101), channel_id=1, source_target_pairs={{0,32},{32,64},{64,96},{96,128},{128,160},{160,192},{192,224},{224... | collective-permute-start | bytes 1572872 | tf_op jit(solution)/shard_map/ppermute | solution.py:28
  78.0 6.9 %collective-permute-start.20 = (bf16[528,256]{1,0:T(8,128)(2,1)S(1)}, bf16[528,256]{1,0:T(8,128)(2,1)S(1)}, u32[]{:S(2)}, u32[]{:S(2)}) collective-permute-start(bf16[528,256]{1,0:T(8,128)(2,1)S(1)} %get-tuple-element.143), channel_id=1, source_target_pairs={{0,6},{1,7},{2,4},{3,5},{4,2},{5,3},{6,0},{7,1},{8,14},{9,15},{10,... | collective-permute-start | bytes 811016 | tf_op jit(solution)/shard_map/ppermute | solution.py:23
  78.8 6.1 %collective-permute-start.19 = (bf16[528,256]{1,0:T(8,128)(2,1)S(1)}, bf16[528,256]{1,0:T(8,128)(2,1)S(1)}, u32[]{:S(2)}, u32[]{:S(2)}) collective-permute-start(bf16[528,256]{1,0:T(8,128)(2,1)S(1)} %get-tuple-element.144), channel_id=1, source_target_pairs={{0,2},{1,3},{2,0},{3,1},{4,6},{5,7},{6,4},{7,5},{8,10},{9,11},{10,... | collective-permute-start | bytes 811016 | tf_op jit(solution)/shard_map/ppermute | solution.py:23
  79.6 21.1 %collective-permute-start.25 = (bf16[512,1024]{1,0:T(8,128)(2,1)S(1)}, bf16[512,1024]{1,0:T(8,128)(2,1)S(1)}, u32[]{:S(2)}, u32[]{:S(2)}) collective-permute-start(bf16[512,1024]{1,0:T(8,128)(2,1)S(1)} %token_grads.1), channel_id=1, source_target_pairs={{0,16},{8,24},{16,0},{24,8},{1,17},{9,25},{17,1},{25,9},{2,18},{10... | collective-permute-start | bytes 3145736 | tf_op jit(solution)/shard_map/ppermute | solution.py:23
  85.2 15.4 %collective-permute-start.24 = (bf16[2,528,256]{2,1,0:T(8,128)(2,1)S(1)}, bf16[2,528,256]{2,1,0:T(8,128)(2,1)S(1)}, u32[]{:S(2)}, u32[]{:S(2)}) collective-permute-start(bf16[2,528,256]{2,1,0:T(8,128)(2,1)S(1)} %pad_maximum_fusion.2), channel_id=1, source_target_pairs={{0,6},{1,7},{2,4},{3,5},{4,2},{5,3},{6,0},{7,1},{8,14},{9,15},{10,... | collective-permute-start | bytes 1622024 | tf_op jit(solution)/shard_map/ppermute | solution.py:23
  86.8 13.8 %collective-permute-start.23 = (bf16[2,528,256]{2,1,0:T(8,128)(2,1)S(1)}, bf16[2,528,256]{2,1,0:T(8,128)(2,1)S(1)}, u32[]{:S(2)}, u32[]{:S(2)}) collective-permute-start(bf16[2,528,256]{2,1,0:T(8,128)(2,1)S(1)} %pad_maximum_fusion.1), channel_id=1, source_target_pairs={{0,2},{1,3},{2,0},{3,1},{4,6},{5,7},{6,4},{7,5},{8,10},{9,11},{10,... | collective-permute-start | bytes 1622024 | tf_op jit(solution)/shard_map/ppermute | solution.py:23
  87.1 9.6 %collective-permute-start.21 = (bf16[1024,256]{1,0:T(8,128)(2,1)S(1)}, bf16[1024,256]{1,0:T(8,128)(2,1)S(1)}, u32[]{:S(2)}, u32[]{:S(2)}) collective-permute-start(bf16[1024,256]{1,0:T(8,128)(2,1)S(1)} %add.131), channel_id=1, source_target_pairs={{0,32},{32,64},{64,96},{96,128},{128,160},{160,192},{192,224},{224... | collective-permute-start | bytes 1572872 | tf_op jit(solution)/shard_map/ppermute | solution.py:28
  87.5 9.4 %collective-permute-start.22 = (bf16[1024,256]{1,0:T(8,128)(2,1)S(1)}, bf16[1024,256]{1,0:T(8,128)(2,1)S(1)}, u32[]{:S(2)}, u32[]{:S(2)}) collective-permute-start(bf16[1024,256]{1,0:T(8,128)(2,1)S(1)} %add.132), channel_id=1, source_target_pairs={{0,224},{32,0},{64,32},{96,64},{128,96},{160,128},{192,160},{224,1... | collective-permute-start | bytes 1572872 | tf_op jit(solution)/shard_map/ppermute | solution.py:28
  101.1 18.4 %collective-permute-start.30 = (bf16[528,256]{1,0:T(8,128)(2,1)S(1)}, bf16[528,256]{1,0:T(8,128)(2,1)S(1)}, u32[]{:S(2)}, u32[]{:S(2)}) collective-permute-start(bf16[528,256]{1,0:T(8,128)(2,1)S(1)} %pad_maximum_fusion.7), channel_id=1, source_target_pairs={{0,17},{1,16},{2,19},{3,18},{4,21},{5,20},{6,23},{7,22},{8,25},{9,... | collective-permute-start | bytes 811016 | tf_op jit(solution)/shard_map/ppermute | solution.py:71
  102.0 17.5 %collective-permute-start.28 = (bf16[528,256]{1,0:T(8,128)(2,1)S(1)}, bf16[528,256]{1,0:T(8,128)(2,1)S(1)}, u32[]{:S(2)}, u32[]{:S(2)}) collective-permute-start(bf16[528,256]{1,0:T(8,128)(2,1)S(1)} %pad_maximum_fusion.7), channel_id=1, source_target_pairs={{0,1},{1,0},{2,3},{3,2},{4,5},{5,4},{6,7},{7,6},{8,9},{9,8},{10,11... | collective-permute-start | bytes 811016 | tf_op jit(solution)/shard_map/ppermute | solution.py:71
  102.0 9.2 %collective-permute-start.26 = (bf16[1024,256]{1,0:T(8,128)(2,1)S(1)}, bf16[1024,256]{1,0:T(8,128)(2,1)S(1)}, u32[]{:S(2)}, u32[]{:S(2)}) collective-permute-start(bf16[1024,256]{1,0:T(8,128)(2,1)S(1)} %add.133), channel_id=1, source_target_pairs={{0,32},{32,64},{64,96},{96,128},{128,160},{160,192},{192,224},{224... | collective-permute-start | bytes 1572872 | tf_op jit(solution)/shard_map/ppermute | solution.py:28
  102.5 16.9 %collective-permute-start.27 = (bf16[1024,256]{1,0:T(8,128)(2,1)S(1)}, bf16[1024,256]{1,0:T(8,128)(2,1)S(1)}, u32[]{:S(2)}, u32[]{:S(2)}) collective-permute-start(bf16[1024,256]{1,0:T(8,128)(2,1)S(1)} %add.134), channel_id=1, source_target_pairs={{0,224},{32,0},{64,32},{96,64},{128,96},{160,128},{192,160},{224,1... | collective-permute-start | bytes 1572872 | tf_op jit(solution)/shard_map/ppermute | solution.py:28
  104.7 14.8 %collective-permute-start.29 = (bf16[528,256]{1,0:T(8,128)(2,1)S(1)}, bf16[528,256]{1,0:T(8,128)(2,1)S(1)}, u32[]{:S(2)}, u32[]{:S(2)}) collective-permute-start(bf16[528,256]{1,0:T(8,128)(2,1)S(1)} %pad_maximum_fusion.6), channel_id=1, source_target_pairs={{0,16},{1,17},{2,18},{3,19},{4,20},{5,21},{6,22},{7,23},{8,24},{9,... | collective-permute-start | bytes 811016 | tf_op jit(solution)/shard_map/ppermute | solution.py:71
  111.2 14.4 %collective-permute-start.32 = (bf16[512,1024]{1,0:T(8,128)(2,1)S(1)}, bf16[512,1024]{1,0:T(8,128)(2,1)S(1)}, u32[]{:S(2)}, u32[]{:S(2)}) collective-permute-start(bf16[512,1024]{1,0:T(8,128)(2,1)S(1)} %broadcast_select_fusion), channel_id=1, source_target_pairs={{0,8},{8,0},{16,24},{24,16},{1,9},{9,1},{17,25},{25,17},{2,10},{10... | collective-permute-start | bytes 3145736 | tf_op jit(solution)/shard_map/ppermute | solution.py:23
  119.8 4.9 %collective-permute-start.31 = (bf16[528,256]{1,0:T(8,128)(2,1)S(1)}, bf16[528,256]{1,0:T(8,128)(2,1)S(1)}, u32[]{:S(2)}, u32[]{:S(2)}) collective-permute-start(bf16[528,256]{1,0:T(8,128)(2,1)S(1)} %broadcast_select_fusion.2), channel_id=1, source_target_pairs={{0,8},{8,0},{16,24},{24,16},{1,9},{9,1},{17,25},{25,17},{2,10},{10... | collective-permute-start | bytes 811016 | tf_op jit(solution)/shard_map/ppermute | solution.py:23
  122.0 9.2 %collective-permute-start.33 = (bf16[512,256]{1,0:T(8,128)(2,1)S(1)}, bf16[512,256]{1,0:T(8,128)(2,1)S(1)}, u32[]{:S(2)}, u32[]{:S(2)}) collective-permute-start(bf16[512,256]{1,0:T(8,128)(2,1)S(1)} %add.135), channel_id=1, source_target_pairs={{0,32},{32,64},{64,96},{96,128},{128,160},{160,192},{192,224},{224... | collective-permute-start | bytes 786440 | tf_op jit(solution)/shard_map/ppermute | solution.py:28
  123.1 8.2 %collective-permute-start.34 = (bf16[512,256]{1,0:T(8,128)(2,1)S(1)}, bf16[512,256]{1,0:T(8,128)(2,1)S(1)}, u32[]{:S(2)}, u32[]{:S(2)}) collective-permute-start(bf16[512,256]{1,0:T(8,128)(2,1)S(1)} %add.136), channel_id=1, source_target_pairs={{0,224},{32,0},{64,32},{96,64},{128,96},{160,128},{192,160},{224,1... | collective-permute-start | bytes 786440 | tf_op jit(solution)/shard_map/ppermute | solution.py:28
